TPU v7x, 256 devices: a whole 4x4x8 slice. The times are simulated.
256 devices in a mesh: rows: 8 (over x, core), cols: 32 (over y, z).
Axes of the slice: x: 4, y: 4, z: 8, core: 2. Of those that a mesh axis runs over, the one named last changes fastest.
Arguments:
- forcing: float32 [32, 2, 512, 8192], P(None, None, 'cols', 'rows'), may hold values from -3 to 3
- material: int32 [2, 512, 8192], P(None, 'cols', 'rows'), may hold values from 0 to 7
- capacity_table: float32 [8], replicated, may hold values from 0.5 to 2
- conductance_table: float32 [8], replicated, may hold values from 0.25 to 2
- sink_table: float32 [8], replicated, may hold values from 0.1 to 1
Outputs:
- initial_sensitivity: float32 [2, 512, 8192], P(None, 'cols', 'rows')
- window_mean: float32 [2, 512, 8192], P(None, 'cols', 'rows')
- residual_norms: float32 [3], replicated
All inputs are finite; a program needn't handle non-finite values.
Results may differ from a plain program's by a relative error of at most 0.0001.
Values sent between devices are 32-bit elements; how exact they have to be, the bound alone decides.
No kernel may reach another device: no remote copies, remote signals or barrier semaphores. Data moves between devices by JAX's collectives and lax.ppermute only.
A program may use at most 128 MiB of HBM per device.

v0:
```python
import jax
import jax.numpy as jnp
from jax import lax
from jax.sharding import PartitionSpec as P

PASSES = 8
SWEEPS = 3


def extended(x, sides, width):
    for axis, dim in sides:
        count, length = (lax.axis_size(axis), x.shape[dim])
        up = [(i, (i + 1) % count) for i in range(count - 1)]
        down = [(j, i) for i, j in up]
        last = lax.slice_in_dim(x, length - width, length, axis=dim)
        leading = lax.slice_in_dim(x, 0, width, axis=dim)
        before = lax.ppermute(last, axis, up)
        after = lax.ppermute(leading, axis, down)
        x = jnp.concatenate([before, x, after], axis=dim)
    return x


def shifted(field, axis, offset):
    length = field.shape[axis]
    widths = [(0, 0)] * field.ndim
    if offset > 0:
        kept = lax.slice_in_dim(field, 1, length, axis=axis)
        widths[axis] = (0, 1)
    else:
        kept = lax.slice_in_dim(field, 0, length - 1, axis=axis)
        widths[axis] = (1, 0)
    return jnp.pad(kept, widths)


def couple(conduct, other):
    return 2.0 * conduct * other / (conduct + other)


def neighbour_sum(field, inner, vertical):
    total = inner[0] * shifted(field, 1, 1) + inner[1] * shifted(field, 1, -1)
    total = total + inner[2] * shifted(field, 2, 1) + inner[3] * shifted(field, 2, -1)
    return total + vertical * field[::-1]


def cross_terms(framed, outer):
    total = outer[0] * framed[:, :, 2:, 1:-1] + outer[1] * framed[:, :, :-2, 1:-1]
    return total + outer[2] * framed[:, :, 1:-1, 2:] + outer[3] * framed[:, :, 1:-1, :-2]


def sweep_total(squares):
    return lax.psum(squares, ("rows", "cols"))


def local(forcing, material, capacity_table, conductance_table, sink_table):
    steps_total, layers, cols_local, rows_local = forcing.shape
    n_cols = lax.axis_size("cols")
    n_rows = lax.axis_size("rows")
    kinds = jnp.arange(capacity_table.shape[0], dtype=jnp.int32)[:, None, None, None]
    onehot = (material[None] == kinds).astype(jnp.float32)

    def lookup(table):
        return jnp.sum(onehot * table[:, None, None, None], 0)

    capacity = lookup(capacity_table)
    conduct = lookup(conductance_table)
    sink = lookup(sink_table)
    framed_conduct = extended(conduct, (("rows", 2), ("cols", 1)), 1)
    others = [
        framed_conduct[:, 2:, 1:-1],
        framed_conduct[:, :-2, 1:-1],
        framed_conduct[:, 1:-1, 2:],
        framed_conduct[:, 1:-1, :-2],
    ]
    edges = [couple(conduct, other) for other in others]
    vertical = couple(conduct, conduct[::-1])
    diagonal = capacity + sink + edges[0] + edges[1] + edges[2] + edges[3] + vertical
    local_col = jnp.arange(cols_local, dtype=jnp.int32)
    local_row = jnp.arange(rows_local, dtype=jnp.int32)
    masks = [
        (local_col != cols_local - 1)[None, :, None],
        (local_col != 0)[None, :, None],
        (local_row != rows_local - 1)[None, None, :],
        (local_row != 0)[None, None, :],
    ]
    inner = [jnp.where(mask, edge, 0.0) for mask, edge in zip(masks, edges)]
    outer = [jnp.where(mask, 0.0, edge) for mask, edge in zip(masks, edges)]
    column = lax.axis_index("cols") * cols_local + local_col
    row = lax.axis_index("rows") * rows_local + local_row
    profile = jnp.power(
        jnp.float32(3.0),
        column.astype(jnp.float32)[:, None] / float(cols_local * n_cols)
        + row.astype(jnp.float32)[None, :] / float(rows_local * n_rows),
    )
    count = float(steps_total * layers * cols_local * rows_local * n_cols * n_rows)
    zeros = jnp.zeros(forcing.shape[1:], jnp.float32)

    def advance(later, inputs):
        force_now, cross_now = inputs
        rhs = force_now * profile + capacity * later + cross_now
        field = later
        for turn in range(PASSES):
            field = (rhs + neighbour_sum(field, inner, vertical)) / diagonal
        return (field, field)

    totals = []
    previous = None
    squares_list = []
    for sweep in range(SWEEPS):
        if previous is None:
            cross = jnp.zeros_like(forcing)
        else:
            framed = extended(previous, (("rows", 3), ("cols", 2)), 1)
            cross = cross_terms(framed, outer)
        first, wave = lax.scan(advance, zeros, (forcing, cross), reverse=True)
        change = wave if previous is None else wave - previous
        squares = jnp.sum(change * change)
        squares_list.append(squares)
        totals.append(sweep_total(squares))
        previous = wave
    window_sum = jnp.sum(previous, 0)
    summed = jnp.stack(totals)
    residual_norms = jnp.sqrt(summed / count + 1e-06)
    initial_sensitivity = capacity * first
    window_mean = window_sum / steps_total
    return (initial_sensitivity, window_mean, residual_norms)


def solution(mesh):
    return jax.shard_map(
        local,
        mesh=mesh,
        in_specs=(P(None, None, "cols", "rows"), P(None, "cols", "rows"), P(), P(), P()),
        out_specs=(P(None, "cols", "rows"), P(None, "cols", "rows"), P()),
        check_vma=False,
    )
```

profile of v0, /device:TPU:1, one launch (start us, length us, event | category | flops | bytes accessed | tf_op | source)
XLA Modules:
  0.0 586.6 jit_solution(14793151015285948663)
XLA Ops:
  2.0 4.5 collective-permute-start
  8.5 3.1 collective-permute-done.1
  13.0 4.2 collective-permute-start.3
  20.9 121.0 %while.51 = (s32[]{:T(128)}, f32[2,16,1024]{2,1,0:T(8,128)S(1)}, f32[32,2,16,1024]{3,2,1,0:T(8,128)}, f32[32,2,16,1024]{3,2,1,0:T(8,128)}, f32[2,16,1024]{2,1,0:...) while((s32[]{:T(128)}, f32[2,16,1024]{2,1,0:T(8,128)S(1)}, ...), condition=%wide.region_4.5_spmd.clone, body=%wide.region_3.4_spmd.clone.sunk | while | flops 3031044 | bytes 22411508 | solution.py:114
  143.3 2.9 collective-permute-start.4
  148.2 4.2 collective-permute-done.4
  152.3 4.4 collective-permute-done.5
  156.7 6.4 %concatenate.53 = f32[32,2,16,1026]{3,2,1,0:T(8,128)} concatenate(f32[32,2,16,1]{3,2,1,0:T(8,128)S(1)} %collective-permute-done.4, f32[32,2,16,1024]{3,2,1,0:T(8,128)} %get-tuple-element.753, f32[32,2,16,1]{3,2,1,0:T(8,128)S(1)} %collective-permute-done.5), dimensions={3} | concatenate | bytes 8404992 | tf_op jit(solution)/shard_map/concatenate | solution.py:19
  163.1 2.8 fusion.82
  167.2 5.3 collective-permute-start.7
  175.4 11.6 %fusion.17 = f32[32,2,16,1024]{3,2,1,0:T(8,128)} fusion(f32[32,2,16,1024]{3,2,1,0:T(8,128)} %get-tuple-element.753, f32[32,2,16,1]{3,2,1,0:T(8,128)S(1)} %collective-permute-done.4, f32[32,2,16,1]{3,2,1,0:T(8,128)S(1)} %collective-permute-done.5, f32[32,2,16,1026]{3,2,1,0:T(8,128)} %concatenate.53, f32[32,2,1,1026]{3,2,1,0:T(1,128)} %collective-permute-done.7, ...), kind=kLoop, calls=%fused_computation.57 | loop fusion | flops 11534336 | bytes 13648896 | tf_op jit(solution)/shard_map/add | solution.py:47
  187.0 2.6 broadcast.272.clone
  189.7 123.7 %while.52 = (s32[]{:T(128)}, f32[2,16,1024]{2,1,0:T(8,128)S(1)}, f32[32,2,16,1024]{3,2,1,0:T(8,128)}, f32[32,2,16,1024]{3,2,1,0:T(8,128)}, f32[2,16,1024]{2,1,0:...) while((s32[]{:T(128)}, f32[2,16,1024]{2,1,0:T(8,128)S(1)}, ...), condition=%wide.region_6.7_spmd.clone, body=%wide.region_5.6_spmd.clone.sunk | while | flops 3063812 | bytes 22542588 | solution.py:114
  314.8 5.0 collective-permute-start.8
  321.7 4.2 collective-permute-done.8
  325.9 4.4 collective-permute-done.9
  330.3 6.4 %concatenate.58 = f32[32,2,16,1026]{3,2,1,0:T(8,128)} concatenate(f32[32,2,16,1]{3,2,1,0:T(8,128)S(1)} %collective-permute-done.8, f32[32,2,16,1024]{3,2,1,0:T(8,128)} %get-tuple-element.754, f32[32,2,16,1]{3,2,1,0:T(8,128)S(1)} %collective-permute-done.9), dimensions={3} | concatenate | bytes 8404992 | tf_op jit(solution)/shard_map/concatenate | solution.py:19
  336.7 2.8 fusion.81
  340.8 5.6 collective-permute-start.11
  349.3 11.6 %fusion.10 = f32[32,2,16,1024]{3,2,1,0:T(8,128)} fusion(f32[32,2,16,1024]{3,2,1,0:T(8,128)} %get-tuple-element.754, f32[32,2,16,1]{3,2,1,0:T(8,128)S(1)} %collective-permute-done.8, f32[32,2,16,1]{3,2,1,0:T(8,128)S(1)} %collective-permute-done.9, f32[32,2,16,1026]{3,2,1,0:T(8,128)} %concatenate.58, f32[32,2,1,1026]{3,2,1,0:T(1,128)} %collective-permute-done.11, ...), kind=kLoop, calls=%fused_computation.46 | loop fusion | flops 11534336 | bytes 13648896 | tf_op jit(solution)/shard_map/add | solution.py:47
  360.9 2.5 broadcast.272
  363.4 123.7 %while.53 = (s32[]{:T(128)}, f32[2,16,1024]{2,1,0:T(8,128)S(1)}, f32[32,2,16,1024]{3,2,1,0:T(8,128)}, f32[32,2,16,1024]{3,2,1,0:T(8,128)}, f32[2,16,1024]{2,1,0:...) while((s32[]{:T(128)}, f32[2,16,1024]{2,1,0:T(8,128)S(1)}, ...), condition=%wide.region_8.9_spmd.clone, body=%wide.region_7.8_spmd.clone.sunk | while | flops 3063812 | bytes 22542588 | solution.py:114
  487.1 6.1 %multiply_reduce_fusion.2 = (f32[]{:T(128)}, f32[]{:T(128)}, f32[]{:T(128)}, f32[2,16,1024]{2,1,0:T(8,128)S(1)}) fusion(f32[32,2,16,1024]{3,2,1,0:T(8,128)} %get-tuple-element.753, f32[32,2,16,1024]{3,2,1,0:T(8,128)} %get-tuple-element.754, f32[32,2,16,1024]{3,2,1,0:T(8,128)} %get-tuple-element.756), kind=kLoop, calls=%fused_computation.68 | loop fusion | flops 9404413 | bytes 12713996 | tf_op jit(solution)/shard_map/reduce_sum | solution.py:116
  494.5 89.7 %all-reduce.96 = (f32[1]{0:T(128)}, f32[1]{0:T(128)}, f32[1]{0:T(128)}) all-reduce(f32[1]{0:T(128)} %bitcast.2, f32[1]{0:T(128)} %bitcast.1, f32[1]{0:T(128)} %bitcast), channel_id=1, replica_groups=mesh['rows'=8,'cols'=32] {'rows','cols'}, use_global_device_ids=true, to_apply=%region_15.16 | all-reduce | flops 3 | bytes 24 | tf_op jit(solution)/shard_map/psum | solution.py:51
  (2530 shorter events, 378.5 us)
Async XLA Ops:
  2.0 6.5 %collective-permute-start = (f32[2,16,1]{2,1,0:T(8,128)S(1)}, f32[2,16,1]{2,1,0:T(8,128)S(1)}, u32[]{:S(2)}, u32[]{:S(2)}) collective-permute-start(f32[2,16,1]{2,1,0:T(8,128)S(1)} %get-tuple-element.1126), channel_id=1, source_target_pairs={{0,32},{32,64},{64,96},{96,128},{128,160},{160,192},{192,224},{1,3... | collective-permute-start | bytes 392 | tf_op jit(solution)/shard_map/ppermute | solution.py:17
  6.5 5.1 collective-permute-start.1
  11.7 5.5 collective-permute-start.2
  13.0 5.0 collective-permute-start.3
  143.3 9.0 %collective-permute-start.4 = (f32[32,2,16,1]{3,2,1,0:T(8,128)S(1)}, f32[32,2,16,1]{3,2,1,0:T(8,128)S(1)}, u32[]{:S(2)}, u32[]{:S(2)}) collective-permute-start(f32[32,2,16,1]{3,2,1,0:T(8,128)S(1)} %get-tuple-element.1112), channel_id=1, source_target_pairs={{0,32},{32,64},{64,96},{96,128},{128,160},{160,192},{192,224},{1,3... | collective-permute-start | bytes 12296 | tf_op jit(solution)/shard_map/ppermute | solution.py:17
  146.2 10.5 %collective-permute-start.5 = (f32[32,2,16,1]{3,2,1,0:T(8,128)S(1)}, f32[32,2,16,1]{3,2,1,0:T(8,128)S(1)}, u32[]{:S(2)}, u32[]{:S(2)}) collective-permute-start(f32[32,2,16,1]{3,2,1,0:T(8,128)S(1)} %get-tuple-element.1111), channel_id=1, source_target_pairs={{32,0},{64,32},{96,64},{128,96},{160,128},{192,160},{224,192},{33,... | collective-permute-start | bytes 12296 | tf_op jit(solution)/shard_map/ppermute | solution.py:18
  165.9 8.1 %collective-permute-start.6 = (f32[32,2,1,1026]{3,2,1,0:T(1,128)S(1)}, f32[32,2,1,1026]{3,2,1,0:T(1,128)}, u32[]{:S(2)}, u32[]{:S(2)}) collective-permute-start(f32[32,2,1,1026]{3,2,1,0:T(1,128)S(1)} %get-tuple-element.1107), channel_id=1, source_target_pairs={{1,0},{2,1},{3,2},{4,3},{5,4},{6,5},{7,6},{8,7},{9,8},{10,9},{11,1... | collective-permute-start | bytes 787976 | tf_op jit(solution)/shard_map/ppermute | solution.py:18
  167.2 8.2 %collective-permute-start.7 = (f32[32,2,1,1026]{3,2,1,0:T(1,128)S(1)}, f32[32,2,1,1026]{3,2,1,0:T(1,128)}, u32[]{:S(2)}, u32[]{:S(2)}) collective-permute-start(f32[32,2,1,1026]{3,2,1,0:T(1,128)S(1)} %get-tuple-element.1108), channel_id=1, source_target_pairs={{0,1},{1,2},{2,3},{3,4},{4,5},{5,6},{6,7},{7,8},{8,9},{9,10},{10,1... | collective-permute-start | bytes 787976 | tf_op jit(solution)/shard_map/ppermute | solution.py:17
  314.8 11.1 %collective-permute-start.8 = (f32[32,2,16,1]{3,2,1,0:T(8,128)S(1)}, f32[32,2,16,1]{3,2,1,0:T(8,128)S(1)}, u32[]{:S(2)}, u32[]{:S(2)}) collective-permute-start(f32[32,2,16,1]{3,2,1,0:T(8,128)S(1)} %get-tuple-element.1110), channel_id=1, source_target_pairs={{0,32},{32,64},{64,96},{96,128},{128,160},{160,192},{192,224},{1,3... | collective-permute-start | bytes 12296 | tf_op jit(solution)/shard_map/ppermute | solution.py:17
  319.8 10.5 %collective-permute-start.9 = (f32[32,2,16,1]{3,2,1,0:T(8,128)S(1)}, f32[32,2,16,1]{3,2,1,0:T(8,128)S(1)}, u32[]{:S(2)}, u32[]{:S(2)}) collective-permute-start(f32[32,2,16,1]{3,2,1,0:T(8,128)S(1)} %get-tuple-element.1109), channel_id=1, source_target_pairs={{32,0},{64,32},{96,64},{128,96},{160,128},{192,160},{224,192},{33,... | collective-permute-start | bytes 12296 | tf_op jit(solution)/shard_map/ppermute | solution.py:18
  339.5 8.4 %collective-permute-start.10 = (f32[32,2,1,1026]{3,2,1,0:T(1,128)S(1)}, f32[32,2,1,1026]{3,2,1,0:T(1,128)}, u32[]{:S(2)}, u32[]{:S(2)}) collective-permute-start(f32[32,2,1,1026]{3,2,1,0:T(1,128)S(1)} %get-tuple-element.1105), channel_id=1, source_target_pairs={{1,0},{2,1},{3,2},{4,3},{5,4},{6,5},{7,6},{8,7},{9,8},{10,9},{11,1... | collective-permute-start | bytes 787976 | tf_op jit(solution)/shard_map/ppermute | solution.py:18
  340.8 8.5 %collective-permute-start.11 = (f32[32,2,1,1026]{3,2,1,0:T(1,128)S(1)}, f32[32,2,1,1026]{3,2,1,0:T(1,128)}, u32[]{:S(2)}, u32[]{:S(2)}) collective-permute-start(f32[32,2,1,1026]{3,2,1,0:T(1,128)S(1)} %get-tuple-element.1106), channel_id=1, source_target_pairs={{0,1},{1,2},{2,3},{3,4},{4,5},{5,6},{6,7},{7,8},{8,9},{9,10},{10,1... | collective-permute-start | bytes 787976 | tf_op jit(solution)/shard_map/ppermute | solution.py:17
where the time goes:
time: 589 us; the launch traced here: 587 us
  other arithmetic  301 us (51%)
  local copies, waits for them, and re-layouts  114 us (19%)
  blocking collectives  89.7 us (15%)
  starting transfers between devices  37 us (6%)
  waiting for transfers between devices  26.8 us (5%)
  loops' own time  17.2 us (3%)
    div x672, other arithmetic, advance(): field = (rhs + neighbour_sum(field, inner, vertical)) / diagonal  181 us
    psum x1, blocking collectives, sweep_total(): return lax.psum(squares, ('rows', 'cols'))  89.7 us
    slice x1536, local copies, waits for them, and re-layouts, shifted(): kept = lax.slice_in_dim(field, 1, length, axis=axis)  85.3 us
    dynamic_update_slice x96, other arithmetic, local(): first, wave = lax.scan(advance, zeros, (forcing, cross), reverse=True)  75.1 us
    ppermute x6, starting transfers between devices, extended(): before = lax.ppermute(last, axis, up)  27.4 us
    add x2, other arithmetic, cross_terms(): total + outer[2] * framed[:, :, 1:-1, 2:]  23.3 us
    another operation x3, loops' own time, local(): first, wave = lax.scan(advance, zeros, (forcing, cross), reverse=True)  17.2 us
    ppermute x6, waiting for transfers between devices, extended(): after = lax.ppermute(leading, axis, down)  15 us
  transfers between devices with their start and end apart: 12, of which 10 were waited for; matrix products, arithmetic and copies ran while one was open for 0% of the time, Pallas kernels for 0%

commit v1 on v0

v1 whole, which is shorter than its diff:
```python
import functools
import math

import jax
import jax.numpy as jnp
from jax import lax
from jax.experimental import pallas as pl
from jax.experimental.pallas import tpu as pltpu
from jax.sharding import PartitionSpec as P

PASSES = 8
SWEEPS = 3
F32 = jnp.float32
BF16 = jnp.bfloat16
VMEM_LIMIT = 56 * 2**20

CELLS = [(a, h, j) for a in range(2) for h in range(2) for j in range(8)]
GHOSTS = [(a, h, j) for a in range(2) for h in range(2) for j in (-1, 8)]
WIDE = CELLS + GHOSTS
CP, CM, RP, RM, VV = range(5)


def home(p):
    return (p[0], p[1], p[2] % 8)


def colour(p):
    return sum(p) % 2


UNIT = set()
for _a in range(2):
    for _h in range(2):
        for _j in range(8):
            if _j > 3:
                UNIT.add((RM, (_a, _h, _j)))
            if _j < 3:
                UNIT.add((RP, (_a, _h, _j)))
    UNIT.add((CM, (_a, 1, 3)))
UNIT.add((VV, (1, 0, 3)))

AT = {p: i for i, p in enumerate(WIDE)}
KEYS = [("w", d, p) for p in WIDE for d in range(5) if (d, home(p)) not in UNIT]
KEYS += [("e", 0, p) for p in WIDE]
KEYS += [("alpha", 0, p) for p in CELLS]
KEYS += [("cap", 0, p) for p in CELLS]
KEYS += [("g", 0, p) for p in CELLS]
KEYS += [("oc", side, a) for side in range(2) for a in range(2)]
KEYS += [("or", side, q) for side in range(2) for q in range(4)]
COEF = {k: i for i, k in enumerate(KEYS)}


def lanes():
    return lax.broadcasted_iota(jnp.int32, (8, 128), 1)


def sublanes():
    return lax.broadcasted_iota(jnp.int32, (8, 128), 0)


def neighbour(x, p, d, cache):
    a, h, j = p

    def turned(source, shift):
        key = (source, shift)
        if key not in cache:
            cache[key] = pltpu.roll(x[source], shift, 0)
        return cache[key]

    if d == VV:
        return x[(1 - a, h, j)]
    if d == CP:
        return x[(a, 1, j)] if h == 0 else turned((a, 0, j), 7)
    if d == CM:
        return x[(a, 0, j)] if h == 1 else turned((a, 1, j), 1)
    return x[(a, h, j + 1)] if d == RP else x[(a, h, j - 1)]


def permutation(to_cells):
    size = 1024
    first = lax.broadcasted_iota(jnp.int32, (size, size), 0)
    second = lax.broadcasted_iota(jnp.int32, (size, size), 1)
    row, place = (first, second) if to_cells else (second, first)
    return jnp.where(row == 8 * (place % 128) + place // 128, 1.0, 0.0).astype(BF16)


def permute_rows(x, matrix):
    high = x.astype(BF16)
    low = (x - high.astype(F32)).astype(BF16)
    return jnp.dot(high, matrix, preferred_element_type=F32) + jnp.dot(low, matrix, preferred_element_type=F32)


def materials_kernel(cap_t, con_t, sink_t, material, cap_o, con_o, sink_o, low_o, high_o, held):
    kinds = material[...].reshape(32, 1024).astype(F32).astype(BF16)
    moved = jnp.dot(kinds, permutation(True), preferred_element_type=F32)
    for j in range(8):
        held[j] = moved[:, j * 128 : (j + 1) * 128]
    for p in CELLS:
        a, h, j = p
        kind = held[j, pl.ds(a * 16 + h, 8, stride=2), :]
        values = [jnp.full((8, 128), t[0], F32) for t in (cap_t, con_t, sink_t)]
        for m in range(1, 8):
            hit = kind > m - 0.5
            values = [jnp.where(hit, t[m], v) for t, v in zip((cap_t, con_t, sink_t), values)]
        i = AT[p]
        cap_o[i], con_o[pl.ds(i * 8, 8), :], sink_o[i] = values
    for a in range(2):
        low_o[a] = con_o[pl.ds(a * 128, 8, stride=8), :]
        high_o[a] = con_o[pl.ds(a * 128 + 64 + 7, 8, stride=8), :]


def forcing_kernel(forcing, out, matrix):
    @pl.when(pl.program_id(0) == 0)
    def _():
        matrix[...] = permutation(True)

    rows = forcing.shape[0] * 32
    moved = permute_rows(forcing[...].reshape(rows, 1024), matrix[...])
    for j in range(8):
        out[j] = moved[:, j * 128 : (j + 1) * 128]


def coefficients(place, sizes, cap, con, sink, con_low, con_high, row_low, row_high, co):
    n_cols, n_rows = sizes
    k = {p: con[pl.ds(AT[p] * 8, 8), :] for p in CELLS}
    edge_in = {}
    edge_out = {}
    lane, sub = lanes(), sublanes()

    def couple(x, y):
        return 2.0 * x * y / (x + y)

    weight = {}
    inverse = {}
    for p in CELLS:
        a, h, j = p
        q = a * 2 + h
        others = []
        if h == 0:
            others.append((k[(a, 1, j)], None))
            left = jnp.broadcast_to(con_low[a, pl.ds(j, 1), :], (8, 128))
            others.append((jnp.where(sub == 0, left, pltpu.roll(k[(a, 1, j)], 1, 0)), sub == 0))
        else:
            right = jnp.broadcast_to(con_high[a, pl.ds(j, 1), :], (8, 128))
            others.append((jnp.where(sub == 7, right, pltpu.roll(k[(a, 0, j)], 7, 0)), sub == 7))
            others.append((k[(a, 0, j)], None))
        if j < 7:
            others.append((k[(a, h, j + 1)], None))
        else:
            after = jnp.where(lane == 127, pltpu.roll(row_high[q], 127, 1), pltpu.roll(k[(a, h, 0)], 127, 1))
            others.append((after, lane == 127))
        if j > 0:
            others.append((k[(a, h, j - 1)], None))
        else:
            before = jnp.where(lane == 0, pltpu.roll(row_low[q], 1, 1), pltpu.roll(k[(a, h, 7)], 1, 1))
            others.append((before, lane == 0))
        others.append((k[(1 - a, h, j)], None))
        edges = [couple(k[p], other) for other, _ in others]
        capacity = cap[AT[p]]
        diagonal = capacity + sink[AT[p]]
        for e in edges:
            diagonal = diagonal + e
        inverse[p] = 1.0 / diagonal
        for d, (e, (_, mask)) in enumerate(zip(edges, others)):
            e = e * inverse[p]
            edge_in[d, p] = e if mask is None else jnp.where(mask, 0.0, e)
            edge_out[d, p] = None if mask is None else jnp.where(mask, e, 0.0)
    alpha = {(0, 0, 3): jnp.ones((8, 128), F32)}
    alpha[(1, 0, 3)] = edge_in[VV, (1, 0, 3)] * alpha[(0, 0, 3)]
    for a in range(2):
        alpha[(a, 1, 3)] = edge_in[CM, (a, 1, 3)] * alpha[(a, 0, 3)]
        for h in range(2):
            for j in range(4, 8):
                alpha[(a, h, j)] = edge_in[RM, (a, h, j)] * alpha[(a, h, j - 1)]
            for j in (2, 1, 0):
                alpha[(a, h, j)] = edge_in[RP, (a, h, j)] * alpha[(a, h, j + 1)]
    for a in range(2):
        for h in range(2):
            alpha[(a, h, -1)] = pltpu.roll(alpha[(a, h, 7)], 1, 1)
            alpha[(a, h, 8)] = pltpu.roll(alpha[(a, h, 0)], 127, 1)

    def put(kind, d, p, value):
        co[COEF[(kind, d, p)]] = value

    cache = {}
    column0 = (place[1] * 16).astype(F32)
    row0 = (place[0] * 1024).astype(F32)
    scaled_out = {}
    for p in CELLS:
        a, h, j = p
        over = 1.0 / alpha[p]
        put("alpha", 0, p, alpha[p])
        put("cap", 0, p, cap[AT[p]] * alpha[p])
        e = cap[AT[p]] * inverse[p] - 1.0
        put("e", 0, p, e)
        column = (2 * sub + h).astype(F32) + column0
        row = (8 * lane + j).astype(F32) + row0
        profile = jnp.exp(math.log(3.0) * (column * (1.0 / n_cols) + row * (1.0 / n_rows)))
        put("g", 0, p, profile * inverse[p] * over)
        if j == 7:
            put("e", 0, (a, h, -1), pltpu.roll(e, 1, 1))
        if j == 0:
            put("e", 0, (a, h, 8), pltpu.roll(e, 127, 1))
        for d in range(5):
            if edge_out[d, p] is not None:
                scaled_out[d, p] = edge_out[d, p] * over
            if (d, p) in UNIT:
                continue
            w = edge_in[d, p] * neighbour(alpha, p, d, cache) * over
            put("w", d, p, w)
            if j == 7:
                put("w", d, (a, h, -1), pltpu.roll(w, 1, 1))
            if j == 0:
                put("w", d, (a, h, 8), pltpu.roll(w, 127, 1))
    for a in range(2):
        low, high = jnp.zeros((8, 128), F32), jnp.zeros((8, 128), F32)
        for j in range(8):
            low = jnp.where(sub == j, jnp.broadcast_to(scaled_out[CM, (a, 0, j)][0:1], (8, 128)), low)
            high = jnp.where(sub == j, jnp.broadcast_to(scaled_out[CP, (a, 1, j)][7:8], (8, 128)), high)
        put("oc", 0, a, low)
        put("oc", 1, a, high)
        for h in range(2):
            put("or", 0, a * 2 + h, scaled_out[RM, (a, h, 0)])
            put("or", 1, a * 2 + h, scaled_out[RP, (a, h, 7)])


def time_step(now, source, extra, co, y, d_ref, t_ref):
    def weight(d, p):
        return co[COEF[("w", d, p)]]

    def load(p):
        return y[pl.ds(AT[p] * 8, 8), :]

    def applied(x, p, cache):
        total = None
        for d in (VV, CP, CM, RP, RM):
            term = neighbour(x, p, d, cache)
            if (d, home(p)) not in UNIT:
                term = weight(d, p) * term
            total = term if total is None else total + term
        return total

    def add_ghosts(x):
        for a, h, j in list(x):
            if j >= 6:
                x[(a, h, j - 8)] = pltpu.roll(x[(a, h, j)], 1, 1)
            if j <= 1:
                x[(a, h, j + 8)] = pltpu.roll(x[(a, h, j)], 127, 1)

    start = [{p: load(p) for p in CELLS if colour(p) == c} for c in range(2)]
    for c in range(2):
        add_ghosts(start[c])
    fields = [dict(start[0]), dict(start[1])]
    done = {}
    for k in range(1, PASSES + 1):
        fresh = [None, None]
        for chain in range(2):
            x = fields[chain]
            to = (chain + k) % 2
            wide = k % 2 == 1
            if wide and k > 1:
                add_ghosts(x)
            cache = {}
            out = {}
            for p in WIDE if wide else CELLS:
                if colour(p) != to:
                    continue
                value = applied(x, p, cache)
                slot = pl.ds(AT[p] * 8, 8)
                if k == 1:
                    base = source(p) + co[COEF[("e", 0, p)]] * start[to][p]
                    if extra is not None and p in extra:
                        base = base + extra[p]
                    value = value + base
                    d_ref[slot, :] = value
                elif k == 5:
                    value = value + d_ref[slot, :]
                    t_ref[slot, :] = value
                elif k == 7:
                    value = value + t_ref[slot, :]
                    d_ref[slot, :] = value
                out[p] = value
            fresh[chain] = out
        fields = fresh
    for p in CELLS:
        slot = pl.ds(AT[p] * 8, 8)
        done[p] = fields[colour(p)][p] + (d_ref[slot, :] + load(p))
    return done


def sweep_kernel(first, last, sizes, *refs):
    refs = list(refs)
    if first:
        (place, cap, con, sink, con_low, con_high, row_low, row_high, forcing) = refs[:9]
        co = refs[9]
        refs = refs[10:]
        coefficients(place, sizes, cap, con, sink, con_low, con_high, row_low, row_high, co)
    else:
        (co, sum_in, final_in, square_in, got_low, got_high, got_row_low, got_row_high) = refs[:8]
        refs = refs[8:]
    if last:
        (start_o, mean_o, square_o, y, d_ref, t_ref, f_ref, sums, squares, held) = refs
    else:
        (sum_o, final_o, square_o, low_o, high_o, row_low_o, row_high_o) = refs[:7]
        (y, d_ref, t_ref, f_ref, sums, squares, rows_ref) = refs[7:]
    steps = 32
    y[...] = jnp.zeros_like(y)
    squares[...] = jnp.zeros_like(squares)
    if first:
        sums[...] = jnp.zeros_like(sums)
    else:
        sums[...] = sum_in[...]
        f_ref[...] = jnp.zeros_like(f_ref)
    if not last:
        rows_ref[...] = jnp.zeros_like(rows_ref)
    lane = lanes()

    def body(i, carry):
        now = steps - 1 - i
        extra = None
        if first:
            memo = {}

            def source(p):
                a, h, j = home(p)
                if (a, h, j) not in memo:
                    rows = pl.ds(now * 32 + a * 16 + h, 8, stride=2)
                    memo[(a, h, j)] = forcing[j, rows, :] * co[COEF[("g", 0, (a, h, j))]]
                value = memo[(a, h, j)]
                if p[2] == -1:
                    value = pltpu.roll(value, 1, 1)
                if p[2] == 8:
                    value = pltpu.roll(value, 127, 1)
                return value

        else:
            extra = {}
            for side, got in enumerate((got_low, got_high)):
                for a in range(2):
                    value = got[now, a] * co[COEF[("oc", side, a)]]
                    base = (a * 2 + side) * 64
                    s = 7 * side
                    f_ref[pl.ds(base + s, 8, stride=8), :] = value
                    f_ref[pl.ds(AT[(a, side, -1)] * 8 + s, 1), :] = pltpu.roll(value, 1, 1)[7:8]
                    f_ref[pl.ds(AT[(a, side, 8)] * 8 + s, 1), :] = pltpu.roll(value, 127, 1)[0:1]
            for q in range(4):
                a, h = q // 2, q % 2
                spot = q * 32 + now
                extra[(a, h, 0)] = co[COEF[("or", 0, q)]] * pltpu.roll(got_row_low[...], (128 - spot) % 128, 1)
                extra[(a, h, 7)] = co[COEF[("or", 1, q)]] * pltpu.roll(got_row_high[...], 127 - spot, 1)

            def source(p):
                return f_ref[pl.ds(AT[p] * 8, 8), :]

        done = time_step(now, source, extra, co, y, d_ref, t_ref)
        for p in CELLS:
            i_p = AT[p]
            x = done[p]
            y[pl.ds(i_p * 8, 8), :] = x
            sums[i_p] += x
            squares[i_p] += x * x
        if not last:
            for a in range(2):
                low_o[now, a] = y[pl.ds(a * 128, 8, stride=8), :]
                high_o[now, a] = y[pl.ds(a * 128 + 64 + 7, 8, stride=8), :]
            lows, highs = rows_ref[0], rows_ref[1]
            for q in range(4):
                a, h = q // 2, q % 2
                spot = q * 32 + now
                lows = jnp.where(lane == spot, pltpu.roll(done[(a, h, 0)], spot, 1), lows)
                highs = jnp.where(lane == spot, pltpu.roll(done[(a, h, 7)], (spot + 1) % 128, 1), highs)
            rows_ref[0] = lows
            rows_ref[1] = highs
        return carry

    lax.fori_loop(0, steps, body, 0)

    def alpha(p):
        return co[COEF[("alpha", 0, p)]]

    total = jnp.zeros((8, 128), F32)
    for p in CELLS:
        total = total + squares[AT[p]] * (alpha(p) * alpha(p))
    total = jnp.sum(jnp.sum(total, axis=1, keepdims=True), axis=0, keepdims=True)
    spread = jnp.broadcast_to(total, (8, 128))
    if first:
        square_o[...] = jnp.where(lane == 0, spread, 0.0)
    else:
        square_o[...] = jnp.where(lane == (2 if last else 1), spread, square_in[...])
    if not last:
        sub = sublanes()
        sum_o[...] = sums[...]
        final = y[...].reshape(32, 8, 128)
        final_o[...] = final if first else final + final_in[...]
        scale = {}
        for side in range(2):
            for a in range(2):
                compact = jnp.zeros((8, 128), F32)
                for j in range(8):
                    row = alpha((a, side, j))[7 * side : 7 * side + 1]
                    compact = jnp.where(sub == j, jnp.broadcast_to(row, (8, 128)), compact)
                out = high_o if side else low_o
                for n in range(steps):
                    out[n, a] = out[n, a] * compact
            spread_row = jnp.zeros((8, 128), F32)
            for q in range(4):
                a, h = q // 2, q % 2
                one = alpha((a, h, 7 * side))
                one = one[:, 127:128] if side else one[:, 0:1]
                spread_row = jnp.where(lane // 32 == q, jnp.broadcast_to(one, (8, 128)), spread_row)
            out = row_high_o if side else row_low_o
            out[...] = rows_ref[side] * spread_row
    else:
        matrix = permutation(False)
        for which, out in ((0, start_o), (1, mean_o)):
            for p in CELLS:
                a, h, j = p
                i_p = AT[p]
                if which == 0:
                    value = (final_in[i_p] + y[pl.ds(i_p * 8, 8), :]) * co[COEF[("cap", 0, p)]]
                else:
                    value = sums[i_p] * alpha(p) * (1.0 / steps)
                held[j, pl.ds(a * 16 + h, 8, stride=2), :] = value
            whole = jnp.concatenate([held[j] for j in range(8)], axis=1)
            out[...] = permute_rows(whole, matrix).reshape(2, 16, 1024)


def struct(*shape):
    return jax.ShapeDtypeStruct(shape, F32)


VM = pl.BlockSpec(memory_space=pltpu.VMEM)
SM = pl.BlockSpec(memory_space=pltpu.SMEM)
PARAMS = pltpu.CompilerParams(vmem_limit_bytes=VMEM_LIMIT)


def call(kernel, in_specs, outs, scratch):
    return pl.pallas_call(
        kernel,
        out_shape=outs,
        in_specs=in_specs,
        out_specs=[VM] * len(outs),
        scratch_shapes=scratch,
        compiler_params=PARAMS,
    )


CELL = struct(32, 8, 128)


def scratch_for(last):
    shared = [
        pltpu.VMEM((256, 128), F32),
        pltpu.VMEM((320, 128), F32),
        pltpu.VMEM((320, 128), F32),
        pltpu.VMEM((320, 128), F32),
        pltpu.VMEM((32, 8, 128), F32),
        pltpu.VMEM((32, 8, 128), F32),
    ]
    return shared + [pltpu.VMEM((8, 32, 128), F32) if last else pltpu.VMEM((2, 8, 128), F32)]


BORDERS = [struct(32, 2, 8, 128), struct(32, 2, 8, 128), struct(8, 128), struct(8, 128)]


def exchange(low, high, row_low, row_high):
    n_cols, n_rows = lax.axis_size("cols"), lax.axis_size("rows")
    cols_up = [(i, i + 1) for i in range(n_cols - 1)]
    cols_down = [(i + 1, i) for i in range(n_cols - 1)]
    rows_up = [(i, i + 1) for i in range(n_rows - 1)]
    rows_down = [(i + 1, i) for i in range(n_rows - 1)]
    from_low = lax.ppermute(high, "cols", cols_up)
    from_high = lax.ppermute(low, "cols", cols_down)
    from_row_low = lax.ppermute(row_high, "rows", rows_up)
    from_row_high = lax.ppermute(row_low, "rows", rows_down)
    return from_low, from_high, from_row_low, from_row_high


def everywhere(x, axis):
    count = lax.axis_size(axis)
    spread = jnp.broadcast_to(x[None], (count,) + x.shape)
    return jnp.sum(lax.all_to_all(spread, axis, 0, 0), axis=0)


def local(forcing, material, capacity_table, conductance_table, sink_table):
    steps = forcing.shape[0]
    n_cols, n_rows = lax.axis_size("cols"), lax.axis_size("rows")
    sizes = (16 * n_cols, 1024 * n_rows)
    place = jnp.stack([lax.axis_index("rows"), lax.axis_index("cols")]).astype(jnp.int32)
    cap, con, sink, low, high = call(
        materials_kernel,
        [SM, SM, SM, VM],
        [CELL, struct(256, 128), CELL, struct(2, 8, 128), struct(2, 8, 128)],
        [pltpu.VMEM((8, 32, 128), F32)],
    )(capacity_table, conductance_table, sink_table, material)
    grouped = con.reshape(4, 8, 8, 128)
    con_low, con_high, row_low, row_high = exchange(low, high, grouped[:, 0], grouped[:, 7])
    block = 4
    moved = pl.pallas_call(
        forcing_kernel,
        grid=(steps // block,),
        out_shape=struct(8, steps * 32, 128),
        in_specs=[pl.BlockSpec((block, 2, 16, 1024), lambda i: (i, 0, 0, 0))],
        out_specs=pl.BlockSpec((8, block * 32, 128), lambda i: (0, i, 0)),
        scratch_shapes=[pltpu.VMEM((1024, 1024), BF16)],
        compiler_params=PARAMS,
    )(forcing)
    co, sums, final, squares, *borders = call(
        functools.partial(sweep_kernel, True, False, sizes),
        [SM] + [VM] * 8,
        [struct(len(KEYS), 8, 128), CELL, CELL, struct(8, 128)] + BORDERS,
        scratch_for(False),
    )(place, cap, con, sink, con_low, con_high, row_low, row_high, moved)
    sums, final, squares, *borders = call(
        functools.partial(sweep_kernel, False, False, sizes),
        [VM] * 8,
        [CELL, CELL, struct(8, 128)] + BORDERS,
        scratch_for(False),
    )(co, sums, final, squares, *exchange(*borders))
    start, mean, squares = call(
        functools.partial(sweep_kernel, False, True, sizes),
        [VM] * 8,
        [struct(2, 16, 1024), struct(2, 16, 1024), struct(8, 128)],
        scratch_for(True),
    )(co, sums, final, squares, *exchange(*borders))
    summed = everywhere(everywhere(squares[0], "rows"), "cols")[:SWEEPS]
    count = float(steps * 2 * sizes[0] * sizes[1])
    return start, mean, jnp.sqrt(summed / count + 1e-06)


def solution(mesh):
    return jax.shard_map(
        local,
        mesh=mesh,
        in_specs=(P(None, None, "cols", "rows"), P(None, "cols", "rows"), P(), P(), P()),
        out_specs=(P(None, "cols", "rows"), P(None, "cols", "rows"), P()),
        check_vma=False,
    )
```

time: 589 us -> 145 us (0.25)
  other arithmetic: 301 us -> 1.15 us
  local copies, waits for them, and re-layouts: 114 us -> 3.45 us
  Pallas kernels: 0 us -> 68.2 us
  blocking collectives: 89.7 us -> 29.3 us
  waiting for transfers between devices: 26.8 us -> 8.7 us
  loops' own time: 17.2 us -> 0 us
    div x675 -> x0, other arithmetic: 182 us -> none  [the longest x672 181 us: advance(): field = (rhs + neighbour_sum(field, inner, vertical)) / diagonal]
    slice x1542 -> x1, local copies, waits for them, and re-layouts: 93.8 us -> 0.68 us  [local(): summed = everywhere(everywhere(squares[0], 'rows'), 'cols')[:SWEEPS]]
    psum x1 -> x0, blocking collectives: 89.7 us -> none  [sweep_total(): return lax.psum(squares, ('rows', 'cols'))]
    dynamic_update_slice x96 -> x0, other arithmetic: 75.1 us -> none  [local(): first, wave = lax.scan(advance, zeros, (forcing, cross), reverse=True)]
    pallas_call x0 -> x5, Pallas kernels: none -> 68.2 us  [the longest x1 20.2 us: local(): call(functools.partial(sweep_kernel, True, False, sizes), [SM] + [VM] * 8...]
    all_to_all x0 -> x2, blocking collectives: none -> 29.3 us  [everywhere(): return jnp.sum(lax.all_to_all(spread, axis, 0, 0), axis=0)]
    add x2 -> x0, other arithmetic: 23.3 us -> none  [cross_terms(): total + outer[2] * framed[:, :, 1:-1, 2:]]
    ppermute x12, waiting for transfers between devices: 26.8 us -> 8.7 us  [the longest x3 6.97 us: exchange(): from_row_high = lax.ppermute(row_low, 'rows', rows_down)]
  transfers between devices with their start and end apart: 12 -> 12, of which waited for: 10 -> 4; matrix products, arithmetic and copies ran while one was open for 0% -> 1% of each run, Pallas kernels for 0% -> 7%
where the time goes in v1:
time: 145 us
  Pallas kernels  68.2 us (47%)
  starting transfers between devices  33.1 us (23%)
  blocking collectives  29.3 us (20%)
  waiting for transfers between devices  8.7 us (6%)
  local copies, waits for them, and re-layouts  3.45 us (2%)
    all_to_all x2, blocking collectives, everywhere(): return jnp.sum(lax.all_to_all(spread, axis, 0, 0), axis=0)  29.3 us
    pallas_call x1, Pallas kernels, local(): call(functools.partial(sweep_kernel, True, False, sizes), [SM] + [VM] * 8...  20.2 us
    pallas_call x1, Pallas kernels, local(): call(functools.partial(sweep_kernel, False, False, sizes), [VM] * 8, [CEL...  18.4 us
    pallas_call x1, Pallas kernels, local(): call(functools.partial(sweep_kernel, False, True, sizes), [VM] * 8, [stru...  17.6 us
    ppermute x3, starting transfers between devices, exchange(): from_low = lax.ppermute(high, 'cols', cols_up)  13.1 us
    pallas_call x1, Pallas kernels, local(): pl.pallas_call(forcing_kernel, grid=(steps // block,), out_shape=struct(8...  9.71 us
    ppermute x3, starting transfers between devices, exchange(): from_row_low = lax.ppermute(row_high, 'rows', rows_up)  9.37 us
    ppermute x3, waiting for transfers between devices, exchange(): from_row_high = lax.ppermute(row_low, 'rows', rows_down)  6.97 us
  transfers between devices with their start and end apart: 12, of which 4 were waited for; matrix products, arithmetic and copies ran while one was open for 1% of the time, Pallas kernels for 7%

profile of v1, /device:TPU:1, one launch (start us, length us, event | category | flops | bytes accessed | tf_op | source)
XLA Modules:
  0.0 144.7 jit_solution(5775163145546576568)
XLA Ops:
  0.6 2.2 %shard_map.76 = (f32[32,8,128]{2,1,0:T(8,128)}, f32[256,128]{1,0:T(8,128)}, f32[32,8,128]{2,1,0:T(8,128)}, f32[2,8,128]{2,1,0:T(8,128)}, f32[2,8,128]{2,1,0:T(8,128)}) custom-call(f32[8]{0:T(128)} %cap_t.1, f32[8]{0:T(128)} %con_t.1, f32[8]{0:T(128)} %sink_t.1, s32[2,16,1024]{2,1,0:T(8,128)} %material.1), custom_call_target="tpu_custom_call" | custom-call | tf_op jit(solution)/shard_map/pallas_call | solution.py:490
  2.9 4.4 %collective-permute-start = (f32[2,8,128]{2,1,0:T(8,128)}, f32[2,8,128]{2,1,0:T(8,128)S(1)}, u32[]{:S(2)}, u32[]{:S(2)}) collective-permute-start(f32[2,8,128]{2,1,0:T(8,128)} %get-tuple-element.29), channel_id=1, source_target_pairs={{0,1},{1,2},{2,3},{3,4},{4,5},{5,6},{6,7},{7,8},{8,9},{9,10},{10,1... | collective-permute-start | bytes 24584 | tf_op jit(solution)/shard_map/ppermute | solution.py:472
  7.2 1.3 collective-permute-start.1
  8.5 0.7 slice_bitcast_fusion
  9.3 2.9 %collective-permute-start.3 = (f32[4,8,128]{2,1,0:T(8,128)S(1)}, f32[4,8,128]{2,1,0:T(8,128)S(1)}, u32[]{:S(2)}, u32[]{:S(2)}) collective-permute-start(f32[4,8,128]{2,1,0:T(8,128)S(1)} %get-tuple-element.49), channel_id=1, source_target_pairs={{32,0},{64,32},{96,64},{128,96},{160,128},{192,160},{224,192},{33,... | collective-permute-start | bytes 49160 | tf_op jit(solution)/shard_map/ppermute | solution.py:475
  12.1 3.0 %collective-permute-start.2 = (f32[4,8,128]{2,1,0:T(8,128)S(1)}, f32[4,8,128]{2,1,0:T(8,128)S(1)}, u32[]{:S(2)}, u32[]{:S(2)}) collective-permute-start(f32[4,8,128]{2,1,0:T(8,128)S(1)} %get-tuple-element.50), channel_id=1, source_target_pairs={{0,32},{32,64},{64,96},{96,128},{128,160},{160,192},{192,224},{1,3... | collective-permute-start | bytes 49160 | tf_op jit(solution)/shard_map/ppermute | solution.py:474
  15.8 9.7 %shard_map.77.refs_8_ = f32[8,1024,128]{2,1,0:T(8,128)} custom-call(f32[32,2,16,1024]{3,2,1,0:T(8,128)} %forcing.1), custom_call_target="tpu_custom_call" | custom-call | tf_op jit(solution)/shard_map/pallas_call | solution.py:499
  26.1 20.2 %shard_map.78 = (f32[309,8,128]{2,1,0:T(8,128)}, f32[32,8,128]{2,1,0:T(8,128)}, f32[32,8,128]{2,1,0:T(8,128)}, f32[8,128]{1,0:T(8,128)}, f32[32,2,8,128]{3,2,1,0...) custom-call(s32[2]{0:T(128)} %pad_add_fusion.refs_0_, ...), custom_call_target="tpu_custom_call" | custom-call | tf_op jit(solution)/shard_map/pallas_call | solution.py:508
  46.4 4.3 %collective-permute-start.4 = (f32[32,2,8,128]{3,2,1,0:T(8,128)}, f32[32,2,8,128]{3,2,1,0:T(8,128)S(1)}, u32[]{:S(2)}, u32[]{:S(2)}) collective-permute-start(f32[32,2,8,128]{3,2,1,0:T(8,128)} %get-tuple-element.35), channel_id=1, source_target_pairs={{0,1},{1,2},{2,3},{3,4},{4,5},{5,6},{6,7},{7,8},{8,9},{9,10},{10,1... | collective-permute-start | bytes 786440 | tf_op jit(solution)/shard_map/ppermute | solution.py:472
  50.6 1.3 collective-permute-start.5
  51.9 2.7 %collective-permute-start.6 = (f32[8,128]{1,0:T(8,128)}, f32[8,128]{1,0:T(8,128)S(1)}, u32[]{:S(2)}, u32[]{:S(2)}) collective-permute-start(f32[8,128]{1,0:T(8,128)} %get-tuple-element.37), channel_id=1, source_target_pairs={{0,32},{32,64},{64,96},{96,128},{128,160},{160,192},{192,224},{1,3... | collective-permute-start | bytes 12296 | tf_op jit(solution)/shard_map/ppermute | solution.py:474
  54.6 1.9 %collective-permute-start.7 = (f32[8,128]{1,0:T(8,128)}, f32[8,128]{1,0:T(8,128)S(1)}, u32[]{:S(2)}, u32[]{:S(2)}) collective-permute-start(f32[8,128]{1,0:T(8,128)} %get-tuple-element.38), channel_id=1, source_target_pairs={{32,0},{64,32},{96,64},{128,96},{160,128},{192,160},{224,192},{33,... | collective-permute-start | bytes 12296 | tf_op jit(solution)/shard_map/ppermute | solution.py:475
  56.6 3.5 %collective-permute-done.7.refs_7_ = f32[8,128]{1,0:T(8,128)S(1)} collective-permute-done((f32[8,128]{1,0:T(8,128)}, f32[8,128]{1,0:T(8,128)S(1)}, u32[]{:S(2)}, u32[]{:S(2)}) %collective-permute-start.7) | collective-permute-done | bytes 4128 | tf_op jit(solution)/shard_map/ppermute | solution.py:475
  60.1 1.1 collective-permute-done.5.refs_5_
  61.2 0.7 copy-done.1
  61.9 18.4 %shard_map.79 = (f32[32,8,128]{2,1,0:T(8,128)}, f32[32,8,128]{2,1,0:T(8,128)}, f32[8,128]{1,0:T(8,128)}, f32[32,2,8,128]{3,2,1,0:T(8,128)}, f32[32,2,8,128]{3,2,...) custom-call(f32[309,8,128]{2,1,0:T(8,128)} %get-tuple-element.31.refs_0_, f32[32,8,128]{2,1,0:T(8,128)} %get-tuple-element.32.refs_1_, ...), custom_call_target="tpu_custom_call" | custom-call | tf_op jit(solution)/shard_map/pallas_call | solution.py:514
  80.2 4.5 %collective-permute-start.8 = (f32[32,2,8,128]{3,2,1,0:T(8,128)}, f32[32,2,8,128]{3,2,1,0:T(8,128)S(1)}, u32[]{:S(2)}, u32[]{:S(2)}) collective-permute-start(f32[32,2,8,128]{3,2,1,0:T(8,128)} %get-tuple-element.42), channel_id=1, source_target_pairs={{0,1},{1,2},{2,3},{3,4},{4,5},{5,6},{6,7},{7,8},{8,9},{9,10},{10,1... | collective-permute-start | bytes 786440 | tf_op jit(solution)/shard_map/ppermute | solution.py:472
  84.7 1.3 collective-permute-start.9
  86.0 3.7 %collective-permute-start.10 = (f32[8,128]{1,0:T(8,128)}, f32[8,128]{1,0:T(8,128)S(1)}, u32[]{:S(2)}, u32[]{:S(2)}) collective-permute-start(f32[8,128]{1,0:T(8,128)} %get-tuple-element.44), channel_id=1, source_target_pairs={{0,32},{32,64},{64,96},{96,128},{128,160},{160,192},{192,224},{1,3... | collective-permute-start | bytes 12296 | tf_op jit(solution)/shard_map/ppermute | solution.py:474
  89.7 1.9 %collective-permute-start.11 = (f32[8,128]{1,0:T(8,128)}, f32[8,128]{1,0:T(8,128)S(1)}, u32[]{:S(2)}, u32[]{:S(2)}) collective-permute-start(f32[8,128]{1,0:T(8,128)} %get-tuple-element.45), channel_id=1, source_target_pairs={{32,0},{64,32},{96,64},{128,96},{160,128},{192,160},{224,192},{33,... | collective-permute-start | bytes 12296 | tf_op jit(solution)/shard_map/ppermute | solution.py:475
  91.6 3.5 %collective-permute-done.11.refs_7_ = f32[8,128]{1,0:T(8,128)S(1)} collective-permute-done((f32[8,128]{1,0:T(8,128)}, f32[8,128]{1,0:T(8,128)S(1)}, u32[]{:S(2)}, u32[]{:S(2)}) %collective-permute-start.11) | collective-permute-done | bytes 4128 | tf_op jit(solution)/shard_map/ppermute | solution.py:475
  96.5 17.6 %shard_map.80 = (f32[2,16,1024]{2,1,0:T(8,128)}, f32[2,16,1024]{2,1,0:T(8,128)}, f32[8,128]{1,0:T(8,128)}) custom-call(f32[309,8,128]{2,1,0:T(8,128)} %get-tuple-element.31.refs_0_, f32[32,8,128]{2,1,0:T(8,128)} %get-tuple-element.39.refs_1_, f32[32,8,128]{2,1,0:T(8,128)} %get-tuple-element.40.refs_2_, f32[8,128]{1,0:T(8,128)} %get-tuple-element.41.refs_3_, ...), custom_call_target="tpu_custom_call" | custom-call | tf_op jit(solution)/shard_map/pallas_call | solution.py:520
  114.8 9.7 %all_to_all.12 = f32[8,1,128]{2,1,0:T(1,128)S(1)} all-to-all(f32[8,1,128]{2,1,0:T(1,128)S(1)} %broadcast_in_dim.4), channel_id=1, replica_groups=mesh['rows'=8,'cols'=32] {'rows'}, dimensions={0} | all-to-all | bytes 8192 | tf_op jit(solution)/shard_map/all_to_all | solution.py:482
  124.5 19.6 %all_to_all.13 = f32[32,1,128]{2,1,0:T(1,128)S(1)} all-to-all(f32[32,1,128]{2,1,0:T(1,128)S(1)} %broadcast_in_dim.5), channel_id=1, replica_groups=mesh['rows'=8,'cols'=32] {'cols'}, dimensions={0} | all-to-all | bytes 32768 | tf_op jit(solution)/shard_map/all_to_all | solution.py:482
  (39 shorter events, 3.8 us)
Async XLA Ops:
  2.9 22.6 %collective-permute-start = (f32[2,8,128]{2,1,0:T(8,128)}, f32[2,8,128]{2,1,0:T(8,128)S(1)}, u32[]{:S(2)}, u32[]{:S(2)}) collective-permute-start(f32[2,8,128]{2,1,0:T(8,128)} %get-tuple-element.29), channel_id=1, source_target_pairs={{0,1},{1,2},{2,3},{3,4},{4,5},{5,6},{6,7},{7,8},{8,9},{9,10},{10,1... | collective-permute-start | bytes 24584 | tf_op jit(solution)/shard_map/ppermute | solution.py:472
  7.2 18.2 %collective-permute-start.1 = (f32[2,8,128]{2,1,0:T(8,128)}, f32[2,8,128]{2,1,0:T(8,128)S(1)}, u32[]{:S(2)}, u32[]{:S(2)}) collective-permute-start(f32[2,8,128]{2,1,0:T(8,128)} %get-tuple-element.30), channel_id=1, source_target_pairs={{1,0},{2,1},{3,2},{4,3},{5,4},{6,5},{7,6},{8,7},{9,8},{10,9},{11,1... | collective-permute-start | bytes 24584 | tf_op jit(solution)/shard_map/ppermute | solution.py:473
  9.3 16.2 %collective-permute-start.3 = (f32[4,8,128]{2,1,0:T(8,128)S(1)}, f32[4,8,128]{2,1,0:T(8,128)S(1)}, u32[]{:S(2)}, u32[]{:S(2)}) collective-permute-start(f32[4,8,128]{2,1,0:T(8,128)S(1)} %get-tuple-element.49), channel_id=1, source_target_pairs={{32,0},{64,32},{96,64},{128,96},{160,128},{192,160},{224,192},{33,... | collective-permute-start | bytes 49160 | tf_op jit(solution)/shard_map/ppermute | solution.py:475
  12.1 13.4 %collective-permute-start.2 = (f32[4,8,128]{2,1,0:T(8,128)S(1)}, f32[4,8,128]{2,1,0:T(8,128)S(1)}, u32[]{:S(2)}, u32[]{:S(2)}) collective-permute-start(f32[4,8,128]{2,1,0:T(8,128)S(1)} %get-tuple-element.50), channel_id=1, source_target_pairs={{0,32},{32,64},{64,96},{96,128},{128,160},{160,192},{192,224},{1,3... | collective-permute-start | bytes 49160 | tf_op jit(solution)/shard_map/ppermute | solution.py:474
  25.5 0.6 copy-start.6
  25.5 0.6 copy-start.7
  25.5 0.6 copy-start.4
  25.5 0.6 copy-start.5
  46.4 13.7 %collective-permute-start.4 = (f32[32,2,8,128]{3,2,1,0:T(8,128)}, f32[32,2,8,128]{3,2,1,0:T(8,128)S(1)}, u32[]{:S(2)}, u32[]{:S(2)}) collective-permute-start(f32[32,2,8,128]{3,2,1,0:T(8,128)} %get-tuple-element.35), channel_id=1, source_target_pairs={{0,1},{1,2},{2,3},{3,4},{4,5},{5,6},{6,7},{7,8},{8,9},{9,10},{10,1... | collective-permute-start | bytes 786440 | tf_op jit(solution)/shard_map/ppermute | solution.py:472
  50.6 10.5 %collective-permute-start.5 = (f32[32,2,8,128]{3,2,1,0:T(8,128)}, f32[32,2,8,128]{3,2,1,0:T(8,128)S(1)}, u32[]{:S(2)}, u32[]{:S(2)}) collective-permute-start(f32[32,2,8,128]{3,2,1,0:T(8,128)} %get-tuple-element.36), channel_id=1, source_target_pairs={{1,0},{2,1},{3,2},{4,3},{5,4},{6,5},{7,6},{8,7},{9,8},{10,9},{11,1... | collective-permute-start | bytes 786440 | tf_op jit(solution)/shard_map/ppermute | solution.py:473
  51.9 4.6 %collective-permute-start.6 = (f32[8,128]{1,0:T(8,128)}, f32[8,128]{1,0:T(8,128)S(1)}, u32[]{:S(2)}, u32[]{:S(2)}) collective-permute-start(f32[8,128]{1,0:T(8,128)} %get-tuple-element.37), channel_id=1, source_target_pairs={{0,32},{32,64},{64,96},{96,128},{128,160},{160,192},{192,224},{1,3... | collective-permute-start | bytes 12296 | tf_op jit(solution)/shard_map/ppermute | solution.py:474
  54.6 5.4 %collective-permute-start.7 = (f32[8,128]{1,0:T(8,128)}, f32[8,128]{1,0:T(8,128)S(1)}, u32[]{:S(2)}, u32[]{:S(2)}) collective-permute-start(f32[8,128]{1,0:T(8,128)} %get-tuple-element.38), channel_id=1, source_target_pairs={{32,0},{64,32},{96,64},{128,96},{160,128},{192,160},{224,192},{33,... | collective-permute-start | bytes 12296 | tf_op jit(solution)/shard_map/ppermute | solution.py:475
  56.6 4.6 %copy-start.8 = (f32[8,128]{1,0:T(8,128)}, f32[8,128]{1,0:T(8,128)S(1)}, u32[]{:S(2)}) copy-start(f32[8,128]{1,0:T(8,128)S(1)} %collective-permute-done.6.refs_6_) | copy-start | bytes 12292
  60.1 1.1 copy-start.9
  60.1 1.1 copy-start
  61.2 0.7 copy-start.1
  80.2 14.9 %collective-permute-start.8 = (f32[32,2,8,128]{3,2,1,0:T(8,128)}, f32[32,2,8,128]{3,2,1,0:T(8,128)S(1)}, u32[]{:S(2)}, u32[]{:S(2)}) collective-permute-start(f32[32,2,8,128]{3,2,1,0:T(8,128)} %get-tuple-element.42), channel_id=1, source_target_pairs={{0,1},{1,2},{2,3},{3,4},{4,5},{5,6},{6,7},{7,8},{8,9},{9,10},{10,1... | collective-permute-start | bytes 786440 | tf_op jit(solution)/shard_map/ppermute | solution.py:472
  84.7 11.1 %collective-permute-start.9 = (f32[32,2,8,128]{3,2,1,0:T(8,128)}, f32[32,2,8,128]{3,2,1,0:T(8,128)S(1)}, u32[]{:S(2)}, u32[]{:S(2)}) collective-permute-start(f32[32,2,8,128]{3,2,1,0:T(8,128)} %get-tuple-element.43), channel_id=1, source_target_pairs={{1,0},{2,1},{3,2},{4,3},{5,4},{6,5},{7,6},{8,7},{9,8},{10,9},{11,1... | collective-permute-start | bytes 786440 | tf_op jit(solution)/shard_map/ppermute | solution.py:473
  86.0 5.6 %collective-permute-start.10 = (f32[8,128]{1,0:T(8,128)}, f32[8,128]{1,0:T(8,128)S(1)}, u32[]{:S(2)}, u32[]{:S(2)}) collective-permute-start(f32[8,128]{1,0:T(8,128)} %get-tuple-element.44), channel_id=1, source_target_pairs={{0,32},{32,64},{64,96},{96,128},{128,160},{160,192},{192,224},{1,3... | collective-permute-start | bytes 12296 | tf_op jit(solution)/shard_map/ppermute | solution.py:474
  89.7 5.4 %collective-permute-start.11 = (f32[8,128]{1,0:T(8,128)}, f32[8,128]{1,0:T(8,128)S(1)}, u32[]{:S(2)}, u32[]{:S(2)}) collective-permute-start(f32[8,128]{1,0:T(8,128)} %get-tuple-element.45), channel_id=1, source_target_pairs={{32,0},{64,32},{96,64},{128,96},{160,128},{192,160},{224,192},{33,... | collective-permute-start | bytes 12296 | tf_op jit(solution)/shard_map/ppermute | solution.py:475
  91.6 4.1 %copy-start.10 = (f32[8,128]{1,0:T(8,128)}, f32[8,128]{1,0:T(8,128)S(1)}, u32[]{:S(2)}) copy-start(f32[8,128]{1,0:T(8,128)S(1)} %collective-permute-done.10.refs_6_) | copy-start | bytes 12292
  95.1 0.7 copy-start.11
  95.1 0.7 copy-start.2
  95.8 0.7 copy-start.3

commit v2 on v1

--- a/solution.py
+++ b/solution.py
@@ -40,6 +40,7 @@
 UNIT.add((VV, (1, 0, 3)))
 
 AT = {p: i for i, p in enumerate(WIDE)}
+CELLS_SET = frozenset(CELLS)
 KEYS = [("w", d, p) for p in WIDE for d in range(5) if (d, home(p)) not in UNIT]
 KEYS += [("e", 0, p) for p in WIDE]
 KEYS += [("alpha", 0, p) for p in CELLS]
@@ -77,24 +78,26 @@
 
 
 def permutation(to_cells):
-    size = 1024
-    first = lax.broadcasted_iota(jnp.int32, (size, size), 0)
-    second = lax.broadcasted_iota(jnp.int32, (size, size), 1)
-    row, place = (first, second) if to_cells else (second, first)
-    return jnp.where(row == 8 * (place % 128) + place // 128, 1.0, 0.0).astype(BF16)
-
-
-def permute_rows(x, matrix):
+    first = lax.broadcasted_iota(jnp.int32, (256, 256), 0)
+    second = lax.broadcasted_iota(jnp.int32, (256, 256), 1)
+    row, spot = (first, second) if to_cells else (second, first)
+    return jnp.where(row == 8 * (spot % 32) + spot // 32, 1.0, 0.0).astype(BF16)
+
+
+def permute(x, matrix):
     high = x.astype(BF16)
     low = (x - high.astype(F32)).astype(BF16)
-    return jnp.dot(high, matrix, preferred_element_type=F32) + jnp.dot(low, matrix, preferred_element_type=F32)
-
-
-def materials_kernel(cap_t, con_t, sink_t, material, cap_o, con_o, sink_o, low_o, high_o, held):
+    both = jnp.dot(jnp.concatenate([high, low], axis=0), matrix, preferred_element_type=F32)
+    return both[: x.shape[0]] + both[x.shape[0] :]
+
+
+def materials_kernel(cap_t, con_t, sink_t, material, cap_o, con_o, sink_o, low_o, high_o, row_low_o, row_high_o, held):
     kinds = material[...].reshape(32, 1024).astype(F32).astype(BF16)
-    moved = jnp.dot(kinds, permutation(True), preferred_element_type=F32)
-    for j in range(8):
-        held[j] = moved[:, j * 128 : (j + 1) * 128]
+    matrix = permutation(True)
+    for t in range(4):
+        moved = jnp.dot(kinds[:, t * 256 : (t + 1) * 256], matrix, preferred_element_type=F32)
+        for j in range(8):
+            held[j, :, t * 32 : (t + 1) * 32] = moved[:, j * 32 : (j + 1) * 32]
     for p in CELLS:
         a, h, j = p
         kind = held[j, pl.ds(a * 16 + h, 8, stride=2), :]
@@ -104,25 +107,34 @@
             values = [jnp.where(hit, t[m], v) for t, v in zip((cap_t, con_t, sink_t), values)]
         i = AT[p]
         cap_o[i], con_o[pl.ds(i * 8, 8), :], sink_o[i] = values
+        if j == 0:
+            row_low_o[a * 2 + h] = values[1]
+        if j == 7:
+            row_high_o[a * 2 + h] = values[1]
     for a in range(2):
         low_o[a] = con_o[pl.ds(a * 128, 8, stride=8), :]
         high_o[a] = con_o[pl.ds(a * 128 + 64 + 7, 8, stride=8), :]
 
 
-def forcing_kernel(forcing, out, matrix):
-    @pl.when(pl.program_id(0) == 0)
-    def _():
-        matrix[...] = permutation(True)
-
-    rows = forcing.shape[0] * 32
-    moved = permute_rows(forcing[...].reshape(rows, 1024), matrix[...])
-    for j in range(8):
-        out[j] = moved[:, j * 128 : (j + 1) * 128]
+def bring(step, matrix):
+    pieces = []
+    for t in range(4):
+        x = step[:, :, t * 256 : (t + 1) * 256].reshape(32, 256)
+        high = x.astype(BF16)
+        pieces += [high, (x - high.astype(F32)).astype(BF16)]
+    both = jnp.dot(jnp.concatenate(pieces, axis=0), matrix, preferred_element_type=F32)
+    return [both[t * 64 : t * 64 + 32] + both[t * 64 + 32 : t * 64 + 64] for t in range(4)]
 
 
 def coefficients(place, sizes, cap, con, sink, con_low, con_high, row_low, row_high, co):
     n_cols, n_rows = sizes
     k = {p: con[pl.ds(AT[p] * 8, 8), :] for p in CELLS}
+    row_at, col_at = place
+    one, none = jnp.float32(1.0), jnp.float32(0.0)
+    has_left = jnp.where(col_at > 0, one, none)
+    has_right = jnp.where(col_at < n_cols // 16 - 1, one, none)
+    has_before = jnp.where(row_at > 0, one, none)
+    has_after = jnp.where(row_at < n_rows // 1024 - 1, one, none)
     edge_in = {}
     edge_out = {}
     lane, sub = lanes(), sublanes()
@@ -138,21 +150,21 @@
         others = []
         if h == 0:
             others.append((k[(a, 1, j)], None))
-            left = jnp.broadcast_to(con_low[a, pl.ds(j, 1), :], (8, 128))
+            left = jnp.broadcast_to(con_low[a, pl.ds(j, 1), :], (8, 128)) * has_left
             others.append((jnp.where(sub == 0, left, pltpu.roll(k[(a, 1, j)], 1, 0)), sub == 0))
         else:
-            right = jnp.broadcast_to(con_high[a, pl.ds(j, 1), :], (8, 128))
+            right = jnp.broadcast_to(con_high[a, pl.ds(j, 1), :], (8, 128)) * has_right
             others.append((jnp.where(sub == 7, right, pltpu.roll(k[(a, 0, j)], 7, 0)), sub == 7))
             others.append((k[(a, 0, j)], None))
         if j < 7:
             others.append((k[(a, h, j + 1)], None))
         else:
-            after = jnp.where(lane == 127, pltpu.roll(row_high[q], 127, 1), pltpu.roll(k[(a, h, 0)], 127, 1))
+            after = jnp.where(lane == 127, pltpu.roll(row_high[q], 127, 1) * has_after, pltpu.roll(k[(a, h, 0)], 127, 1))
             others.append((after, lane == 127))
         if j > 0:
             others.append((k[(a, h, j - 1)], None))
         else:
-            before = jnp.where(lane == 0, pltpu.roll(row_low[q], 1, 1), pltpu.roll(k[(a, h, 7)], 1, 1))
+            before = jnp.where(lane == 0, pltpu.roll(row_low[q], 1, 1) * has_before, pltpu.roll(k[(a, h, 7)], 1, 1))
             others.append((before, lane == 0))
         others.append((k[(1 - a, h, j)], None))
         edges = [couple(k[p], other) for other, _ in others]
@@ -183,8 +195,8 @@
         co[COEF[(kind, d, p)]] = value
 
     cache = {}
-    column0 = (place[1] * 16).astype(F32)
-    row0 = (place[0] * 1024).astype(F32)
+    column0 = (col_at * 16).astype(F32)
+    row0 = (row_at * 1024).astype(F32)
     scaled_out = {}
     for p in CELLS:
         a, h, j = p
@@ -224,19 +236,22 @@
             put("or", 1, a * 2 + h, scaled_out[RP, (a, h, 7)])
 
 
-def time_step(now, source, extra, co, y, d_ref, t_ref):
-    def weight(d, p):
-        return co[COEF[("w", d, p)]]
-
-    def load(p):
-        return y[pl.ds(AT[p] * 8, 8), :]
-
-    def applied(x, p, cache):
+SKEW = True
+
+
+def rows_of(p):
+    return pl.ds(AT[p] * 8, 8)
+
+
+def time_step(source, extra, co, held):
+    def applied(x, p, cache, memo):
         total = None
         for d in (VV, CP, CM, RP, RM):
             term = neighbour(x, p, d, cache)
             if (d, home(p)) not in UNIT:
-                term = weight(d, p) * term
+                if d not in memo:
+                    memo[d] = co[COEF[("w", d, p)]]
+                term = memo[d] * term
             total = term if total is None else total + term
         return total
 
@@ -247,64 +262,80 @@
             if j <= 1:
                 x[(a, h, j + 8)] = pltpu.roll(x[(a, h, j)], 127, 1)
 
-    start = [{p: load(p) for p in CELLS if colour(p) == c} for c in range(2)]
+    start = [{p: held[0][rows_of(p), :] for p in CELLS if colour(p) == c} for c in range(2)]
     for c in range(2):
         add_ghosts(start[c])
     fields = [dict(start[0]), dict(start[1])]
-    done = {}
-    for k in range(1, PASSES + 1):
-        fresh = [None, None]
-        for chain in range(2):
-            x = fields[chain]
-            to = (chain + k) % 2
-            wide = k % 2 == 1
-            if wide and k > 1:
-                add_ghosts(x)
-            cache = {}
-            out = {}
-            for p in WIDE if wide else CELLS:
-                if colour(p) != to:
+    lag = 1 if SKEW else 0
+    for stage in range(1, PASSES + 1 + lag):
+        jobs = []
+        for chain in (1, 0):
+            k = stage - chain * lag
+            if 1 <= k <= PASSES:
+                wide = k % 2 == 1
+                if wide and k > 1:
+                    add_ghosts(fields[chain])
+                jobs.append((chain, k, wide, (chain + k) % 2, {}, {}))
+        memos = {}
+        for p in WIDE:
+            for chain, k, wide, to, cache, out in jobs:
+                if colour(p) != to or (not wide and p not in CELLS_SET):
                     continue
-                value = applied(x, p, cache)
-                slot = pl.ds(AT[p] * 8, 8)
+                value = applied(fields[chain], p, cache, memos.setdefault(p, {}))
                 if k == 1:
                     base = source(p) + co[COEF[("e", 0, p)]] * start[to][p]
                     if extra is not None and p in extra:
                         base = base + extra[p]
                     value = value + base
-                    d_ref[slot, :] = value
-                elif k == 5:
-                    value = value + d_ref[slot, :]
-                    t_ref[slot, :] = value
-                elif k == 7:
-                    value = value + t_ref[slot, :]
-                    d_ref[slot, :] = value
+                elif k == 2:
+                    value = value + held[1][rows_of(p), :]
+                elif k == 4:
+                    value = value + held[2][rows_of(p), :]
+                elif k == 8:
+                    value = value + (held[3][rows_of(p), :] + held[0][rows_of(p), :])
+                if k == 1 and p in CELLS_SET:
+                    held[1][rows_of(p), :] = value
+                elif k in (2, 4):
+                    held[k // 2 + 1][rows_of(p), :] = value
                 out[p] = value
-            fresh[chain] = out
-        fields = fresh
-    for p in CELLS:
-        slot = pl.ds(AT[p] * 8, 8)
-        done[p] = fields[colour(p)][p] + (d_ref[slot, :] + load(p))
-    return done
+        for chain, k, wide, to, cache, out in jobs:
+            fields[chain] = out
+    return {**fields[0], **fields[1]}
 
 
 def sweep_kernel(first, last, sizes, *refs):
     refs = list(refs)
     if first:
-        (place, cap, con, sink, con_low, con_high, row_low, row_high, forcing) = refs[:9]
-        co = refs[9]
-        refs = refs[10:]
+        (cap, con, sink, con_low, con_high, row_low, row_high, forcing) = refs[:8]
+        co = refs[8]
+        refs = refs[9:]
+        place = (lax.axis_index("rows"), lax.axis_index("cols"))
+        (matrix, raw, force, arrived) = refs[-4:]
+        refs = refs[:-4]
+        copy = pltpu.make_async_copy(forcing, raw, arrived)
+        copy.start()
+        matrix[...] = permutation(True)
         coefficients(place, sizes, cap, con, sink, con_low, con_high, row_low, row_high, co)
+        copy.wait()
+
+        def fetch(now, slot):
+            for t, block in enumerate(bring(raw[now], matrix[...])):
+                for j in range(8):
+                    force[slot, j, :, t * 32 : (t + 1) * 32] = block[:, j * 32 : (j + 1) * 32]
+
+        fetch(31, 1)
     else:
         (co, sum_in, final_in, square_in, got_low, got_high, got_row_low, got_row_high) = refs[:8]
         refs = refs[8:]
     if last:
-        (start_o, mean_o, square_o, y, d_ref, t_ref, f_ref, sums, squares, held) = refs
+        (start_o, mean_o, square_o, fields, f_ref, sums, squares, held) = refs
     else:
         (sum_o, final_o, square_o, low_o, high_o, row_low_o, row_high_o) = refs[:7]
-        (y, d_ref, t_ref, f_ref, sums, squares, rows_ref) = refs[7:]
+        (fields, f_ref, sums, squares, rows_ref) = refs[7:]
     steps = 32
-    y[...] = jnp.zeros_like(y)
+    fields[...] = jnp.zeros_like(fields)
+    stages = [fields.at[k] for k in range(4)]
+    y = stages[0]
     squares[...] = jnp.zeros_like(squares)
     if first:
         sums[...] = jnp.zeros_like(sums)
@@ -315,8 +346,7 @@
         rows_ref[...] = jnp.zeros_like(rows_ref)
     lane = lanes()
 
-    def body(i, carry):
-        now = steps - 1 - i
+    def one(now, slot):
         extra = None
         if first:
             memo = {}
@@ -324,8 +354,8 @@
             def source(p):
                 a, h, j = home(p)
                 if (a, h, j) not in memo:
-                    rows = pl.ds(now * 32 + a * 16 + h, 8, stride=2)
-                    memo[(a, h, j)] = forcing[j, rows, :] * co[COEF[("g", 0, (a, h, j))]]
+                    rows = pl.ds(a * 16 + h, 8, stride=2)
+                    memo[(a, h, j)] = force[slot, j, rows, :] * co[COEF[("g", 0, (a, h, j))]]
                 value = memo[(a, h, j)]
                 if p[2] == -1:
                     value = pltpu.roll(value, 1, 1)
@@ -352,11 +382,13 @@
             def source(p):
                 return f_ref[pl.ds(AT[p] * 8, 8), :]
 
-        done = time_step(now, source, extra, co, y, d_ref, t_ref)
+        done = time_step(source, extra, co, stages)
+        if first:
+            fetch(jnp.maximum(now - 1, 0), 1 - slot)
         for p in CELLS:
             i_p = AT[p]
             x = done[p]
-            y[pl.ds(i_p * 8, 8), :] = x
+            y[rows_of(p), :] = x
             sums[i_p] += x
             squares[i_p] += x * x
         if not last:
@@ -371,9 +403,13 @@
                 highs = jnp.where(lane == spot, pltpu.roll(done[(a, h, 7)], (spot + 1) % 128, 1), highs)
             rows_ref[0] = lows
             rows_ref[1] = highs
+
+    def body(i, carry):
+        one(steps - 1 - 2 * i, 1)
+        one(steps - 2 - 2 * i, 0)
         return carry
 
-    lax.fori_loop(0, steps, body, 0)
+    lax.fori_loop(0, steps // 2, body, 0)
 
     def alpha(p):
         return co[COEF[("alpha", 0, p)]]
@@ -417,12 +453,13 @@
                 a, h, j = p
                 i_p = AT[p]
                 if which == 0:
-                    value = (final_in[i_p] + y[pl.ds(i_p * 8, 8), :]) * co[COEF[("cap", 0, p)]]
+                    value = (final_in[i_p] + y[rows_of(p), :]) * co[COEF[("cap", 0, p)]]
                 else:
                     value = sums[i_p] * alpha(p) * (1.0 / steps)
                 held[j, pl.ds(a * 16 + h, 8, stride=2), :] = value
-            whole = jnp.concatenate([held[j] for j in range(8)], axis=1)
-            out[...] = permute_rows(whole, matrix).reshape(2, 16, 1024)
+            for t in range(4):
+                piece = jnp.concatenate([held[j, :, t * 32 : (t + 1) * 32] for j in range(8)], axis=1)
+                out[:, :, t * 256 : (t + 1) * 256] = permute(piece, matrix).reshape(2, 16, 256)
 
 
 def struct(*shape):
@@ -450,9 +487,7 @@
 
 def scratch_for(last):
     shared = [
-        pltpu.VMEM((256, 128), F32),
-        pltpu.VMEM((320, 128), F32),
-        pltpu.VMEM((320, 128), F32),
+        pltpu.VMEM((4, 256, 128), F32),
         pltpu.VMEM((320, 128), F32),
         pltpu.VMEM((32, 8, 128), F32),
         pltpu.VMEM((32, 8, 128), F32),
@@ -460,15 +495,21 @@
     return shared + [pltpu.VMEM((8, 32, 128), F32) if last else pltpu.VMEM((2, 8, 128), F32)]
 
 
+FORCING = [
+    pltpu.VMEM((256, 256), BF16),
+    pltpu.VMEM((32, 2, 16, 1024), F32),
+    pltpu.VMEM((2, 8, 32, 128), F32),
+    pltpu.SemaphoreType.DMA,
+]
 BORDERS = [struct(32, 2, 8, 128), struct(32, 2, 8, 128), struct(8, 128), struct(8, 128)]
 
 
 def exchange(low, high, row_low, row_high):
     n_cols, n_rows = lax.axis_size("cols"), lax.axis_size("rows")
-    cols_up = [(i, i + 1) for i in range(n_cols - 1)]
-    cols_down = [(i + 1, i) for i in range(n_cols - 1)]
-    rows_up = [(i, i + 1) for i in range(n_rows - 1)]
-    rows_down = [(i + 1, i) for i in range(n_rows - 1)]
+    cols_up = [(i, (i + 1) % n_cols) for i in range(n_cols)]
+    cols_down = [(j, i) for i, j in cols_up]
+    rows_up = [(i, (i + 1) % n_rows) for i in range(n_rows)]
+    rows_down = [(j, i) for i, j in rows_up]
     from_low = lax.ppermute(high, "cols", cols_up)
     from_high = lax.ppermute(low, "cols", cols_down)
     from_row_low = lax.ppermute(row_high, "rows", rows_up)
@@ -486,31 +527,19 @@
     steps = forcing.shape[0]
     n_cols, n_rows = lax.axis_size("cols"), lax.axis_size("rows")
     sizes = (16 * n_cols, 1024 * n_rows)
-    place = jnp.stack([lax.axis_index("rows"), lax.axis_index("cols")]).astype(jnp.int32)
-    cap, con, sink, low, high = call(
+    cap, con, sink, *facing = call(
         materials_kernel,
         [SM, SM, SM, VM],
-        [CELL, struct(256, 128), CELL, struct(2, 8, 128), struct(2, 8, 128)],
+        [CELL, struct(256, 128), CELL] + [struct(2, 8, 128)] * 2 + [struct(4, 8, 128)] * 2,
         [pltpu.VMEM((8, 32, 128), F32)],
     )(capacity_table, conductance_table, sink_table, material)
-    grouped = con.reshape(4, 8, 8, 128)
-    con_low, con_high, row_low, row_high = exchange(low, high, grouped[:, 0], grouped[:, 7])
-    block = 4
-    moved = pl.pallas_call(
-        forcing_kernel,
-        grid=(steps // block,),
-        out_shape=struct(8, steps * 32, 128),
-        in_specs=[pl.BlockSpec((block, 2, 16, 1024), lambda i: (i, 0, 0, 0))],
-        out_specs=pl.BlockSpec((8, block * 32, 128), lambda i: (0, i, 0)),
-        scratch_shapes=[pltpu.VMEM((1024, 1024), BF16)],
-        compiler_params=PARAMS,
-    )(forcing)
+    con_low, con_high, row_low, row_high = exchange(*facing)
     co, sums, final, squares, *borders = call(
         functools.partial(sweep_kernel, True, False, sizes),
-        [SM] + [VM] * 8,
+        [VM] * 7 + [pl.BlockSpec(memory_space=pl.ANY)],
         [struct(len(KEYS), 8, 128), CELL, CELL, struct(8, 128)] + BORDERS,
-        scratch_for(False),
-    )(place, cap, con, sink, con_low, con_high, row_low, row_high, moved)
+        scratch_for(False) + FORCING,
+    )(cap, con, sink, con_low, con_high, row_low, row_high, forcing)
     sums, final, squares, *borders = call(
         functools.partial(sweep_kernel, False, False, sizes),
         [VM] * 8,

time: 145 us -> 120 us (0.83)
  Pallas kernels: 68.2 us -> 56.1 us
  starting transfers between devices: 33.1 us -> 26 us
  blocking collectives: 29.3 us -> 25 us
    ppermute x3, starting transfers between devices: 3.88 us -> 16 us  [exchange(): from_high = lax.ppermute(low, 'cols', cols_down)]
    ppermute x3, starting transfers between devices: 13.1 us -> 1.07 us  [exchange(): from_low = lax.ppermute(high, 'cols', cols_up)]
    pallas_call x3 -> x2, Pallas kernels: 32.2 us -> 23.1 us  [the longest x1 21 us: local(): call(functools.partial(sweep_kernel, True, False, sizes), [VM] * 7 + [pl....]
    ppermute x3, starting transfers between devices: 6.69 us -> 0.78 us  [exchange(): from_row_high = lax.ppermute(row_low, 'rows', rows_down)]
    all_to_all x2, blocking collectives: 29.3 us -> 25 us  [everywhere(): return jnp.sum(lax.all_to_all(spread, axis, 0, 0), axis=0)]
    ppermute x3, waiting for transfers between devices: 6.97 us -> 5.12 us  [exchange(): from_row_high = lax.ppermute(row_low, 'rows', rows_down)]
    ppermute x3, waiting for transfers between devices: 0.01 us -> 1.83 us  [exchange(): from_row_low = lax.ppermute(row_high, 'rows', rows_up)]
    ppermute x3, waiting for transfers between devices: 1.72 us -> 0.01 us  [exchange(): from_high = lax.ppermute(low, 'cols', cols_down)]
  transfers between devices with their start and end apart: 12 -> 12, of which waited for: 4 -> 5; matrix products, arithmetic and copies ran while one was open for 1% -> 0% of each run, Pallas kernels for 7% -> 0%
where the time goes in v2:
time: 120 us; the launch traced here: 119 us
  Pallas kernels  56.1 us (47%)
  starting transfers between devices  26 us (22%)
  blocking collectives  25 us (21%)
  waiting for transfers between devices  8.21 us (7%)
  local copies, waits for them, and re-layouts  2.84 us (2%)
    all_to_all x2, blocking collectives, everywhere(): return jnp.sum(lax.all_to_all(spread, axis, 0, 0), axis=0)  25 us
    pallas_call x1, Pallas kernels, local(): call(functools.partial(sweep_kernel, True, False, sizes), [VM] * 7 + [pl....  21 us
    pallas_call x1, Pallas kernels, local(): call(functools.partial(sweep_kernel, False, False, sizes), [VM] * 8, [CEL...  17 us
    ppermute x3, starting transfers between devices, exchange(): from_high = lax.ppermute(low, 'cols', cols_down)  16 us
    pallas_call x1, Pallas kernels, local(): call(functools.partial(sweep_kernel, False, True, sizes), [VM] * 8, [stru...  16 us
    ppermute x3, starting transfers between devices, exchange(): from_row_low = lax.ppermute(row_high, 'rows', rows_up)  8.12 us
    ppermute x3, waiting for transfers between devices, exchange(): from_row_high = lax.ppermute(row_low, 'rows', rows_down)  5.12 us
  transfers between devices with their start and end apart: 12, of which 5 were waited for; matrix products, arithmetic and copies ran while one was open for 0% of the time, Pallas kernels for 0%

profile of v2, /device:TPU:1, one launch (start us, length us, event | category | flops | bytes accessed | tf_op | source)
XLA Modules:
  0.0 119.4 jit_solution(12609083570904632859)
XLA Ops:
  0.6 2.1 %shard_map.76 = (f32[32,8,128]{2,1,0:T(8,128)}, f32[256,128]{1,0:T(8,128)}, f32[32,8,128]{2,1,0:T(8,128)}, f32[2,8,128]{2,1,0:T(8,128)}, f32[2,8,128]{2,1,0:T(8,...) custom-call(f32[8]{0:T(128)} %cap_t.1, f32[8]{0:T(128)} %con_t.1, f32[8]{0:T(128)} %sink_t.1, s32[2,16,1024]{2,1,0:T(8,128)} %material.1), custom_call_target="tpu_custom_call" | custom-call | tf_op jit(solution)/shard_map/pallas_call | solution.py:530
  2.7 2.6 %collective-permute-start.2 = (f32[4,8,128]{2,1,0:T(8,128)}, f32[4,8,128]{2,1,0:T(8,128)S(1)}, u32[]{:S(2)}, u32[]{:S(2)}) collective-permute-start(f32[4,8,128]{2,1,0:T(8,128)} %get-tuple-element.33), channel_id=1, source_target_pairs={{0,32},{32,64},{64,96},{96,128},{128,160},{160,192},{192,224},{224... | collective-permute-start | bytes 49160 | tf_op jit(solution)/shard_map/ppermute | solution.py:515
  5.3 0.7 collective-permute-start.3
  6.0 1.0 collective-permute-start
  7.0 6.4 %collective-permute-start.1 = (f32[2,8,128]{2,1,0:T(8,128)}, f32[2,8,128]{2,1,0:T(8,128)S(1)}, u32[]{:S(2)}, u32[]{:S(2)}) collective-permute-start(f32[2,8,128]{2,1,0:T(8,128)} %get-tuple-element.32), channel_id=1, source_target_pairs={{1,0},{2,1},{3,2},{4,3},{5,4},{6,5},{7,6},{8,7},{9,8},{10,9},{11,1... | collective-permute-start | bytes 24584 | tf_op jit(solution)/shard_map/ppermute | solution.py:514
  13.4 1.2 %collective-permute-done.refs_3_ = f32[2,8,128]{2,1,0:T(8,128)S(1)} collective-permute-done((f32[2,8,128]{2,1,0:T(8,128)}, f32[2,8,128]{2,1,0:T(8,128)S(1)}, u32[]{:S(2)}, u32[]{:S(2)}) %collective-permute-start) | collective-permute-done | bytes 8224 | tf_op jit(solution)/shard_map/ppermute | solution.py:513
  14.6 0.6 copy-done.6
  15.2 21.0 %shard_map.77 = (f32[309,8,128]{2,1,0:T(8,128)}, f32[32,8,128]{2,1,0:T(8,128)}, f32[32,8,128]{2,1,0:T(8,128)}, f32[8,128]{1,0:T(8,128)}, f32[32,2,8,128]{3,2,1,0...) custom-call(f32[32,8,128]{2,1,0:T(8,128)} %get-tuple-element.28.refs_0_, ...), custom_call_target="tpu_custom_call" | custom-call | tf_op jit(solution)/shard_map/pallas_call | solution.py:537
  36.4 4.8 %collective-permute-start.5 = (f32[32,2,8,128]{3,2,1,0:T(8,128)}, f32[32,2,8,128]{3,2,1,0:T(8,128)S(1)}, u32[]{:S(2)}, u32[]{:S(2)}) collective-permute-start(f32[32,2,8,128]{3,2,1,0:T(8,128)} %get-tuple-element.40), channel_id=1, source_target_pairs={{1,0},{2,1},{3,2},{4,3},{5,4},{6,5},{7,6},{8,7},{9,8},{10,9},{11,1... | collective-permute-start | bytes 786440 | tf_op jit(solution)/shard_map/ppermute | solution.py:514
  41.2 3.2 %collective-permute-start.6 = (f32[8,128]{1,0:T(8,128)}, f32[8,128]{1,0:T(8,128)S(1)}, u32[]{:S(2)}, u32[]{:S(2)}) collective-permute-start(f32[8,128]{1,0:T(8,128)} %get-tuple-element.41), channel_id=1, source_target_pairs={{0,32},{32,64},{64,96},{96,128},{128,160},{160,192},{192,224},{224... | collective-permute-start | bytes 12296 | tf_op jit(solution)/shard_map/ppermute | solution.py:515
  44.5 0.9 collective-permute-done.6.refs_6_
  45.4 2.6 %collective-permute-done.7.refs_7_ = f32[8,128]{1,0:T(8,128)S(1)} collective-permute-done((f32[8,128]{1,0:T(8,128)}, f32[8,128]{1,0:T(8,128)S(1)}, u32[]{:S(2)}, u32[]{:S(2)}) %collective-permute-start.7) | collective-permute-done | bytes 4128 | tf_op jit(solution)/shard_map/ppermute | solution.py:516
  48.0 0.6 copy-done.9
  48.7 17.0 %shard_map.78 = (f32[32,8,128]{2,1,0:T(8,128)}, f32[32,8,128]{2,1,0:T(8,128)}, f32[8,128]{1,0:T(8,128)}, f32[32,2,8,128]{3,2,1,0:T(8,128)}, f32[32,2,8,128]{3,2,...) custom-call(f32[309,8,128]{2,1,0:T(8,128)} %get-tuple-element.35.refs_0_, f32[32,8,128]{2,1,0:T(8,128)} %get-tuple-element.36.refs_1_, ...), custom_call_target="tpu_custom_call" | custom-call | tf_op jit(solution)/shard_map/pallas_call | solution.py:543
  65.7 4.8 %collective-permute-start.9 = (f32[32,2,8,128]{3,2,1,0:T(8,128)}, f32[32,2,8,128]{3,2,1,0:T(8,128)S(1)}, u32[]{:S(2)}, u32[]{:S(2)}) collective-permute-start(f32[32,2,8,128]{3,2,1,0:T(8,128)} %get-tuple-element.47), channel_id=1, source_target_pairs={{1,0},{2,1},{3,2},{4,3},{5,4},{6,5},{7,6},{8,7},{9,8},{10,9},{11,1... | collective-permute-start | bytes 786440 | tf_op jit(solution)/shard_map/ppermute | solution.py:514
  70.5 2.3 %collective-permute-start.10 = (f32[8,128]{1,0:T(8,128)}, f32[8,128]{1,0:T(8,128)S(1)}, u32[]{:S(2)}, u32[]{:S(2)}) collective-permute-start(f32[8,128]{1,0:T(8,128)} %get-tuple-element.48), channel_id=1, source_target_pairs={{0,32},{32,64},{64,96},{96,128},{128,160},{160,192},{192,224},{224... | collective-permute-start | bytes 12296 | tf_op jit(solution)/shard_map/ppermute | solution.py:515
  72.8 1.0 collective-permute-done.10.refs_6_
  73.8 2.6 %collective-permute-done.11.refs_7_ = f32[8,128]{1,0:T(8,128)S(1)} collective-permute-done((f32[8,128]{1,0:T(8,128)}, f32[8,128]{1,0:T(8,128)S(1)}, u32[]{:S(2)}, u32[]{:S(2)}) %collective-permute-start.11) | collective-permute-done | bytes 4128 | tf_op jit(solution)/shard_map/ppermute | solution.py:516
  76.4 0.6 copy-done.11
  77.2 16.0 %shard_map.79 = (f32[2,16,1024]{2,1,0:T(8,128)}, f32[2,16,1024]{2,1,0:T(8,128)}, f32[8,128]{1,0:T(8,128)}) custom-call(f32[309,8,128]{2,1,0:T(8,128)} %get-tuple-element.35.refs_0_, f32[32,8,128]{2,1,0:T(8,128)} %get-tuple-element.43.refs_1_, f32[32,8,128]{2,1,0:T(8,128)} %get-tuple-element.44.refs_2_, f32[8,128]{1,0:T(8,128)} %get-tuple-element.45.refs_3_, ...), custom_call_target="tpu_custom_call" | custom-call | tf_op jit(solution)/shard_map/pallas_call | solution.py:549
  93.1 0.7 slice_bitcast_fusion
  93.8 9.9 %all_to_all.12 = f32[8,1,128]{2,1,0:T(1,128)S(1)} all-to-all(f32[8,1,128]{2,1,0:T(1,128)S(1)} %broadcast_in_dim.4), channel_id=1, replica_groups=mesh['rows'=8,'cols'=32] {'rows'}, dimensions={0} | all-to-all | bytes 8192 | tf_op jit(solution)/shard_map/all_to_all | solution.py:523
  103.8 15.1 %all_to_all.13 = f32[32,1,128]{2,1,0:T(1,128)S(1)} all-to-all(f32[32,1,128]{2,1,0:T(1,128)S(1)} %broadcast_in_dim.5), channel_id=1, replica_groups=mesh['rows'=8,'cols'=32] {'cols'}, dimensions={0} | all-to-all | bytes 32768 | tf_op jit(solution)/shard_map/all_to_all | solution.py:523
  118.9 0.5 add_sqrt_fusion
  (36 shorter events, 0.8 us)
Async XLA Ops:
  2.7 11.9 %collective-permute-start.2 = (f32[4,8,128]{2,1,0:T(8,128)}, f32[4,8,128]{2,1,0:T(8,128)S(1)}, u32[]{:S(2)}, u32[]{:S(2)}) collective-permute-start(f32[4,8,128]{2,1,0:T(8,128)} %get-tuple-element.33), channel_id=1, source_target_pairs={{0,32},{32,64},{64,96},{96,128},{128,160},{160,192},{192,224},{224... | collective-permute-start | bytes 49160 | tf_op jit(solution)/shard_map/ppermute | solution.py:515
  5.3 9.3 %collective-permute-start.3 = (f32[4,8,128]{2,1,0:T(8,128)}, f32[4,8,128]{2,1,0:T(8,128)S(1)}, u32[]{:S(2)}, u32[]{:S(2)}) collective-permute-start(f32[4,8,128]{2,1,0:T(8,128)} %get-tuple-element.34), channel_id=1, source_target_pairs={{32,0},{64,32},{96,64},{128,96},{160,128},{192,160},{224,192},{0,2... | collective-permute-start | bytes 49160 | tf_op jit(solution)/shard_map/ppermute | solution.py:516
  6.0 8.6 %collective-permute-start = (f32[2,8,128]{2,1,0:T(8,128)}, f32[2,8,128]{2,1,0:T(8,128)S(1)}, u32[]{:S(2)}, u32[]{:S(2)}) collective-permute-start(f32[2,8,128]{2,1,0:T(8,128)} %get-tuple-element.31), channel_id=1, source_target_pairs={{0,1},{1,2},{2,3},{3,4},{4,5},{5,6},{6,7},{7,8},{8,9},{9,10},{10,1... | collective-permute-start | bytes 24584 | tf_op jit(solution)/shard_map/ppermute | solution.py:513
  7.0 7.6 %collective-permute-start.1 = (f32[2,8,128]{2,1,0:T(8,128)}, f32[2,8,128]{2,1,0:T(8,128)S(1)}, u32[]{:S(2)}, u32[]{:S(2)}) collective-permute-start(f32[2,8,128]{2,1,0:T(8,128)} %get-tuple-element.32), channel_id=1, source_target_pairs={{1,0},{2,1},{3,2},{4,3},{5,4},{6,5},{7,6},{8,7},{9,8},{10,9},{11,1... | collective-permute-start | bytes 24584 | tf_op jit(solution)/shard_map/ppermute | solution.py:514
  14.6 0.6 copy-start.6
  14.6 0.6 copy-start.7
  14.6 0.6 copy-start.4
  14.6 0.6 copy-start.5
  36.3 11.6 %collective-permute-start.4 = (f32[32,2,8,128]{3,2,1,0:T(8,128)}, f32[32,2,8,128]{3,2,1,0:T(8,128)S(1)}, u32[]{:S(2)}, u32[]{:S(2)}) collective-permute-start(f32[32,2,8,128]{3,2,1,0:T(8,128)} %get-tuple-element.39), channel_id=1, source_target_pairs={{0,1},{1,2},{2,3},{3,4},{4,5},{5,6},{6,7},{7,8},{8,9},{9,10},{10,1... | collective-permute-start | bytes 786440 | tf_op jit(solution)/shard_map/ppermute | solution.py:513
  36.4 11.6 %collective-permute-start.5 = (f32[32,2,8,128]{3,2,1,0:T(8,128)}, f32[32,2,8,128]{3,2,1,0:T(8,128)S(1)}, u32[]{:S(2)}, u32[]{:S(2)}) collective-permute-start(f32[32,2,8,128]{3,2,1,0:T(8,128)} %get-tuple-element.40), channel_id=1, source_target_pairs={{1,0},{2,1},{3,2},{4,3},{5,4},{6,5},{7,6},{8,7},{9,8},{10,9},{11,1... | collective-permute-start | bytes 786440 | tf_op jit(solution)/shard_map/ppermute | solution.py:514
  41.2 4.2 %collective-permute-start.6 = (f32[8,128]{1,0:T(8,128)}, f32[8,128]{1,0:T(8,128)S(1)}, u32[]{:S(2)}, u32[]{:S(2)}) collective-permute-start(f32[8,128]{1,0:T(8,128)} %get-tuple-element.41), channel_id=1, source_target_pairs={{0,32},{32,64},{64,96},{96,128},{128,160},{160,192},{192,224},{224... | collective-permute-start | bytes 12296 | tf_op jit(solution)/shard_map/ppermute | solution.py:515
  44.4 3.5 %collective-permute-start.7 = (f32[8,128]{1,0:T(8,128)}, f32[8,128]{1,0:T(8,128)S(1)}, u32[]{:S(2)}, u32[]{:S(2)}) collective-permute-start(f32[8,128]{1,0:T(8,128)} %get-tuple-element.42), channel_id=1, source_target_pairs={{32,0},{64,32},{96,64},{128,96},{160,128},{192,160},{224,192},{0,2... | collective-permute-start | bytes 12296 | tf_op jit(solution)/shard_map/ppermute | solution.py:516
  45.4 2.6 %copy-start.8 = (f32[8,128]{1,0:T(8,128)}, f32[8,128]{1,0:T(8,128)S(1)}, u32[]{:S(2)}) copy-start(f32[8,128]{1,0:T(8,128)S(1)} %collective-permute-done.6.refs_6_) | copy-start | bytes 12292
  47.9 0.6 copy-start.9
  47.9 0.7 copy-start
  48.0 0.8 copy-start.1
  65.7 10.7 %collective-permute-start.8 = (f32[32,2,8,128]{3,2,1,0:T(8,128)}, f32[32,2,8,128]{3,2,1,0:T(8,128)S(1)}, u32[]{:S(2)}, u32[]{:S(2)}) collective-permute-start(f32[32,2,8,128]{3,2,1,0:T(8,128)} %get-tuple-element.46), channel_id=1, source_target_pairs={{0,1},{1,2},{2,3},{3,4},{4,5},{5,6},{6,7},{7,8},{8,9},{9,10},{10,1... | collective-permute-start | bytes 786440 | tf_op jit(solution)/shard_map/ppermute | solution.py:513
  65.7 10.7 %collective-permute-start.9 = (f32[32,2,8,128]{3,2,1,0:T(8,128)}, f32[32,2,8,128]{3,2,1,0:T(8,128)S(1)}, u32[]{:S(2)}, u32[]{:S(2)}) collective-permute-start(f32[32,2,8,128]{3,2,1,0:T(8,128)} %get-tuple-element.47), channel_id=1, source_target_pairs={{1,0},{2,1},{3,2},{4,3},{5,4},{6,5},{7,6},{8,7},{9,8},{10,9},{11,1... | collective-permute-start | bytes 786440 | tf_op jit(solution)/shard_map/ppermute | solution.py:514
  70.5 3.3 %collective-permute-start.10 = (f32[8,128]{1,0:T(8,128)}, f32[8,128]{1,0:T(8,128)S(1)}, u32[]{:S(2)}, u32[]{:S(2)}) collective-permute-start(f32[8,128]{1,0:T(8,128)} %get-tuple-element.48), channel_id=1, source_target_pairs={{0,32},{32,64},{64,96},{96,128},{128,160},{160,192},{192,224},{224... | collective-permute-start | bytes 12296 | tf_op jit(solution)/shard_map/ppermute | solution.py:515
  72.8 3.5 %collective-permute-start.11 = (f32[8,128]{1,0:T(8,128)}, f32[8,128]{1,0:T(8,128)S(1)}, u32[]{:S(2)}, u32[]{:S(2)}) collective-permute-start(f32[8,128]{1,0:T(8,128)} %get-tuple-element.49), channel_id=1, source_target_pairs={{32,0},{64,32},{96,64},{128,96},{160,128},{192,160},{224,192},{0,2... | collective-permute-start | bytes 12296 | tf_op jit(solution)/shard_map/ppermute | solution.py:516
  73.8 2.6 %copy-start.10 = (f32[8,128]{1,0:T(8,128)}, f32[8,128]{1,0:T(8,128)S(1)}, u32[]{:S(2)}) copy-start(f32[8,128]{1,0:T(8,128)S(1)} %collective-permute-done.10.refs_6_) | copy-start | bytes 12292
  76.4 0.6 copy-start.11
  76.4 0.7 copy-start.2
  76.4 0.8 copy-start.3

commit v3 on v2

--- a/solution.py
+++ b/solution.py
@@ -1,5 +1,4 @@
 import functools
-import math
 
 import jax
 import jax.numpy as jnp
@@ -12,7 +11,7 @@
 SWEEPS = 3
 F32 = jnp.float32
 BF16 = jnp.bfloat16
-VMEM_LIMIT = 56 * 2**20
+VMEM_LIMIT = 24 * 2**20
 
 CELLS = [(a, h, j) for a in range(2) for h in range(2) for j in range(8)]
 GHOSTS = [(a, h, j) for a in range(2) for h in range(2) for j in (-1, 8)]
@@ -91,7 +90,17 @@
     return both[: x.shape[0]] + both[x.shape[0] :]
 
 
-def materials_kernel(cap_t, con_t, sink_t, material, cap_o, con_o, sink_o, low_o, high_o, row_low_o, row_high_o, held):
+def materials_kernel(*refs):
+    (tables_in, material_in, cap_o, con_o, sink_o, low_o, high_o, row_low_o, row_high_o, held, tables, material) = refs[:12]
+    arrived = refs[12]
+    copies = [
+        pltpu.make_async_copy(tables_in, tables, arrived.at[0]),
+        pltpu.make_async_copy(material_in, material, arrived.at[1]),
+    ]
+    for copy in copies:
+        copy.start()
+    for copy in copies:
+        copy.wait()
     kinds = material[...].reshape(32, 1024).astype(F32).astype(BF16)
     matrix = permutation(True)
     for t in range(4):
@@ -101,10 +110,10 @@
     for p in CELLS:
         a, h, j = p
         kind = held[j, pl.ds(a * 16 + h, 8, stride=2), :]
-        values = [jnp.full((8, 128), t[0], F32) for t in (cap_t, con_t, sink_t)]
+        values = [jnp.full((8, 128), tables[t, 0], F32) for t in range(3)]
         for m in range(1, 8):
             hit = kind > m - 0.5
-            values = [jnp.where(hit, t[m], v) for t, v in zip((cap_t, con_t, sink_t), values)]
+            values = [jnp.where(hit, tables[t, m], v) for t, v in enumerate(values)]
         i = AT[p]
         cap_o[i], con_o[pl.ds(i * 8, 8), :], sink_o[i] = values
         if j == 0:
@@ -195,8 +204,6 @@
         co[COEF[(kind, d, p)]] = value
 
     cache = {}
-    column0 = (col_at * 16).astype(F32)
-    row0 = (row_at * 1024).astype(F32)
     scaled_out = {}
     for p in CELLS:
         a, h, j = p
@@ -205,10 +212,7 @@
         put("cap", 0, p, cap[AT[p]] * alpha[p])
         e = cap[AT[p]] * inverse[p] - 1.0
         put("e", 0, p, e)
-        column = (2 * sub + h).astype(F32) + column0
-        row = (8 * lane + j).astype(F32) + row0
-        profile = jnp.exp(math.log(3.0) * (column * (1.0 / n_cols) + row * (1.0 / n_rows)))
-        put("g", 0, p, profile * inverse[p] * over)
+        put("g", 0, p, inverse[p] * over)
         if j == 7:
             put("e", 0, (a, h, -1), pltpu.roll(e, 1, 1))
         if j == 0:
@@ -310,27 +314,24 @@
         co = refs[8]
         refs = refs[9:]
         place = (lax.axis_index("rows"), lax.axis_index("cols"))
-        (matrix, raw, force, arrived) = refs[-4:]
-        refs = refs[:-4]
-        copy = pltpu.make_async_copy(forcing, raw, arrived)
-        copy.start()
+        (matrix, force) = refs[-2:]
+        refs = refs[:-2]
         matrix[...] = permutation(True)
         coefficients(place, sizes, cap, con, sink, con_low, con_high, row_low, row_high, co)
-        copy.wait()
 
         def fetch(now, slot):
-            for t, block in enumerate(bring(raw[now], matrix[...])):
+            for t, block in enumerate(bring(forcing[now], matrix[...])):
                 for j in range(8):
                     force[slot, j, :, t * 32 : (t + 1) * 32] = block[:, j * 32 : (j + 1) * 32]
 
         fetch(31, 1)
     else:
-        (co, sum_in, final_in, square_in, got_low, got_high, got_row_low, got_row_high) = refs[:8]
+        (co, sum_in, final_in, square_in, got_near, got_far, got_row_low, got_row_high) = refs[:8]
         refs = refs[8:]
     if last:
         (start_o, mean_o, square_o, fields, f_ref, sums, squares, held) = refs
     else:
-        (sum_o, final_o, square_o, low_o, high_o, row_low_o, row_high_o) = refs[:7]
+        (sum_o, final_o, square_o, near_o, far_o, row_low_o, row_high_o) = refs[:7]
         (fields, f_ref, sums, squares, rows_ref) = refs[7:]
     steps = 32
     fields[...] = jnp.zeros_like(fields)
@@ -346,7 +347,26 @@
         rows_ref[...] = jnp.zeros_like(rows_ref)
     lane = lanes()
 
+    even = lax.axis_index("cols") % 2 == 0
+
+    def record(at):
+        for a in range(2):
+            low = y[pl.ds(a * 128, 8, stride=8), :]
+            high = y[pl.ds(a * 128 + 64 + 7, 8, stride=8), :]
+            near_o[at, a] = jnp.where(even, high, low)
+            far_o[at, a] = jnp.where(even, low, high)
+        lows, highs = rows_ref[0], rows_ref[1]
+        for q in range(4):
+            a, h = q // 2, q % 2
+            spot = q * 32 + at
+            lows = jnp.where(lane == spot, pltpu.roll(y[rows_of((a, h, 0)), :], spot, 1), lows)
+            highs = jnp.where(lane == spot, pltpu.roll(y[rows_of((a, h, 7)), :], (spot + 1) % 128, 1), highs)
+        rows_ref[0] = lows
+        rows_ref[1] = highs
+
     def one(now, slot):
+        if not last:
+            record(jnp.minimum(now + 1, steps - 1))
         extra = None
         if first:
             memo = {}
@@ -365,9 +385,11 @@
 
         else:
             extra = {}
-            for side, got in enumerate((got_low, got_high)):
+            for side in range(2):
                 for a in range(2):
-                    value = got[now, a] * co[COEF[("oc", side, a)]]
+                    near, far = got_near[now, a], got_far[now, a]
+                    got = jnp.where(even, near, far) if side else jnp.where(even, far, near)
+                    value = got * co[COEF[("oc", side, a)]]
                     base = (a * 2 + side) * 64
                     s = 7 * side
                     f_ref[pl.ds(base + s, 8, stride=8), :] = value
@@ -391,25 +413,14 @@
             y[rows_of(p), :] = x
             sums[i_p] += x
             squares[i_p] += x * x
-        if not last:
-            for a in range(2):
-                low_o[now, a] = y[pl.ds(a * 128, 8, stride=8), :]
-                high_o[now, a] = y[pl.ds(a * 128 + 64 + 7, 8, stride=8), :]
-            lows, highs = rows_ref[0], rows_ref[1]
-            for q in range(4):
-                a, h = q // 2, q % 2
-                spot = q * 32 + now
-                lows = jnp.where(lane == spot, pltpu.roll(done[(a, h, 0)], spot, 1), lows)
-                highs = jnp.where(lane == spot, pltpu.roll(done[(a, h, 7)], (spot + 1) % 128, 1), highs)
-            rows_ref[0] = lows
-            rows_ref[1] = highs
-
     def body(i, carry):
         one(steps - 1 - 2 * i, 1)
         one(steps - 2 - 2 * i, 0)
         return carry
 
     lax.fori_loop(0, steps // 2, body, 0)
+    if not last:
+        record(0)
 
     def alpha(p):
         return co[COEF[("alpha", 0, p)]]
@@ -422,22 +433,31 @@
     if first:
         square_o[...] = jnp.where(lane == 0, spread, 0.0)
     else:
-        square_o[...] = jnp.where(lane == (2 if last else 1), spread, square_in[...])
+        spread = jnp.where(lane == (2 if last else 1), spread, square_in[...])
+        if last:
+            for n in range(square_o.shape[0]):
+                square_o[n] = spread[0:1]
+        else:
+            square_o[...] = spread
     if not last:
         sub = sublanes()
         sum_o[...] = sums[...]
         final = y[...].reshape(32, 8, 128)
         final_o[...] = final if first else final + final_in[...]
-        scale = {}
-        for side in range(2):
-            for a in range(2):
+        for a in range(2):
+            scale = []
+            for side in range(2):
                 compact = jnp.zeros((8, 128), F32)
                 for j in range(8):
                     row = alpha((a, side, j))[7 * side : 7 * side + 1]
                     compact = jnp.where(sub == j, jnp.broadcast_to(row, (8, 128)), compact)
-                out = high_o if side else low_o
-                for n in range(steps):
-                    out[n, a] = out[n, a] * compact
+                scale.append(compact)
+            near_scale = jnp.where(even, scale[1], scale[0])
+            far_scale = jnp.where(even, scale[0], scale[1])
+            for n in range(steps):
+                near_o[n, a] = near_o[n, a] * near_scale
+                far_o[n, a] = far_o[n, a] * far_scale
+        for side in range(2):
             spread_row = jnp.zeros((8, 128), F32)
             for q in range(4):
                 a, h = q // 2, q % 2
@@ -467,7 +487,7 @@
 
 
 VM = pl.BlockSpec(memory_space=pltpu.VMEM)
-SM = pl.BlockSpec(memory_space=pltpu.SMEM)
+HBM = pl.BlockSpec(memory_space=pltpu.HBM)
 PARAMS = pltpu.CompilerParams(vmem_limit_bytes=VMEM_LIMIT)
 
 
@@ -497,30 +517,39 @@
 
 FORCING = [
     pltpu.VMEM((256, 256), BF16),
-    pltpu.VMEM((32, 2, 16, 1024), F32),
     pltpu.VMEM((2, 8, 32, 128), F32),
-    pltpu.SemaphoreType.DMA,
 ]
 BORDERS = [struct(32, 2, 8, 128), struct(32, 2, 8, 128), struct(8, 128), struct(8, 128)]
 
 
-def exchange(low, high, row_low, row_high):
-    n_cols, n_rows = lax.axis_size("cols"), lax.axis_size("rows")
-    cols_up = [(i, (i + 1) % n_cols) for i in range(n_cols)]
-    cols_down = [(j, i) for i, j in cols_up]
-    rows_up = [(i, (i + 1) % n_rows) for i in range(n_rows)]
-    rows_down = [(j, i) for i, j in rows_up]
-    from_low = lax.ppermute(high, "cols", cols_up)
-    from_high = lax.ppermute(low, "cols", cols_down)
-    from_row_low = lax.ppermute(row_high, "rows", rows_up)
-    from_row_high = lax.ppermute(row_low, "rows", rows_down)
-    return from_low, from_high, from_row_low, from_row_high
-
-
-def everywhere(x, axis):
+def shifts(axis):
     count = lax.axis_size(axis)
-    spread = jnp.broadcast_to(x[None], (count,) + x.shape)
-    return jnp.sum(lax.all_to_all(spread, axis, 0, 0), axis=0)
+    up = [(i, (i + 1) % count) for i in range(count)]
+    return up, [(j, i) for i, j in up]
+
+
+def swap_rows(row_low, row_high):
+    up, down = shifts("rows")
+    return lax.ppermute(row_high, "rows", up), lax.ppermute(row_low, "rows", down)
+
+
+def swap_all(low, high, row_low, row_high):
+    up, down = shifts("cols")
+    return lax.ppermute(high, "cols", up), lax.ppermute(low, "cols", down), *swap_rows(row_low, row_high)
+
+
+def swap_waves(near, far, row_low, row_high):
+    count = lax.axis_size("cols")
+    near_pairs = [(i, i ^ 1) for i in range(count)]
+    far_pairs = [(i, (i - 1 if i % 2 == 0 else i + 1) % count) for i in range(count)]
+    got = lax.ppermute(near, "cols", near_pairs), lax.ppermute(far, "cols", far_pairs)
+    return *got, *swap_rows(row_low, row_high)
+
+
+def everywhere(x):
+    x = jnp.sum(lax.all_to_all(x, "rows", 0, 0), axis=0)
+    x = jnp.broadcast_to(x[None], (lax.axis_size("cols"),) + x.shape)
+    return jnp.sum(lax.all_to_all(x, "cols", 0, 0), axis=0)
 
 
 def local(forcing, material, capacity_table, conductance_table, sink_table):
@@ -529,30 +558,35 @@
     sizes = (16 * n_cols, 1024 * n_rows)
     cap, con, sink, *facing = call(
         materials_kernel,
-        [SM, SM, SM, VM],
+        [HBM] * 2,
         [CELL, struct(256, 128), CELL] + [struct(2, 8, 128)] * 2 + [struct(4, 8, 128)] * 2,
-        [pltpu.VMEM((8, 32, 128), F32)],
-    )(capacity_table, conductance_table, sink_table, material)
-    con_low, con_high, row_low, row_high = exchange(*facing)
+        [pltpu.VMEM((8, 32, 128), F32)]
+        + [pltpu.SMEM((3, 8), F32), pltpu.VMEM(material.shape, jnp.int32), pltpu.SemaphoreType.DMA((2,))],
+    )(jnp.stack([capacity_table, conductance_table, sink_table]), material)
+    con_low, con_high, row_low, row_high = swap_all(*facing)
+    column = lax.axis_index("cols") * 16 + jnp.arange(16, dtype=jnp.int32)
+    row = lax.axis_index("rows") * 1024 + jnp.arange(1024, dtype=jnp.int32)
+    power = column.astype(F32)[:, None] / float(sizes[0]) + row.astype(F32)[None, :] / float(sizes[1])
+    source = forcing * jnp.power(jnp.float32(3.0), power)
     co, sums, final, squares, *borders = call(
         functools.partial(sweep_kernel, True, False, sizes),
-        [VM] * 7 + [pl.BlockSpec(memory_space=pl.ANY)],
+        [VM] * 8,
         [struct(len(KEYS), 8, 128), CELL, CELL, struct(8, 128)] + BORDERS,
         scratch_for(False) + FORCING,
-    )(cap, con, sink, con_low, con_high, row_low, row_high, forcing)
+    )(cap, con, sink, con_low, con_high, row_low, row_high, source)
     sums, final, squares, *borders = call(
         functools.partial(sweep_kernel, False, False, sizes),
         [VM] * 8,
         [CELL, CELL, struct(8, 128)] + BORDERS,
         scratch_for(False),
-    )(co, sums, final, squares, *exchange(*borders))
+    )(co, sums, final, squares, *swap_waves(*borders))
     start, mean, squares = call(
         functools.partial(sweep_kernel, False, True, sizes),
         [VM] * 8,
-        [struct(2, 16, 1024), struct(2, 16, 1024), struct(8, 128)],
+        [struct(2, 16, 1024), struct(2, 16, 1024), struct(n_rows, 1, 128)],
         scratch_for(True),
-    )(co, sums, final, squares, *exchange(*borders))
-    summed = everywhere(everywhere(squares[0], "rows"), "cols")[:SWEEPS]
+    )(co, sums, final, squares, *swap_waves(*borders))
+    summed = everywhere(squares)[0, :SWEEPS]
     count = float(steps * 2 * sizes[0] * sizes[1])
     return start, mean, jnp.sqrt(summed / count + 1e-06)
 

time: 120 us -> 106 us (0.88)
  Pallas kernels: 56.1 us -> 44.6 us
  other arithmetic: 0.56 us -> 4.38 us
  starting transfers between devices: 26 us -> 22.6 us
  local copies, waits for them, and re-layouts: 2.84 us -> 0.92 us
    pallas_call x2, Pallas kernels: 23.1 us -> 16.4 us  [the longest x1 15.3 us: local(): call(functools.partial(sweep_kernel, True, False, sizes), [VM] * 8, [stru...]
    ppermute x12, starting transfers between devices: 26 us -> 22.6 us  [the longest x3 8.79 us: swap_rows(): lax.ppermute(row_high, 'rows', up)]
    pallas_call x1, Pallas kernels: 17 us -> 13.7 us  [local(): call(functools.partial(sweep_kernel, False, False, sizes), [VM] * 8, [CEL...]
    mul x0 -> x1, other arithmetic: none -> 3.02 us  [local(): source = forcing * jnp.power(jnp.float32(3.0), power)]
    pallas_call x1, Pallas kernels: 16 us -> 14.5 us  [local(): call(functools.partial(sweep_kernel, False, True, sizes), [VM] * 8, [stru...]
    unnamed x24 -> x2, local copies, waits for them, and re-layouts: 2.13 us -> 0.9 us
  transfers between devices with their start and end apart: 12 -> 12, of which waited for: 5 -> 5; matrix products, arithmetic and copies ran while one was open for 0% -> 3% of each run, Pallas kernels for 0% -> 0%
where the time goes in v3:
time: 106 us; the launch traced here: 105 us
  Pallas kernels  44.6 us (42%)
  blocking collectives  24.4 us (23%)
  starting transfers between devices  22.6 us (21%)
  waiting for transfers between devices  7.9 us (7%)
  other arithmetic  4.38 us (4%)
    pallas_call x1, Pallas kernels, local(): call(functools.partial(sweep_kernel, True, False, sizes), [VM] * 8, [stru...  15.3 us
    pallas_call x1, Pallas kernels, local(): call(functools.partial(sweep_kernel, False, True, sizes), [VM] * 8, [stru...  14.5 us
    pallas_call x1, Pallas kernels, local(): call(functools.partial(sweep_kernel, False, False, sizes), [VM] * 8, [CEL...  13.7 us
    all_to_all x1, blocking collectives, everywhere(): x = jnp.sum(lax.all_to_all(x, 'rows', 0, 0), axis=0)  12.3 us
    all_to_all x1, blocking collectives, everywhere(): return jnp.sum(lax.all_to_all(x, 'cols', 0, 0), axis=0)  12.1 us
    ppermute x3, starting transfers between devices, swap_rows(): lax.ppermute(row_high, 'rows', up)  8.79 us
    ppermute x1, starting transfers between devices, swap_all(): lax.ppermute(low, 'cols', down)  6.48 us
    ppermute x3, waiting for transfers between devices, swap_rows(): lax.ppermute(row_low, 'rows', down)  5.13 us
  transfers between devices with their start and end apart: 12, of which 5 were waited for; matrix products, arithmetic and copies ran while one was open for 3% of the time, Pallas kernels for 0%

profile of v3, /device:TPU:1, one launch (start us, length us, event | category | flops | bytes accessed | tf_op | source)
XLA Modules:
  0.0 105.4 jit_solution(13495049855779676004)
XLA Ops:
  0.6 0.7 pad_maximum_fusion.refs_0_
  1.3 0.9 copy-done
  2.2 1.0 shard_map.76
  3.3 2.5 %collective-permute-start = (f32[2,8,128]{2,1,0:T(8,128)S(1)}, f32[2,8,128]{2,1,0:T(8,128)S(1)}, u32[]{:S(2)}, u32[]{:S(2)}) collective-permute-start(f32[2,8,128]{2,1,0:T(8,128)S(1)} %get-tuple-element.31), channel_id=1, source_target_pairs={{0,1},{1,2},{2,3},{3,4},{4,5},{5,6},{6,7},{7,8},{8,9},{9,10},{10,1... | collective-permute-start | bytes 24584 | tf_op jit(solution)/shard_map/ppermute | solution.py:538
  5.8 6.5 %collective-permute-start.1 = (f32[2,8,128]{2,1,0:T(8,128)S(1)}, f32[2,8,128]{2,1,0:T(8,128)S(1)}, u32[]{:S(2)}, u32[]{:S(2)}) collective-permute-start(f32[2,8,128]{2,1,0:T(8,128)S(1)} %get-tuple-element.32), channel_id=1, source_target_pairs={{1,0},{2,1},{3,2},{4,3},{5,4},{6,5},{7,6},{8,7},{9,8},{10,9},{11,1... | collective-permute-start | bytes 24584 | tf_op jit(solution)/shard_map/ppermute | solution.py:538
  12.3 2.1 %collective-permute-start.2 = (f32[4,8,128]{2,1,0:T(8,128)S(1)}, f32[4,8,128]{2,1,0:T(8,128)S(1)}, u32[]{:S(2)}, u32[]{:S(2)}) collective-permute-start(f32[4,8,128]{2,1,0:T(8,128)S(1)} %get-tuple-element.33), channel_id=1, source_target_pairs={{0,32},{32,64},{64,96},{96,128},{128,160},{160,192},{192,224},{224... | collective-permute-start | bytes 49160 | tf_op jit(solution)/shard_map/ppermute | solution.py:533
  14.4 3.0 %broadcast_multiply_fusion.refs_7_ = f32[32,2,16,1024]{3,2,1,0:T(8,128)S(1)} fusion(f32[32,2,16,1024]{3,2,1,0:T(8,128)} %param.5, f32[16,1024]{1,0:T(8,128)S(1)} %add_power_fusion), kind=kLoop, calls=%fused_computation | loop fusion | flops 1048576 | bytes 8454144 | tf_op jit(solution)/shard_map/mul | solution.py:570
  17.5 15.3 %shard_map.77 = (f32[309,8,128]{2,1,0:T(8,128)S(1)}, f32[32,8,128]{2,1,0:T(8,128)S(1)}, f32[32,8,128]{2,1,0:T(8,128)S(1)}, f32[8,128]{1,0:T(8,128)S(1)}, f32[32,...) custom-call(f32[32,8,128]{2,1,0:T(8,128)S(1)} %get-tuple-element.28.refs_0_, ...), custom_call_target="tpu_custom_call" | custom-call | tf_op jit(solution)/shard_map/pallas_call | solution.py:571
  32.9 2.4 %collective-permute-start.5 = (f32[32,2,8,128]{3,2,1,0:T(8,128)S(1)}, f32[32,2,8,128]{3,2,1,0:T(8,128)S(1)}, u32[]{:S(2)}, u32[]{:S(2)}) collective-permute-start(f32[32,2,8,128]{3,2,1,0:T(8,128)S(1)} %get-tuple-element.40), channel_id=1, source_target_pairs={{0,31},{1,2},{2,1},{3,4},{4,3},{5,6},{6,5},{7,8},{8,7},{9,10},{10,... | collective-permute-start | bytes 786440 | tf_op jit(solution)/shard_map/ppermute | solution.py:545
  35.3 2.3 %collective-permute-start.6 = (f32[8,128]{1,0:T(8,128)S(1)}, f32[8,128]{1,0:T(8,128)S(1)}, u32[]{:S(2)}, u32[]{:S(2)}) collective-permute-start(f32[8,128]{1,0:T(8,128)S(1)} %get-tuple-element.41), channel_id=1, source_target_pairs={{0,32},{32,64},{64,96},{96,128},{128,160},{160,192},{192,224},{224... | collective-permute-start | bytes 12296 | tf_op jit(solution)/shard_map/ppermute | solution.py:533
  37.6 0.1 collective-permute-start.7
  37.7 0.7 collective-permute-done.6.refs_6_
  38.4 2.6 %collective-permute-done.7.refs_7_ = f32[8,128]{1,0:T(8,128)S(1)} collective-permute-done((f32[8,128]{1,0:T(8,128)S(1)}, f32[8,128]{1,0:T(8,128)S(1)}, u32[]{:S(2)}, u32[]{:S(2)}) %collective-permute-start.7) | collective-permute-done | bytes 4128 | tf_op jit(solution)/shard_map/ppermute | solution.py:533
  40.9 1.3 %collective-permute-done.5.refs_5_ = f32[32,2,8,128]{3,2,1,0:T(8,128)S(1)} collective-permute-done((f32[32,2,8,128]{3,2,1,0:T(8,128)S(1)}, f32[32,2,8,128]{3,2,1,0:T(8,128)S(1)}, u32[]{:S(2)}, u32[]{:S(2)}) %collective-permute-start.5) | collective-permute-done | bytes 262176 | tf_op jit(solution)/shard_map/ppermute | solution.py:545
  42.3 13.7 %shard_map.78 = (f32[32,8,128]{2,1,0:T(8,128)S(1)}, f32[32,8,128]{2,1,0:T(8,128)S(1)}, f32[8,128]{1,0:T(8,128)S(1)}, f32[32,2,8,128]{3,2,1,0:T(8,128)S(1)}, f32[...) custom-call(f32[309,8,128]{2,1,0:T(8,128)S(1)} %get-tuple-element.35.refs_0_, ...), custom_call_target="tpu_custom_call" | custom-call | tf_op jit(solution)/shard_map/pallas_call | solution.py:577
  56.0 0.1 collective-permute-start.8
  56.1 2.1 %collective-permute-start.9 = (f32[32,2,8,128]{3,2,1,0:T(8,128)S(1)}, f32[32,2,8,128]{3,2,1,0:T(8,128)S(1)}, u32[]{:S(2)}, u32[]{:S(2)}) collective-permute-start(f32[32,2,8,128]{3,2,1,0:T(8,128)S(1)} %get-tuple-element.47), channel_id=1, source_target_pairs={{0,31},{1,2},{2,1},{3,4},{4,3},{5,6},{6,5},{7,8},{8,7},{9,10},{10,... | collective-permute-start | bytes 786440 | tf_op jit(solution)/shard_map/ppermute | solution.py:545
  58.2 4.4 %collective-permute-start.10 = (f32[8,128]{1,0:T(8,128)S(1)}, f32[8,128]{1,0:T(8,128)S(1)}, u32[]{:S(2)}, u32[]{:S(2)}) collective-permute-start(f32[8,128]{1,0:T(8,128)S(1)} %get-tuple-element.48), channel_id=1, source_target_pairs={{0,32},{32,64},{64,96},{96,128},{128,160},{160,192},{192,224},{224... | collective-permute-start | bytes 12296 | tf_op jit(solution)/shard_map/ppermute | solution.py:533
  62.6 0.8 collective-permute-done.10.refs_6_
  63.4 2.6 %collective-permute-done.11.refs_7_ = f32[8,128]{1,0:T(8,128)S(1)} collective-permute-done((f32[8,128]{1,0:T(8,128)S(1)}, f32[8,128]{1,0:T(8,128)S(1)}, u32[]{:S(2)}, u32[]{:S(2)}) %collective-permute-start.11) | collective-permute-done | bytes 4128 | tf_op jit(solution)/shard_map/ppermute | solution.py:533
  65.9 14.5 %shard_map.79 = (f32[2,16,1024]{2,1,0:T(8,128)}, f32[2,16,1024]{2,1,0:T(8,128)}, f32[8,1,128]{2,1,0:T(1,128)S(1)}) custom-call(f32[309,8,128]{2,1,0:T(8,128)S(1)} %get-tuple-element.35.refs_0_, f32[32,8,128]{2,1,0:T(8,128)S(1)} %get-tuple-element.43.refs_1_, f32[32,8,128]{2,1,0:T(8,128)S(1)} %get-tuple-element.44.refs_2_, ...), custom_call_target="tpu_custom_call" | custom-call | tf_op jit(solution)/shard_map/pallas_call | solution.py:583
  80.5 12.3 %all_to_all.10 = f32[8,1,128]{2,1,0:T(1,128)S(1)} all-to-all(f32[8,1,128]{2,1,0:T(1,128)S(1)} %get-tuple-element.52), channel_id=1, replica_groups=mesh['rows'=8,'cols'=32] {'rows'}, dimensions={0} | all-to-all | bytes 8192 | tf_op jit(solution)/shard_map/all_to_all | solution.py:550
  92.8 12.1 %all_to_all.11 = f32[32,1,128]{2,1,0:T(1,128)S(1)} all-to-all(f32[32,1,128]{2,1,0:T(1,128)S(1)} %broadcast_in_dim.2), channel_id=1, replica_groups=mesh['rows'=8,'cols'=32] {'cols'}, dimensions={0} | all-to-all | bytes 32768 | tf_op jit(solution)/shard_map/all_to_all | solution.py:552
  104.9 0.5 sqrt_bitcast_fusion
  (17 shorter events, 0.3 us)
Async XLA Ops:
  1.3 0.9 copy-start
  3.3 14.2 %collective-permute-start = (f32[2,8,128]{2,1,0:T(8,128)S(1)}, f32[2,8,128]{2,1,0:T(8,128)S(1)}, u32[]{:S(2)}, u32[]{:S(2)}) collective-permute-start(f32[2,8,128]{2,1,0:T(8,128)S(1)} %get-tuple-element.31), channel_id=1, source_target_pairs={{0,1},{1,2},{2,3},{3,4},{4,5},{5,6},{6,7},{7,8},{8,9},{9,10},{10,1... | collective-permute-start | bytes 24584 | tf_op jit(solution)/shard_map/ppermute | solution.py:538
  5.8 11.7 %collective-permute-start.1 = (f32[2,8,128]{2,1,0:T(8,128)S(1)}, f32[2,8,128]{2,1,0:T(8,128)S(1)}, u32[]{:S(2)}, u32[]{:S(2)}) collective-permute-start(f32[2,8,128]{2,1,0:T(8,128)S(1)} %get-tuple-element.32), channel_id=1, source_target_pairs={{1,0},{2,1},{3,2},{4,3},{5,4},{6,5},{7,6},{8,7},{9,8},{10,9},{11,1... | collective-permute-start | bytes 24584 | tf_op jit(solution)/shard_map/ppermute | solution.py:538
  12.3 5.2 %collective-permute-start.2 = (f32[4,8,128]{2,1,0:T(8,128)S(1)}, f32[4,8,128]{2,1,0:T(8,128)S(1)}, u32[]{:S(2)}, u32[]{:S(2)}) collective-permute-start(f32[4,8,128]{2,1,0:T(8,128)S(1)} %get-tuple-element.33), channel_id=1, source_target_pairs={{0,32},{32,64},{64,96},{96,128},{128,160},{160,192},{192,224},{224... | collective-permute-start | bytes 49160 | tf_op jit(solution)/shard_map/ppermute | solution.py:533
  14.3 3.2 %collective-permute-start.3 = (f32[4,8,128]{2,1,0:T(8,128)S(1)}, f32[4,8,128]{2,1,0:T(8,128)S(1)}, u32[]{:S(2)}, u32[]{:S(2)}) collective-permute-start(f32[4,8,128]{2,1,0:T(8,128)S(1)} %get-tuple-element.34), channel_id=1, source_target_pairs={{32,0},{64,32},{96,64},{128,96},{160,128},{192,160},{224,192},{0,2... | collective-permute-start | bytes 49160 | tf_op jit(solution)/shard_map/ppermute | solution.py:533
  32.8 8.1 %collective-permute-start.4 = (f32[32,2,8,128]{3,2,1,0:T(8,128)S(1)}, f32[32,2,8,128]{3,2,1,0:T(8,128)S(1)}, u32[]{:S(2)}, u32[]{:S(2)}) collective-permute-start(f32[32,2,8,128]{3,2,1,0:T(8,128)S(1)} %get-tuple-element.39), channel_id=1, source_target_pairs={{0,1},{1,0},{2,3},{3,2},{4,5},{5,4},{6,7},{7,6},{8,9},{9,8},{10,11... | collective-permute-start | bytes 786440 | tf_op jit(solution)/shard_map/ppermute | solution.py:545
  32.9 9.3 %collective-permute-start.5 = (f32[32,2,8,128]{3,2,1,0:T(8,128)S(1)}, f32[32,2,8,128]{3,2,1,0:T(8,128)S(1)}, u32[]{:S(2)}, u32[]{:S(2)}) collective-permute-start(f32[32,2,8,128]{3,2,1,0:T(8,128)S(1)} %get-tuple-element.40), channel_id=1, source_target_pairs={{0,31},{1,2},{2,1},{3,4},{4,3},{5,6},{6,5},{7,8},{8,7},{9,10},{10,... | collective-permute-start | bytes 786440 | tf_op jit(solution)/shard_map/ppermute | solution.py:545
  35.3 3.1 %collective-permute-start.6 = (f32[8,128]{1,0:T(8,128)S(1)}, f32[8,128]{1,0:T(8,128)S(1)}, u32[]{:S(2)}, u32[]{:S(2)}) collective-permute-start(f32[8,128]{1,0:T(8,128)S(1)} %get-tuple-element.41), channel_id=1, source_target_pairs={{0,32},{32,64},{64,96},{96,128},{128,160},{160,192},{192,224},{224... | collective-permute-start | bytes 12296 | tf_op jit(solution)/shard_map/ppermute | solution.py:533
  37.6 3.3 %collective-permute-start.7 = (f32[8,128]{1,0:T(8,128)S(1)}, f32[8,128]{1,0:T(8,128)S(1)}, u32[]{:S(2)}, u32[]{:S(2)}) collective-permute-start(f32[8,128]{1,0:T(8,128)S(1)} %get-tuple-element.42), channel_id=1, source_target_pairs={{32,0},{64,32},{96,64},{128,96},{160,128},{192,160},{224,192},{0,2... | collective-permute-start | bytes 12296 | tf_op jit(solution)/shard_map/ppermute | solution.py:533
  56.0 10.0 %collective-permute-start.8 = (f32[32,2,8,128]{3,2,1,0:T(8,128)S(1)}, f32[32,2,8,128]{3,2,1,0:T(8,128)S(1)}, u32[]{:S(2)}, u32[]{:S(2)}) collective-permute-start(f32[32,2,8,128]{3,2,1,0:T(8,128)S(1)} %get-tuple-element.46), channel_id=1, source_target_pairs={{0,1},{1,0},{2,3},{3,2},{4,5},{5,4},{6,7},{7,6},{8,9},{9,8},{10,11... | collective-permute-start | bytes 786440 | tf_op jit(solution)/shard_map/ppermute | solution.py:545
  56.1 9.9 %collective-permute-start.9 = (f32[32,2,8,128]{3,2,1,0:T(8,128)S(1)}, f32[32,2,8,128]{3,2,1,0:T(8,128)S(1)}, u32[]{:S(2)}, u32[]{:S(2)}) collective-permute-start(f32[32,2,8,128]{3,2,1,0:T(8,128)S(1)} %get-tuple-element.47), channel_id=1, source_target_pairs={{0,31},{1,2},{2,1},{3,4},{4,3},{5,6},{6,5},{7,8},{8,7},{9,10},{10,... | collective-permute-start | bytes 786440 | tf_op jit(solution)/shard_map/ppermute | solution.py:545
  58.2 5.2 %collective-permute-start.10 = (f32[8,128]{1,0:T(8,128)S(1)}, f32[8,128]{1,0:T(8,128)S(1)}, u32[]{:S(2)}, u32[]{:S(2)}) collective-permute-start(f32[8,128]{1,0:T(8,128)S(1)} %get-tuple-element.48), channel_id=1, source_target_pairs={{0,32},{32,64},{64,96},{96,128},{128,160},{160,192},{192,224},{224... | collective-permute-start | bytes 12296 | tf_op jit(solution)/shard_map/ppermute | solution.py:533
  62.6 3.3 %collective-permute-start.11 = (f32[8,128]{1,0:T(8,128)S(1)}, f32[8,128]{1,0:T(8,128)S(1)}, u32[]{:S(2)}, u32[]{:S(2)}) collective-permute-start(f32[8,128]{1,0:T(8,128)S(1)} %get-tuple-element.49), channel_id=1, source_target_pairs={{32,0},{64,32},{96,64},{128,96},{160,128},{192,160},{224,192},{0,2... | collective-permute-start | bytes 12296 | tf_op jit(solution)/shard_map/ppermute | solution.py:533

commit v4 on v3

--- a/solution.py
+++ b/solution.py
@@ -9,6 +9,8 @@
 
 PASSES = 8
 SWEEPS = 3
+STEPS = 32
+HALF = 16
 F32 = jnp.float32
 BF16 = jnp.bfloat16
 VMEM_LIMIT = 24 * 2**20
@@ -307,54 +309,49 @@
     return {**fields[0], **fields[1]}
 
 
-def sweep_kernel(first, last, sizes, *refs):
-    refs = list(refs)
+def sweep_kernel(first, last, top, bottom, sizes, names, *refs):
+    r = dict(zip(names, refs))
+    whole, ends = top - bottom == STEPS - 1, bottom == 0
+    co, sums, squares, f_ref, lane = r["co"], r["sums"], r["squares"], r["f"], lanes()
     if first:
-        (cap, con, sink, con_low, con_high, row_low, row_high, forcing) = refs[:8]
-        co = refs[8]
-        refs = refs[9:]
+        facing = [r[k] for k in ("cap", "con", "sink", "con_low", "con_high", "row_low", "row_high")]
+        matrix, force, forcing = r["matrix"], r["force"], r["forcing"]
         place = (lax.axis_index("rows"), lax.axis_index("cols"))
-        (matrix, force) = refs[-2:]
-        refs = refs[:-2]
         matrix[...] = permutation(True)
-        coefficients(place, sizes, cap, con, sink, con_low, con_high, row_low, row_high, co)
+        coefficients(place, sizes, *facing, co)
 
         def fetch(now, slot):
             for t, block in enumerate(bring(forcing[now], matrix[...])):
                 for j in range(8):
                     force[slot, j, :, t * 32 : (t + 1) * 32] = block[:, j * 32 : (j + 1) * 32]
 
-        fetch(31, 1)
+        fetch(top, 1)
+    stages = [r["fields"].at[k] for k in range(4)]
+    y = stages[0]
+    if top == STEPS - 1:
+        y[...] = jnp.zeros_like(y)
+        squares[...] = jnp.zeros_like(squares)
     else:
-        (co, sum_in, final_in, square_in, got_near, got_far, got_row_low, got_row_high) = refs[:8]
-        refs = refs[8:]
-    if last:
-        (start_o, mean_o, square_o, fields, f_ref, sums, squares, held) = refs
-    else:
-        (sum_o, final_o, square_o, near_o, far_o, row_low_o, row_high_o) = refs[:7]
-        (fields, f_ref, sums, squares, rows_ref) = refs[7:]
-    steps = 32
-    fields[...] = jnp.zeros_like(fields)
-    stages = [fields.at[k] for k in range(4)]
-    y = stages[0]
-    squares[...] = jnp.zeros_like(squares)
+        y[...] = r["y_in"][...]
+        squares[...] = r["squares_in"][...]
     if first:
         sums[...] = jnp.zeros_like(sums)
     else:
-        sums[...] = sum_in[...]
+        sums[...] = r["sums_in"][...]
         f_ref[...] = jnp.zeros_like(f_ref)
     if not last:
-        rows_ref[...] = jnp.zeros_like(rows_ref)
-    lane = lanes()
-
+        rows_ref = r["rows"]
+        rows_ref[...] = jnp.zeros_like(rows_ref) if top == STEPS - 1 else r["rows_in"][...]
     even = lax.axis_index("cols") % 2 == 0
+    even_row = lax.axis_index("rows") % 2 == 0
 
     def record(at):
+        edges = r["edges"]
         for a in range(2):
             low = y[pl.ds(a * 128, 8, stride=8), :]
             high = y[pl.ds(a * 128 + 64 + 7, 8, stride=8), :]
-            near_o[at, a] = jnp.where(even, high, low)
-            far_o[at, a] = jnp.where(even, low, high)
+            edges[0, at - bottom, a] = jnp.where(even, high, low)
+            edges[1, at - bottom, a] = jnp.where(even, low, high)
         lows, highs = rows_ref[0], rows_ref[1]
         for q in range(4):
             a, h = q // 2, q % 2
@@ -366,7 +363,7 @@
 
     def one(now, slot):
         if not last:
-            record(jnp.minimum(now + 1, steps - 1))
+            record(jnp.minimum(now + 1, top))
         extra = None
         if first:
             memo = {}
@@ -387,7 +384,7 @@
             extra = {}
             for side in range(2):
                 for a in range(2):
-                    near, far = got_near[now, a], got_far[now, a]
+                    near, far = r["got_near"][now - bottom, a], r["got_far"][now - bottom, a]
                     got = jnp.where(even, near, far) if side else jnp.where(even, far, near)
                     value = got * co[COEF[("oc", side, a)]]
                     base = (a * 2 + side) * 64
@@ -395,11 +392,14 @@
                     f_ref[pl.ds(base + s, 8, stride=8), :] = value
                     f_ref[pl.ds(AT[(a, side, -1)] * 8 + s, 1), :] = pltpu.roll(value, 1, 1)[7:8]
                     f_ref[pl.ds(AT[(a, side, 8)] * 8 + s, 1), :] = pltpu.roll(value, 127, 1)[0:1]
+            row_near, row_far = r["got_row_near"][0], r["got_row_far"][0]
+            row_low = jnp.where(even_row, row_far, row_near)
+            row_high = jnp.where(even_row, row_near, row_far)
             for q in range(4):
                 a, h = q // 2, q % 2
                 spot = q * 32 + now
-                extra[(a, h, 0)] = co[COEF[("or", 0, q)]] * pltpu.roll(got_row_low[...], (128 - spot) % 128, 1)
-                extra[(a, h, 7)] = co[COEF[("or", 1, q)]] * pltpu.roll(got_row_high[...], 127 - spot, 1)
+                extra[(a, h, 0)] = co[COEF[("or", 0, q)]] * pltpu.roll(row_low, (128 - spot) % 128, 1)
+                extra[(a, h, 7)] = co[COEF[("or", 1, q)]] * pltpu.roll(row_high, 127 - spot, 1)
 
             def source(p):
                 return f_ref[pl.ds(AT[p] * 8, 8), :]
@@ -413,37 +413,20 @@
             y[rows_of(p), :] = x
             sums[i_p] += x
             squares[i_p] += x * x
+
     def body(i, carry):
-        one(steps - 1 - 2 * i, 1)
-        one(steps - 2 - 2 * i, 0)
+        one(top - 2 * i, 1)
+        one(top - 1 - 2 * i, 0)
         return carry
 
-    lax.fori_loop(0, steps // 2, body, 0)
-    if not last:
-        record(0)
+    lax.fori_loop(0, (top - bottom + 1) // 2, body, 0)
 
     def alpha(p):
         return co[COEF[("alpha", 0, p)]]
 
-    total = jnp.zeros((8, 128), F32)
-    for p in CELLS:
-        total = total + squares[AT[p]] * (alpha(p) * alpha(p))
-    total = jnp.sum(jnp.sum(total, axis=1, keepdims=True), axis=0, keepdims=True)
-    spread = jnp.broadcast_to(total, (8, 128))
-    if first:
-        square_o[...] = jnp.where(lane == 0, spread, 0.0)
-    else:
-        spread = jnp.where(lane == (2 if last else 1), spread, square_in[...])
-        if last:
-            for n in range(square_o.shape[0]):
-                square_o[n] = spread[0:1]
-        else:
-            square_o[...] = spread
+    sub = sublanes()
     if not last:
-        sub = sublanes()
-        sum_o[...] = sums[...]
-        final = y[...].reshape(32, 8, 128)
-        final_o[...] = final if first else final + final_in[...]
+        record(bottom)
         for a in range(2):
             scale = []
             for side in range(2):
@@ -454,32 +437,55 @@
                 scale.append(compact)
             near_scale = jnp.where(even, scale[1], scale[0])
             far_scale = jnp.where(even, scale[0], scale[1])
-            for n in range(steps):
-                near_o[n, a] = near_o[n, a] * near_scale
-                far_o[n, a] = far_o[n, a] * far_scale
+            for n in range(bottom, top + 1):
+                half, k = ("upper", n - HALF) if n >= HALF else ("lower", n)
+                r["near_" + half][k, a] = r["edges"][0, n - bottom, a] * near_scale
+                r["far_" + half][k, a] = r["edges"][1, n - bottom, a] * far_scale
+    if not ends:
+        r["y_out"][...] = y[...]
+        return
+    total = jnp.zeros((8, 128), F32)
+    for p in CELLS:
+        total = total + squares[AT[p]] * (alpha(p) * alpha(p))
+    total = jnp.sum(jnp.sum(total, axis=1, keepdims=True), axis=0, keepdims=True)
+    spread = jnp.broadcast_to(total, (8, 128))
+    if first:
+        r["norms"][...] = jnp.where(lane == 0, spread, 0.0)
+    else:
+        spread = jnp.where(lane == (2 if last else 1), spread, r["norms_in"][...])
+        if last:
+            for n in range(r["norms"].shape[0]):
+                r["norms"][n] = spread[0:1]
+        else:
+            r["norms"][...] = spread
+    if not last:
+        final = y[...].reshape(32, 8, 128)
+        r["final"][...] = final if first else final + r["final_in"][...]
+        turned = []
         for side in range(2):
             spread_row = jnp.zeros((8, 128), F32)
             for q in range(4):
                 a, h = q // 2, q % 2
-                one = alpha((a, h, 7 * side))
-                one = one[:, 127:128] if side else one[:, 0:1]
-                spread_row = jnp.where(lane // 32 == q, jnp.broadcast_to(one, (8, 128)), spread_row)
-            out = row_high_o if side else row_low_o
-            out[...] = rows_ref[side] * spread_row
+                one_lane = alpha((a, h, 7 * side))
+                one_lane = one_lane[:, 127:128] if side else one_lane[:, 0:1]
+                spread_row = jnp.where(lane // 32 == q, jnp.broadcast_to(one_lane, (8, 128)), spread_row)
+            turned.append(rows_ref[side] * spread_row)
+        for name, value in (("row_near", (turned[1], turned[0])), ("row_far", turned)):
+            r[name][...] = jnp.zeros_like(r[name])
+            r[name][0] = jnp.where(even_row, *value)
     else:
-        matrix = permutation(False)
-        for which, out in ((0, start_o), (1, mean_o)):
-            for p in CELLS:
-                a, h, j = p
-                i_p = AT[p]
-                if which == 0:
-                    value = (final_in[i_p] + y[rows_of(p), :]) * co[COEF[("cap", 0, p)]]
-                else:
-                    value = sums[i_p] * alpha(p) * (1.0 / steps)
-                held[j, pl.ds(a * 16 + h, 8, stride=2), :] = value
-            for t in range(4):
-                piece = jnp.concatenate([held[j, :, t * 32 : (t + 1) * 32] for j in range(8)], axis=1)
-                out[:, :, t * 256 : (t + 1) * 256] = permute(piece, matrix).reshape(2, 16, 256)
+        matrix, held = permutation(False), r["held"]
+        for p in CELLS:
+            a, h, j = p
+            i_p = AT[p]
+            start = (r["final_in"][i_p] + y[rows_of(p), :]) * co[COEF[("cap", 0, p)]]
+            held[j, pl.ds(a * 16 + h, 8, stride=2), :] = start
+            held[j, pl.ds(32 + a * 16 + h, 8, stride=2), :] = sums[i_p] * alpha(p) * (1.0 / STEPS)
+        for t in range(4):
+            piece = jnp.concatenate([held[j, :, t * 32 : (t + 1) * 32] for j in range(8)], axis=1)
+            moved = permute(piece, matrix).reshape(4, 16, 256)
+            r["start"][:, :, t * 256 : (t + 1) * 256] = moved[:2]
+            r["mean"][:, :, t * 256 : (t + 1) * 256] = moved[2:]
 
 
 def struct(*shape):
@@ -503,23 +509,28 @@
 
 
 CELL = struct(32, 8, 128)
-
-
-def scratch_for(last):
-    shared = [
-        pltpu.VMEM((4, 256, 128), F32),
-        pltpu.VMEM((320, 128), F32),
-        pltpu.VMEM((32, 8, 128), F32),
-        pltpu.VMEM((32, 8, 128), F32),
-    ]
-    return shared + [pltpu.VMEM((8, 32, 128), F32) if last else pltpu.VMEM((2, 8, 128), F32)]
-
-
-FORCING = [
-    pltpu.VMEM((256, 256), BF16),
-    pltpu.VMEM((2, 8, 32, 128), F32),
-]
-BORDERS = [struct(32, 2, 8, 128), struct(32, 2, 8, 128), struct(8, 128), struct(8, 128)]
+WAVE = struct(HALF, 2, 8, 128)
+LANES = struct(8, 128)
+ROWS = struct(64, 8, 128)
+
+
+def run_sweep(first, last, top, bottom, sizes, inputs, outs):
+    scratch = {"fields": pltpu.VMEM((4, 256, 128), F32), "f": pltpu.VMEM((320, 128), F32)}
+    kept = {name: pltpu.VMEM((32, 8, 128), F32) for name in ("sums", "squares") if name not in outs}
+    if not last:
+        scratch["edges"] = pltpu.VMEM((2, top - bottom + 1, 2, 8, 128), F32)
+        if "rows" not in outs:
+            scratch["rows"] = pltpu.VMEM((2, 8, 128), F32)
+    elif bottom == 0:
+        scratch["held"] = pltpu.VMEM((8, 64, 128), F32)
+    if first:
+        scratch["matrix"] = pltpu.VMEM((256, 256), BF16)
+        scratch["force"] = pltpu.VMEM((2, 8, 32, 128), F32)
+    scratch = scratch | kept
+    names = [*inputs, *outs, *scratch]
+    kernel = functools.partial(sweep_kernel, first, last, top, bottom, sizes, names)
+    got = call(kernel, [VM] * len(inputs), list(outs.values()), list(scratch.values()))(*inputs.values())
+    return dict(zip(outs, got))
 
 
 def shifts(axis):
@@ -528,22 +539,51 @@
     return up, [(j, i) for i, j in up]
 
 
-def swap_rows(row_low, row_high):
-    up, down = shifts("rows")
-    return lax.ppermute(row_high, "rows", up), lax.ppermute(row_low, "rows", down)
-
-
 def swap_all(low, high, row_low, row_high):
     up, down = shifts("cols")
-    return lax.ppermute(high, "cols", up), lax.ppermute(low, "cols", down), *swap_rows(row_low, row_high)
-
-
-def swap_waves(near, far, row_low, row_high):
-    count = lax.axis_size("cols")
+    rows_up, rows_down = shifts("rows")
+    return (
+        lax.ppermute(high, "cols", up),
+        lax.ppermute(low, "cols", down),
+        lax.ppermute(row_high, "rows", rows_up),
+        lax.ppermute(row_low, "rows", rows_down),
+    )
+
+
+def swap_pairs(near, far, axis):
+    count = lax.axis_size(axis)
     near_pairs = [(i, i ^ 1) for i in range(count)]
     far_pairs = [(i, (i - 1 if i % 2 == 0 else i + 1) % count) for i in range(count)]
-    got = lax.ppermute(near, "cols", near_pairs), lax.ppermute(far, "cols", far_pairs)
-    return *got, *swap_rows(row_low, row_high)
+    got_far = lax.ppermute(far, axis, far_pairs)
+    return lax.ppermute(near, axis, near_pairs), got_far
+
+
+def swap_waves(waves):
+    upper = swap_pairs(waves["near_upper"], waves["far_upper"], "cols")
+    rows = swap_pairs(waves["row_near"], waves["row_far"], "rows")
+    lower = swap_pairs(waves["near_lower"], waves["far_lower"], "cols")
+    return upper, rows, lower
+
+
+def later_sweep(last, sizes, n_rows, before, co, sums, waves):
+    upper, rows, lower = swap_waves(waves)
+    row_in = {"got_row_near": rows[0], "got_row_far": rows[1]}
+    inputs = {"co": co, "sums_in": sums, "got_near": upper[0], "got_far": upper[1]} | row_in
+    outs = {"y_out": struct(256, 128), "sums": CELL, "squares": CELL}
+    if not last:
+        outs |= {"rows": struct(2, 8, 128), "near_upper": WAVE, "far_upper": WAVE}
+    mid = run_sweep(False, last, STEPS - 1, HALF, sizes, inputs, outs)
+    inputs = {"co": co, "sums_in": mid["sums"], "squares_in": mid["squares"], "y_in": mid["y_out"]}
+    inputs |= {"got_near": lower[0], "got_far": lower[1], "final_in": before["final"], "norms_in": before["norms"]}
+    inputs |= row_in
+    if last:
+        whole = struct(2, 16, 1024)
+        outs = {"start": whole, "mean": whole, "norms": struct(n_rows, 1, 128)}
+    else:
+        inputs["rows_in"] = mid["rows"]
+        outs = {"sums": CELL, "final": CELL, "norms": LANES, "near_lower": WAVE, "far_lower": WAVE}
+        outs |= {"row_near": ROWS, "row_far": ROWS}
+    return mid | run_sweep(False, last, HALF - 1, 0, sizes, inputs, outs)
 
 
 def everywhere(x):
@@ -568,25 +608,16 @@
     row = lax.axis_index("rows") * 1024 + jnp.arange(1024, dtype=jnp.int32)
     power = column.astype(F32)[:, None] / float(sizes[0]) + row.astype(F32)[None, :] / float(sizes[1])
     source = forcing * jnp.power(jnp.float32(3.0), power)
-    co, sums, final, squares, *borders = call(
-        functools.partial(sweep_kernel, True, False, sizes),
-        [VM] * 8,
-        [struct(len(KEYS), 8, 128), CELL, CELL, struct(8, 128)] + BORDERS,
-        scratch_for(False) + FORCING,
-    )(cap, con, sink, con_low, con_high, row_low, row_high, source)
-    sums, final, squares, *borders = call(
-        functools.partial(sweep_kernel, False, False, sizes),
-        [VM] * 8,
-        [CELL, CELL, struct(8, 128)] + BORDERS,
-        scratch_for(False),
-    )(co, sums, final, squares, *swap_waves(*borders))
-    start, mean, squares = call(
-        functools.partial(sweep_kernel, False, True, sizes),
-        [VM] * 8,
-        [struct(2, 16, 1024), struct(2, 16, 1024), struct(n_rows, 1, 128)],
-        scratch_for(True),
-    )(co, sums, final, squares, *swap_waves(*borders))
-    summed = everywhere(squares)[0, :SWEEPS]
+    inputs = {"cap": cap, "con": con, "sink": sink, "con_low": con_low, "con_high": con_high}
+    inputs |= {"row_low": row_low, "row_high": row_high, "forcing": source}
+    outs = {"co": struct(len(KEYS), 8, 128), "sums": CELL, "final": CELL, "norms": LANES}
+    outs |= {name: WAVE for name in ("near_upper", "far_upper", "near_lower", "far_lower")}
+    outs |= {"row_near": ROWS, "row_far": ROWS}
+    one = run_sweep(True, False, STEPS - 1, 0, sizes, inputs, outs)
+    two = later_sweep(False, sizes, n_rows, one, one["co"], one["sums"], one)
+    three = later_sweep(True, sizes, n_rows, two, one["co"], two["sums"], two)
+    start, mean = three["start"], three["mean"]
+    summed = everywhere(three["norms"])[0, :SWEEPS]
     count = float(steps * 2 * sizes[0] * sizes[1])
     return start, mean, jnp.sqrt(summed / count + 1e-06)
 

time: 106 us -> 105 us (level)
  starting transfers between devices: 22.6 us -> 25.2 us
  waiting for transfers between devices: 7.9 us -> 5.45 us
  blocking collectives: 24.4 us -> 23.1 us
  Pallas kernels: 44.6 us -> 45.7 us
    ppermute x10 -> x14, starting transfers between devices: 13.5 us -> 16.2 us  [the longest x6 9.69 us: swap_pairs(): got_far = lax.ppermute(far, axis, far_pairs)]
    ppermute x10 -> x14, waiting for transfers between devices: 7.89 us -> 5.45 us  [the longest x6 3.46 us: swap_pairs(): return (lax.ppermute(near, axis, near_pairs), got_far)]
    all_to_all x1, blocking collectives: 12.3 us -> 10.7 us  [everywhere(): x = jnp.sum(lax.all_to_all(x, 'rows', 0, 0), axis=0)]
    pallas_call x3 -> x5, Pallas kernels: 43.6 us -> 44.7 us  [run_sweep(): call(kernel, [VM] * len(inputs), list(outs.values()), list(scratch.values...]
  transfers between devices with their start and end apart: 12 -> 16, of which waited for: 5 -> 5; matrix products, arithmetic and copies ran while one was open for 3% -> 3% of each run, Pallas kernels for 0% -> 13%
where the time goes in v4:
time: 105 us
  Pallas kernels  45.7 us (44%)
  starting transfers between devices  25.2 us (24%)
  blocking collectives  23.1 us (22%)
  waiting for transfers between devices  5.45 us (5%)
  other arithmetic  4.06 us (4%)
    pallas_call x5, Pallas kernels, run_sweep(): call(kernel, [VM] * len(inputs), list(outs.values()), list(scratch.values...  44.7 us
    all_to_all x1, blocking collectives, everywhere(): return jnp.sum(lax.all_to_all(x, 'cols', 0, 0), axis=0)  12.5 us
    all_to_all x1, blocking collectives, everywhere(): x = jnp.sum(lax.all_to_all(x, 'rows', 0, 0), axis=0)  10.7 us
    ppermute x6, starting transfers between devices, swap_pairs(): got_far = lax.ppermute(far, axis, far_pairs)  9.69 us
    ppermute x1, starting transfers between devices, swap_all(): lax.ppermute(low, 'cols', down)  6.48 us
    ppermute x6, starting transfers between devices, swap_pairs(): return (lax.ppermute(near, axis, near_pairs), got_far)  4.44 us
    ppermute x6, waiting for transfers between devices, swap_pairs(): return (lax.ppermute(near, axis, near_pairs), got_far)  3.46 us
    mul x1, other arithmetic, local(): source = forcing * jnp.power(jnp.float32(3.0), power)  2.69 us
  transfers between devices with their start and end apart: 16, of which 5 were waited for; matrix products, arithmetic and copies ran while one was open for 3% of the time, Pallas kernels for 13%

profile of v4, /device:TPU:1, one launch (start us, length us, event | category | flops | bytes accessed | tf_op | source)
XLA Modules:
  0.0 105.2 jit_solution(4533665383460425767)
XLA Ops:
  0.6 0.7 pad_maximum_fusion.refs_0_
  1.3 0.9 copy-done
  2.2 1.0 shard_map.76
  3.3 2.5 %collective-permute-start = (f32[2,8,128]{2,1,0:T(8,128)S(1)}, f32[2,8,128]{2,1,0:T(8,128)S(1)}, u32[]{:S(2)}, u32[]{:S(2)}) collective-permute-start(f32[2,8,128]{2,1,0:T(8,128)S(1)} %get-tuple-element.42), channel_id=1, source_target_pairs={{0,1},{1,2},{2,3},{3,4},{4,5},{5,6},{6,7},{7,8},{8,9},{9,10},{10,1... | collective-permute-start | bytes 24584 | tf_op jit(solution)/shard_map/ppermute | solution.py:546
  5.8 6.5 %collective-permute-start.1 = (f32[2,8,128]{2,1,0:T(8,128)S(1)}, f32[2,8,128]{2,1,0:T(8,128)S(1)}, u32[]{:S(2)}, u32[]{:S(2)}) collective-permute-start(f32[2,8,128]{2,1,0:T(8,128)S(1)} %get-tuple-element.43), channel_id=1, source_target_pairs={{1,0},{2,1},{3,2},{4,3},{5,4},{6,5},{7,6},{8,7},{9,8},{10,9},{11,1... | collective-permute-start | bytes 24584 | tf_op jit(solution)/shard_map/ppermute | solution.py:547
  12.3 2.1 %collective-permute-start.2 = (f32[4,8,128]{2,1,0:T(8,128)S(1)}, f32[4,8,128]{2,1,0:T(8,128)S(1)}, u32[]{:S(2)}, u32[]{:S(2)}) collective-permute-start(f32[4,8,128]{2,1,0:T(8,128)S(1)} %get-tuple-element.44), channel_id=1, source_target_pairs={{0,32},{32,64},{64,96},{96,128},{128,160},{160,192},{192,224},{224... | collective-permute-start | bytes 49160 | tf_op jit(solution)/shard_map/ppermute | solution.py:548
  14.4 2.7 %broadcast_multiply_fusion.refs_7_ = f32[32,2,16,1024]{3,2,1,0:T(8,128)S(1)} fusion(f32[32,2,16,1024]{3,2,1,0:T(8,128)} %param.5, f32[16,1024]{1,0:T(8,128)S(1)} %add_power_fusion), kind=kLoop, calls=%fused_computation | loop fusion | flops 1048576 | bytes 8454144 | tf_op jit(solution)/shard_map/mul | solution.py:610
  17.5 15.7 %shard_map.77 = (f32[309,8,128]{2,1,0:T(8,128)S(1)}, f32[32,8,128]{2,1,0:T(8,128)S(1)}, f32[32,8,128]{2,1,0:T(8,128)S(1)}, f32[8,128]{1,0:T(8,128)S(1)}, f32[16,...) custom-call(f32[32,8,128]{2,1,0:T(8,128)S(1)} %get-tuple-element.39., ...), custom_call_target="tpu_custom_call" | custom-call | tf_op jit(solution)/shard_map/pallas_call | solution.py:532
  33.2 1.6 %collective-permute-start.6 = (f32[64,8,128]{2,1,0:T(8,128)S(1)}, f32[64,8,128]{2,1,0:T(8,128)S(1)}, u32[]{:S(2)}, u32[]{:S(2)}) collective-permute-start(f32[64,8,128]{2,1,0:T(8,128)S(1)} %get-tuple-element.50), channel_id=1, source_target_pairs={{0,32},{32,0},{64,96},{96,64},{128,160},{160,128},{192,224},{224,1... | collective-permute-start | bytes 786440 | tf_op jit(solution)/shard_map/ppermute | solution.py:558
  34.9 2.4 %collective-permute-start.5 = (f32[16,2,8,128]{3,2,1,0:T(8,128)S(1)}, f32[16,2,8,128]{3,2,1,0:T(8,128)S(1)}, u32[]{:S(2)}, u32[]{:S(2)}) collective-permute-start(f32[16,2,8,128]{3,2,1,0:T(8,128)S(1)} %get-tuple-element.49), channel_id=1, source_target_pairs={{0,31},{1,2},{2,1},{3,4},{4,3},{5,6},{6,5},{7,8},{8,7},{9,10},{10,... | collective-permute-start | bytes 393224 | tf_op jit(solution)/shard_map/ppermute | solution.py:557
  37.3 1.7 %collective-permute-done.4.refs_2_ = f32[16,2,8,128]{3,2,1,0:T(8,128)S(1)} collective-permute-done((f32[16,2,8,128]{3,2,1,0:T(8,128)S(1)}, f32[16,2,8,128]{3,2,1,0:T(8,128)S(1)}, u32[]{:S(2)}, u32[]{:S(2)}) %collective-permute-start.4) | collective-permute-done | bytes 131104 | tf_op jit(solution)/shard_map/ppermute | solution.py:558
  39.0 2.0 %collective-permute-start.9 = (f32[16,2,8,128]{3,2,1,0:T(8,128)S(1)}, f32[16,2,8,128]{3,2,1,0:T(8,128)S(1)}, u32[]{:S(2)}, u32[]{:S(2)}) collective-permute-start(f32[16,2,8,128]{3,2,1,0:T(8,128)S(1)} %get-tuple-element.56), channel_id=1, source_target_pairs={{0,31},{1,2},{2,1},{3,4},{4,3},{5,6},{6,5},{7,8},{8,7},{9,10},{10,... | collective-permute-start | bytes 393224 | tf_op jit(solution)/shard_map/ppermute | solution.py:557
  41.0 1.0 collective-permute-done.5.refs_3_
  42.0 7.1 %shard_map.78 = (f32[256,128]{1,0:T(8,128)S(1)}, f32[32,8,128]{2,1,0:T(8,128)S(1)}, f32[32,8,128]{2,1,0:T(8,128)S(1)}, f32[2,8,128]{2,1,0:T(8,128)S(1)}, f32[16,...) custom-call(f32[309,8,128]{2,1,0:T(8,128)S(1)} %get-tuple-element.46.refs_0_, ...), custom_call_target="tpu_custom_call" | custom-call | tf_op jit(solution)/shard_map/pallas_call | solution.py:532
  49.2 7.0 %shard_map.79 = (f32[32,8,128]{2,1,0:T(8,128)S(1)}, f32[32,8,128]{2,1,0:T(8,128)S(1)}, f32[8,128]{1,0:T(8,128)S(1)}, f32[16,2,8,128]{3,2,1,0:T(8,128)S(1)}, f32[...) custom-call(f32[309,8,128]{2,1,0:T(8,128)S(1)} %get-tuple-element.46.refs_0_, ...), custom_call_target="tpu_custom_call" | custom-call | tf_op jit(solution)/shard_map/pallas_call | solution.py:532
  56.2 2.8 %collective-permute-start.12 = (f32[64,8,128]{2,1,0:T(8,128)S(1)}, f32[64,8,128]{2,1,0:T(8,128)S(1)}, u32[]{:S(2)}, u32[]{:S(2)}) collective-permute-start(f32[64,8,128]{2,1,0:T(8,128)S(1)} %get-tuple-element.63), channel_id=1, source_target_pairs={{0,32},{32,0},{64,96},{96,64},{128,160},{160,128},{192,224},{224,1... | collective-permute-start | bytes 786440 | tf_op jit(solution)/shard_map/ppermute | solution.py:558
  59.5 2.4 %collective-permute-start.11 = (f32[16,2,8,128]{3,2,1,0:T(8,128)S(1)}, f32[16,2,8,128]{3,2,1,0:T(8,128)S(1)}, u32[]{:S(2)}, u32[]{:S(2)}) collective-permute-start(f32[16,2,8,128]{3,2,1,0:T(8,128)S(1)} %get-tuple-element.62), channel_id=1, source_target_pairs={{0,31},{1,2},{2,1},{3,4},{4,3},{5,6},{6,5},{7,8},{8,7},{9,10},{10,... | collective-permute-start | bytes 393224 | tf_op jit(solution)/shard_map/ppermute | solution.py:557
  61.9 1.7 %collective-permute-done.10.refs_2_ = f32[16,2,8,128]{3,2,1,0:T(8,128)S(1)} collective-permute-done((f32[16,2,8,128]{3,2,1,0:T(8,128)S(1)}, f32[16,2,8,128]{3,2,1,0:T(8,128)S(1)}, u32[]{:S(2)}, u32[]{:S(2)}) %collective-permute-start.10) | collective-permute-done | bytes 131104 | tf_op jit(solution)/shard_map/ppermute | solution.py:558
  63.6 2.4 %collective-permute-start.15 = (f32[16,2,8,128]{3,2,1,0:T(8,128)S(1)}, f32[16,2,8,128]{3,2,1,0:T(8,128)S(1)}, u32[]{:S(2)}, u32[]{:S(2)}) collective-permute-start(f32[16,2,8,128]{3,2,1,0:T(8,128)S(1)} %get-tuple-element.69), channel_id=1, source_target_pairs={{0,31},{1,2},{2,1},{3,4},{4,3},{5,6},{6,5},{7,8},{8,7},{9,10},{10,... | collective-permute-start | bytes 393224 | tf_op jit(solution)/shard_map/ppermute | solution.py:557
  66.0 0.6 collective-permute-done.11.refs_3_
  66.7 7.0 %shard_map.80 = (f32[256,128]{1,0:T(8,128)S(1)}, f32[32,8,128]{2,1,0:T(8,128)S(1)}, f32[32,8,128]{2,1,0:T(8,128)S(1)}) custom-call(f32[309,8,128]{2,1,0:T(8,128)S(1)} %get-tuple-element.46.refs_0_, f32[32,8,128]{2,1,0:T(8,128)S(1)} %get-tuple-element.60.refs_1_, f32[16,2,8,128]{3,2,1,0:T(8,128)S(1)} %collective-permute-done.10.refs_2_, ...), custom_call_target="tpu_custom_call" | custom-call | tf_op jit(solution)/shard_map/pallas_call | solution.py:532
  73.7 7.9 %shard_map.81 = (f32[2,16,1024]{2,1,0:T(8,128)}, f32[2,16,1024]{2,1,0:T(8,128)}, f32[8,1,128]{2,1,0:T(1,128)S(1)}) custom-call(f32[309,8,128]{2,1,0:T(8,128)S(1)} %get-tuple-element.46.refs_0_, f32[32,8,128]{2,1,0:T(8,128)S(1)} %get-tuple-element.65.refs_1_, f32[32,8,128]{2,1,0:T(8,128)S(1)} %get-tuple-element.66.refs_2_, ...), custom_call_target="tpu_custom_call" | custom-call | tf_op jit(solution)/shard_map/pallas_call | solution.py:532
  81.5 10.7 %all_to_all.10 = f32[8,1,128]{2,1,0:T(1,128)S(1)} all-to-all(f32[8,1,128]{2,1,0:T(1,128)S(1)} %get-tuple-element.74), channel_id=1, replica_groups=mesh['rows'=8,'cols'=32] {'rows'}, dimensions={0} | all-to-all | bytes 8192 | tf_op jit(solution)/shard_map/all_to_all | solution.py:590
  92.2 12.5 %all_to_all.11 = f32[32,1,128]{2,1,0:T(1,128)S(1)} all-to-all(f32[32,1,128]{2,1,0:T(1,128)S(1)} %broadcast_in_dim.2), channel_id=1, replica_groups=mesh['rows'=8,'cols'=32] {'cols'}, dimensions={0} | all-to-all | bytes 32768 | tf_op jit(solution)/shard_map/all_to_all | solution.py:592
  (27 shorter events, 1.6 us)
Async XLA Ops:
  1.3 0.9 copy-start
  3.3 13.9 %collective-permute-start = (f32[2,8,128]{2,1,0:T(8,128)S(1)}, f32[2,8,128]{2,1,0:T(8,128)S(1)}, u32[]{:S(2)}, u32[]{:S(2)}) collective-permute-start(f32[2,8,128]{2,1,0:T(8,128)S(1)} %get-tuple-element.42), channel_id=1, source_target_pairs={{0,1},{1,2},{2,3},{3,4},{4,5},{5,6},{6,7},{7,8},{8,9},{9,10},{10,1... | collective-permute-start | bytes 24584 | tf_op jit(solution)/shard_map/ppermute | solution.py:546
  5.8 11.4 %collective-permute-start.1 = (f32[2,8,128]{2,1,0:T(8,128)S(1)}, f32[2,8,128]{2,1,0:T(8,128)S(1)}, u32[]{:S(2)}, u32[]{:S(2)}) collective-permute-start(f32[2,8,128]{2,1,0:T(8,128)S(1)} %get-tuple-element.43), channel_id=1, source_target_pairs={{1,0},{2,1},{3,2},{4,3},{5,4},{6,5},{7,6},{8,7},{9,8},{10,9},{11,1... | collective-permute-start | bytes 24584 | tf_op jit(solution)/shard_map/ppermute | solution.py:547
  12.3 4.9 %collective-permute-start.2 = (f32[4,8,128]{2,1,0:T(8,128)S(1)}, f32[4,8,128]{2,1,0:T(8,128)S(1)}, u32[]{:S(2)}, u32[]{:S(2)}) collective-permute-start(f32[4,8,128]{2,1,0:T(8,128)S(1)} %get-tuple-element.44), channel_id=1, source_target_pairs={{0,32},{32,64},{64,96},{96,128},{128,160},{160,192},{192,224},{224... | collective-permute-start | bytes 49160 | tf_op jit(solution)/shard_map/ppermute | solution.py:548
  14.3 3.2 %collective-permute-start.3 = (f32[4,8,128]{2,1,0:T(8,128)S(1)}, f32[4,8,128]{2,1,0:T(8,128)S(1)}, u32[]{:S(2)}, u32[]{:S(2)}) collective-permute-start(f32[4,8,128]{2,1,0:T(8,128)S(1)} %get-tuple-element.45), channel_id=1, source_target_pairs={{32,0},{64,32},{96,64},{128,96},{160,128},{192,160},{224,192},{0,2... | collective-permute-start | bytes 49160 | tf_op jit(solution)/shard_map/ppermute | solution.py:549
  33.2 8.8 %collective-permute-start.6 = (f32[64,8,128]{2,1,0:T(8,128)S(1)}, f32[64,8,128]{2,1,0:T(8,128)S(1)}, u32[]{:S(2)}, u32[]{:S(2)}) collective-permute-start(f32[64,8,128]{2,1,0:T(8,128)S(1)} %get-tuple-element.50), channel_id=1, source_target_pairs={{0,32},{32,0},{64,96},{96,64},{128,160},{160,128},{192,224},{224,1... | collective-permute-start | bytes 786440 | tf_op jit(solution)/shard_map/ppermute | solution.py:558
  34.8 7.2 %collective-permute-start.7 = (f32[64,8,128]{2,1,0:T(8,128)S(1)}, f32[64,8,128]{2,1,0:T(8,128)S(1)}, u32[]{:S(2)}, u32[]{:S(2)}) collective-permute-start(f32[64,8,128]{2,1,0:T(8,128)S(1)} %get-tuple-element.51), channel_id=1, source_target_pairs={{0,224},{32,64},{64,32},{96,128},{128,96},{160,192},{192,160},{224... | collective-permute-start | bytes 786440 | tf_op jit(solution)/shard_map/ppermute | solution.py:557
  34.9 4.1 %collective-permute-start.4 = (f32[16,2,8,128]{3,2,1,0:T(8,128)S(1)}, f32[16,2,8,128]{3,2,1,0:T(8,128)S(1)}, u32[]{:S(2)}, u32[]{:S(2)}) collective-permute-start(f32[16,2,8,128]{3,2,1,0:T(8,128)S(1)} %get-tuple-element.48), channel_id=1, source_target_pairs={{0,1},{1,0},{2,3},{3,2},{4,5},{5,4},{6,7},{7,6},{8,9},{9,8},{10,11... | collective-permute-start | bytes 393224 | tf_op jit(solution)/shard_map/ppermute | solution.py:558
  34.9 7.1 %collective-permute-start.5 = (f32[16,2,8,128]{3,2,1,0:T(8,128)S(1)}, f32[16,2,8,128]{3,2,1,0:T(8,128)S(1)}, u32[]{:S(2)}, u32[]{:S(2)}) collective-permute-start(f32[16,2,8,128]{3,2,1,0:T(8,128)S(1)} %get-tuple-element.49), channel_id=1, source_target_pairs={{0,31},{1,2},{2,1},{3,4},{4,3},{5,6},{6,5},{7,8},{8,7},{9,10},{10,... | collective-permute-start | bytes 393224 | tf_op jit(solution)/shard_map/ppermute | solution.py:557
  37.3 11.9 %collective-permute-start.8 = (f32[16,2,8,128]{3,2,1,0:T(8,128)S(1)}, f32[16,2,8,128]{3,2,1,0:T(8,128)S(1)}, u32[]{:S(2)}, u32[]{:S(2)}) collective-permute-start(f32[16,2,8,128]{3,2,1,0:T(8,128)S(1)} %get-tuple-element.55), channel_id=1, source_target_pairs={{0,1},{1,0},{2,3},{3,2},{4,5},{5,4},{6,7},{7,6},{8,9},{9,8},{10,11... | collective-permute-start | bytes 393224 | tf_op jit(solution)/shard_map/ppermute | solution.py:558
  39.0 10.2 %collective-permute-start.9 = (f32[16,2,8,128]{3,2,1,0:T(8,128)S(1)}, f32[16,2,8,128]{3,2,1,0:T(8,128)S(1)}, u32[]{:S(2)}, u32[]{:S(2)}) collective-permute-start(f32[16,2,8,128]{3,2,1,0:T(8,128)S(1)} %get-tuple-element.56), channel_id=1, source_target_pairs={{0,31},{1,2},{2,1},{3,4},{4,3},{5,6},{6,5},{7,8},{8,7},{9,10},{10,... | collective-permute-start | bytes 393224 | tf_op jit(solution)/shard_map/ppermute | solution.py:557
  56.2 10.4 %collective-permute-start.12 = (f32[64,8,128]{2,1,0:T(8,128)S(1)}, f32[64,8,128]{2,1,0:T(8,128)S(1)}, u32[]{:S(2)}, u32[]{:S(2)}) collective-permute-start(f32[64,8,128]{2,1,0:T(8,128)S(1)} %get-tuple-element.63), channel_id=1, source_target_pairs={{0,32},{32,0},{64,96},{96,64},{128,160},{160,128},{192,224},{224,1... | collective-permute-start | bytes 786440 | tf_op jit(solution)/shard_map/ppermute | solution.py:558
  59.1 7.6 %collective-permute-start.13 = (f32[64,8,128]{2,1,0:T(8,128)S(1)}, f32[64,8,128]{2,1,0:T(8,128)S(1)}, u32[]{:S(2)}, u32[]{:S(2)}) collective-permute-start(f32[64,8,128]{2,1,0:T(8,128)S(1)} %get-tuple-element.64), channel_id=1, source_target_pairs={{0,224},{32,64},{64,32},{96,128},{128,96},{160,192},{192,160},{224... | collective-permute-start | bytes 786440 | tf_op jit(solution)/shard_map/ppermute | solution.py:557
  59.5 4.1 %collective-permute-start.10 = (f32[16,2,8,128]{3,2,1,0:T(8,128)S(1)}, f32[16,2,8,128]{3,2,1,0:T(8,128)S(1)}, u32[]{:S(2)}, u32[]{:S(2)}) collective-permute-start(f32[16,2,8,128]{3,2,1,0:T(8,128)S(1)} %get-tuple-element.61), channel_id=1, source_target_pairs={{0,1},{1,0},{2,3},{3,2},{4,5},{5,4},{6,7},{7,6},{8,9},{9,8},{10,11... | collective-permute-start | bytes 393224 | tf_op jit(solution)/shard_map/ppermute | solution.py:558
  59.5 7.1 %collective-permute-start.11 = (f32[16,2,8,128]{3,2,1,0:T(8,128)S(1)}, f32[16,2,8,128]{3,2,1,0:T(8,128)S(1)}, u32[]{:S(2)}, u32[]{:S(2)}) collective-permute-start(f32[16,2,8,128]{3,2,1,0:T(8,128)S(1)} %get-tuple-element.62), channel_id=1, source_target_pairs={{0,31},{1,2},{2,1},{3,4},{4,3},{5,6},{6,5},{7,8},{8,7},{9,10},{10,... | collective-permute-start | bytes 393224 | tf_op jit(solution)/shard_map/ppermute | solution.py:557
  61.9 11.7 %collective-permute-start.14 = (f32[16,2,8,128]{3,2,1,0:T(8,128)S(1)}, f32[16,2,8,128]{3,2,1,0:T(8,128)S(1)}, u32[]{:S(2)}, u32[]{:S(2)}) collective-permute-start(f32[16,2,8,128]{3,2,1,0:T(8,128)S(1)} %get-tuple-element.68), channel_id=1, source_target_pairs={{0,1},{1,0},{2,3},{3,2},{4,5},{5,4},{6,7},{7,6},{8,9},{9,8},{10,11... | collective-permute-start | bytes 393224 | tf_op jit(solution)/shard_map/ppermute | solution.py:558
  63.6 10.0 %collective-permute-start.15 = (f32[16,2,8,128]{3,2,1,0:T(8,128)S(1)}, f32[16,2,8,128]{3,2,1,0:T(8,128)S(1)}, u32[]{:S(2)}, u32[]{:S(2)}) collective-permute-start(f32[16,2,8,128]{3,2,1,0:T(8,128)S(1)} %get-tuple-element.69), channel_id=1, source_target_pairs={{0,31},{1,2},{2,1},{3,4},{4,3},{5,6},{6,5},{7,8},{8,7},{9,10},{10,... | collective-permute-start | bytes 393224 | tf_op jit(solution)/shard_map/ppermute | solution.py:557

commit v5 on v4

--- a/solution.py
+++ b/solution.py
@@ -474,18 +474,23 @@
             r[name][...] = jnp.zeros_like(r[name])
             r[name][0] = jnp.where(even_row, *value)
     else:
-        matrix, held = permutation(False), r["held"]
-        for p in CELLS:
-            a, h, j = p
-            i_p = AT[p]
-            start = (r["final_in"][i_p] + y[rows_of(p), :]) * co[COEF[("cap", 0, p)]]
-            held[j, pl.ds(a * 16 + h, 8, stride=2), :] = start
-            held[j, pl.ds(32 + a * 16 + h, 8, stride=2), :] = sums[i_p] * alpha(p) * (1.0 / STEPS)
-        for t in range(4):
-            piece = jnp.concatenate([held[j, :, t * 32 : (t + 1) * 32] for j in range(8)], axis=1)
-            moved = permute(piece, matrix).reshape(4, 16, 256)
-            r["start"][:, :, t * 256 : (t + 1) * 256] = moved[:2]
-            r["mean"][:, :, t * 256 : (t + 1) * 256] = moved[2:]
+        r["final"][...] = y[...].reshape(32, 8, 128) + r["final_in"][...]
+
+
+def outputs_kernel(co, sums, final, start_o, mean_o, held):
+    matrix = permutation(False)
+    for p in CELLS:
+        a, h, j = p
+        i_p = AT[p]
+        start = final[i_p] * co[COEF[("cap", 0, p)]]
+        mean = sums[i_p] * co[COEF[("alpha", 0, p)]] * (1.0 / STEPS)
+        held[j, pl.ds(a * 16 + h, 8, stride=2), :] = start
+        held[j, pl.ds(32 + a * 16 + h, 8, stride=2), :] = mean
+    for t in range(4):
+        piece = jnp.concatenate([held[j, :, t * 32 : (t + 1) * 32] for j in range(8)], axis=1)
+        moved = permute(piece, matrix).reshape(4, 16, 256)
+        start_o[:, :, t * 256 : (t + 1) * 256] = moved[:2]
+        mean_o[:, :, t * 256 : (t + 1) * 256] = moved[2:]
 
 
 def struct(*shape):
@@ -521,8 +526,6 @@
         scratch["edges"] = pltpu.VMEM((2, top - bottom + 1, 2, 8, 128), F32)
         if "rows" not in outs:
             scratch["rows"] = pltpu.VMEM((2, 8, 128), F32)
-    elif bottom == 0:
-        scratch["held"] = pltpu.VMEM((8, 64, 128), F32)
     if first:
         scratch["matrix"] = pltpu.VMEM((256, 256), BF16)
         scratch["force"] = pltpu.VMEM((2, 8, 32, 128), F32)
@@ -577,8 +580,7 @@
     inputs |= {"got_near": lower[0], "got_far": lower[1], "final_in": before["final"], "norms_in": before["norms"]}
     inputs |= row_in
     if last:
-        whole = struct(2, 16, 1024)
-        outs = {"start": whole, "mean": whole, "norms": struct(n_rows, 1, 128)}
+        outs = {"sums": CELL, "final": CELL, "norms": struct(n_rows, 1, 128)}
     else:
         inputs["rows_in"] = mid["rows"]
         outs = {"sums": CELL, "final": CELL, "norms": LANES, "near_lower": WAVE, "far_lower": WAVE}
@@ -616,7 +618,10 @@
     one = run_sweep(True, False, STEPS - 1, 0, sizes, inputs, outs)
     two = later_sweep(False, sizes, n_rows, one, one["co"], one["sums"], one)
     three = later_sweep(True, sizes, n_rows, two, one["co"], two["sums"], two)
-    start, mean = three["start"], three["mean"]
+    whole = struct(2, 16, 1024)
+    start, mean = call(outputs_kernel, [VM] * 3, [whole, whole], [pltpu.VMEM((8, 64, 128), F32)])(
+        one["co"], three["sums"], three["final"]
+    )
     summed = everywhere(three["norms"])[0, :SWEEPS]
     count = float(steps * 2 * sizes[0] * sizes[1])
     return start, mean, jnp.sqrt(summed / count + 1e-06)

time: 105 us -> 106 us (level)
  blocking collectives: 23.1 us -> 10.7 us
  waiting for transfers between devices: 5.45 us -> 12.9 us
  starting transfers between devices: 25.2 us -> 29.3 us
    all_to_all x1 -> x0, blocking collectives: 12.5 us -> none  [everywhere(): return jnp.sum(lax.all_to_all(x, 'cols', 0, 0), axis=0)]
    all_to_all x0 -> x1, waiting for transfers between devices: none -> 7.49 us  [everywhere(): return jnp.sum(lax.all_to_all(x, 'cols', 0, 0), axis=0)]
    all_to_all x0 -> x1, starting transfers between devices: none -> 4.05 us  [everywhere(): return jnp.sum(lax.all_to_all(x, 'cols', 0, 0), axis=0)]
    pallas_call x0 -> x1, Pallas kernels: none -> 1.14 us  [local(): call(outputs_kernel, [VM] * 3, [whole, whole], [pltpu.VMEM((8, 64, 128),...]
  transfers between devices with their start and end apart: 16 -> 17, of which waited for: 5 -> 6; matrix products, arithmetic and copies ran while one was open for 3% -> 3% of each run, Pallas kernels for 13% -> 14%
where the time goes in v5:
time: 106 us; the launch traced here: 105 us
  Pallas kernels  46.2 us (44%)
  starting transfers between devices  29.3 us (28%)
  waiting for transfers between devices  12.9 us (12%)
  blocking collectives  10.7 us (10%)
  other arithmetic  4.09 us (4%)
  local copies, waits for them, and re-layouts  1.51 us (1%)
    pallas_call x5, Pallas kernels, run_sweep(): call(kernel, [VM] * len(inputs), list(outs.values()), list(scratch.values...  44.1 us
    all_to_all x1, blocking collectives, everywhere(): x = jnp.sum(lax.all_to_all(x, 'rows', 0, 0), axis=0)  10.7 us
    ppermute x6, starting transfers between devices, swap_pairs(): got_far = lax.ppermute(far, axis, far_pairs)  9.7 us
    all_to_all x1, waiting for transfers between devices, everywhere(): return jnp.sum(lax.all_to_all(x, 'cols', 0, 0), axis=0)  7.49 us
    ppermute x1, starting transfers between devices, swap_all(): lax.ppermute(low, 'cols', down)  6.48 us
    ppermute x6, starting transfers between devices, swap_pairs(): return (lax.ppermute(near, axis, near_pairs), got_far)  4.5 us
    all_to_all x1, starting transfers between devices, everywhere(): return jnp.sum(lax.all_to_all(x, 'cols', 0, 0), axis=0)  4.05 us
    ppermute x6, waiting for transfers between devices, swap_pairs(): return (lax.ppermute(near, axis, near_pairs), got_far)  3.44 us
  transfers between devices with their start and end apart: 17, of which 6 were waited for; matrix products, arithmetic and copies ran while one was open for 3% of the time, Pallas kernels for 14%

profile of v5, /device:TPU:1, one launch (start us, length us, event | category | flops | bytes accessed | tf_op | source)
XLA Modules:
  0.0 105.4 jit_solution(4542811121401559809)
XLA Ops:
  1.3 0.9 copy-done
  2.2 1.0 shard_map.76
  3.3 2.5 %collective-permute-start = (f32[2,8,128]{2,1,0:T(8,128)S(1)}, f32[2,8,128]{2,1,0:T(8,128)S(1)}, u32[]{:S(2)}, u32[]{:S(2)}) collective-permute-start(f32[2,8,128]{2,1,0:T(8,128)S(1)} %get-tuple-element.44), channel_id=1, source_target_pairs={{0,1},{1,2},{2,3},{3,4},{4,5},{5,6},{6,7},{7,8},{8,9},{9,10},{10,1... | collective-permute-start | bytes 24584 | tf_op jit(solution)/shard_map/ppermute | solution.py:549
  5.8 6.5 %collective-permute-start.1 = (f32[2,8,128]{2,1,0:T(8,128)S(1)}, f32[2,8,128]{2,1,0:T(8,128)S(1)}, u32[]{:S(2)}, u32[]{:S(2)}) collective-permute-start(f32[2,8,128]{2,1,0:T(8,128)S(1)} %get-tuple-element.45), channel_id=1, source_target_pairs={{1,0},{2,1},{3,2},{4,3},{5,4},{6,5},{7,6},{8,7},{9,8},{10,9},{11,1... | collective-permute-start | bytes 24584 | tf_op jit(solution)/shard_map/ppermute | solution.py:550
  12.3 2.1 %collective-permute-start.2 = (f32[4,8,128]{2,1,0:T(8,128)S(1)}, f32[4,8,128]{2,1,0:T(8,128)S(1)}, u32[]{:S(2)}, u32[]{:S(2)}) collective-permute-start(f32[4,8,128]{2,1,0:T(8,128)S(1)} %get-tuple-element.46), channel_id=1, source_target_pairs={{0,32},{32,64},{64,96},{96,128},{128,160},{160,192},{192,224},{224... | collective-permute-start | bytes 49160 | tf_op jit(solution)/shard_map/ppermute | solution.py:551
  14.4 2.7 %broadcast_multiply_fusion.refs_7_ = f32[32,2,16,1024]{3,2,1,0:T(8,128)S(1)} fusion(f32[32,2,16,1024]{3,2,1,0:T(8,128)} %param.5, f32[16,1024]{1,0:T(8,128)S(1)} %add_power_fusion), kind=kLoop, calls=%fused_computation | loop fusion | flops 1048576 | bytes 8454144 | tf_op jit(solution)/shard_map/mul | solution.py:612
  17.5 15.9 %shard_map.77 = (f32[309,8,128]{2,1,0:T(8,128)S(1)}, f32[32,8,128]{2,1,0:T(8,128)S(1)}, f32[32,8,128]{2,1,0:T(8,128)S(1)}, f32[8,128]{1,0:T(8,128)S(1)}, f32[16,...) custom-call(f32[32,8,128]{2,1,0:T(8,128)S(1)} %get-tuple-element.41., ...), custom_call_target="tpu_custom_call" | custom-call | tf_op jit(solution)/shard_map/pallas_call | solution.py:535
  33.4 1.6 %collective-permute-start.6 = (f32[64,8,128]{2,1,0:T(8,128)S(1)}, f32[64,8,128]{2,1,0:T(8,128)S(1)}, u32[]{:S(2)}, u32[]{:S(2)}) collective-permute-start(f32[64,8,128]{2,1,0:T(8,128)S(1)} %get-tuple-element.52), channel_id=1, source_target_pairs={{0,32},{32,0},{64,96},{96,64},{128,160},{160,128},{192,224},{224,1... | collective-permute-start | bytes 786440 | tf_op jit(solution)/shard_map/ppermute | solution.py:561
  35.1 2.4 %collective-permute-start.5 = (f32[16,2,8,128]{3,2,1,0:T(8,128)S(1)}, f32[16,2,8,128]{3,2,1,0:T(8,128)S(1)}, u32[]{:S(2)}, u32[]{:S(2)}) collective-permute-start(f32[16,2,8,128]{3,2,1,0:T(8,128)S(1)} %get-tuple-element.51), channel_id=1, source_target_pairs={{0,31},{1,2},{2,1},{3,4},{4,3},{5,6},{6,5},{7,8},{8,7},{9,10},{10,... | collective-permute-start | bytes 393224 | tf_op jit(solution)/shard_map/ppermute | solution.py:560
  37.5 1.7 %collective-permute-done.4.refs_2_ = f32[16,2,8,128]{3,2,1,0:T(8,128)S(1)} collective-permute-done((f32[16,2,8,128]{3,2,1,0:T(8,128)S(1)}, f32[16,2,8,128]{3,2,1,0:T(8,128)S(1)}, u32[]{:S(2)}, u32[]{:S(2)}) %collective-permute-start.4) | collective-permute-done | bytes 131104 | tf_op jit(solution)/shard_map/ppermute | solution.py:561
  39.2 2.0 %collective-permute-start.9 = (f32[16,2,8,128]{3,2,1,0:T(8,128)S(1)}, f32[16,2,8,128]{3,2,1,0:T(8,128)S(1)}, u32[]{:S(2)}, u32[]{:S(2)}) collective-permute-start(f32[16,2,8,128]{3,2,1,0:T(8,128)S(1)} %get-tuple-element.58), channel_id=1, source_target_pairs={{0,31},{1,2},{2,1},{3,4},{4,3},{5,6},{6,5},{7,8},{8,7},{9,10},{10,... | collective-permute-start | bytes 393224 | tf_op jit(solution)/shard_map/ppermute | solution.py:560
  41.2 1.0 collective-permute-done.5.refs_3_
  42.2 7.1 %shard_map.78 = (f32[256,128]{1,0:T(8,128)S(1)}, f32[32,8,128]{2,1,0:T(8,128)S(1)}, f32[32,8,128]{2,1,0:T(8,128)S(1)}, f32[2,8,128]{2,1,0:T(8,128)S(1)}, f32[16,...) custom-call(f32[309,8,128]{2,1,0:T(8,128)S(1)} %get-tuple-element.48.refs_0_.co, ...), custom_call_target="tpu_custom_call" | custom-call | tf_op jit(solution)/shard_map/pallas_call | solution.py:535
  49.4 7.1 %shard_map.79 = (f32[32,8,128]{2,1,0:T(8,128)S(1)}, f32[32,8,128]{2,1,0:T(8,128)S(1)}, f32[8,128]{1,0:T(8,128)S(1)}, f32[16,2,8,128]{3,2,1,0:T(8,128)S(1)}, f32[...) custom-call(f32[309,8,128]{2,1,0:T(8,128)S(1)} %get-tuple-element.48.refs_0_.co, ...), custom_call_target="tpu_custom_call" | custom-call | tf_op jit(solution)/shard_map/pallas_call | solution.py:535
  56.5 2.9 %collective-permute-start.12 = (f32[64,8,128]{2,1,0:T(8,128)S(1)}, f32[64,8,128]{2,1,0:T(8,128)S(1)}, u32[]{:S(2)}, u32[]{:S(2)}) collective-permute-start(f32[64,8,128]{2,1,0:T(8,128)S(1)} %get-tuple-element.65), channel_id=1, source_target_pairs={{0,32},{32,0},{64,96},{96,64},{128,160},{160,128},{192,224},{224,1... | collective-permute-start | bytes 786440 | tf_op jit(solution)/shard_map/ppermute | solution.py:561
  59.8 2.4 %collective-permute-start.11 = (f32[16,2,8,128]{3,2,1,0:T(8,128)S(1)}, f32[16,2,8,128]{3,2,1,0:T(8,128)S(1)}, u32[]{:S(2)}, u32[]{:S(2)}) collective-permute-start(f32[16,2,8,128]{3,2,1,0:T(8,128)S(1)} %get-tuple-element.64), channel_id=1, source_target_pairs={{0,31},{1,2},{2,1},{3,4},{4,3},{5,6},{6,5},{7,8},{8,7},{9,10},{10,... | collective-permute-start | bytes 393224 | tf_op jit(solution)/shard_map/ppermute | solution.py:560
  62.2 1.7 %collective-permute-done.10.refs_2_ = f32[16,2,8,128]{3,2,1,0:T(8,128)S(1)} collective-permute-done((f32[16,2,8,128]{3,2,1,0:T(8,128)S(1)}, f32[16,2,8,128]{3,2,1,0:T(8,128)S(1)}, u32[]{:S(2)}, u32[]{:S(2)}) %collective-permute-start.10) | collective-permute-done | bytes 131104 | tf_op jit(solution)/shard_map/ppermute | solution.py:561
  63.9 2.4 %collective-permute-start.15 = (f32[16,2,8,128]{3,2,1,0:T(8,128)S(1)}, f32[16,2,8,128]{3,2,1,0:T(8,128)S(1)}, u32[]{:S(2)}, u32[]{:S(2)}) collective-permute-start(f32[16,2,8,128]{3,2,1,0:T(8,128)S(1)} %get-tuple-element.71), channel_id=1, source_target_pairs={{0,31},{1,2},{2,1},{3,4},{4,3},{5,6},{6,5},{7,8},{8,7},{9,10},{10,... | collective-permute-start | bytes 393224 | tf_op jit(solution)/shard_map/ppermute | solution.py:560
  66.9 7.0 %shard_map.80 = (f32[256,128]{1,0:T(8,128)S(1)}, f32[32,8,128]{2,1,0:T(8,128)S(1)}, f32[32,8,128]{2,1,0:T(8,128)S(1)}) custom-call(f32[309,8,128]{2,1,0:T(8,128)S(1)} %get-tuple-element.48.refs_0_.co, f32[32,8,128]{2,1,0:T(8,128)S(1)} %get-tuple-element.62.refs_1_, f32[16,2,8,128]{3,2,1,0:T(8,128)S(1)} %collective-permute-done.10.refs_2_, ...), custom_call_target="tpu_custom_call" | custom-call | tf_op jit(solution)/shard_map/pallas_call | solution.py:535
  73.9 7.0 %shard_map.81 = (f32[32,8,128]{2,1,0:T(8,128)S(1)}, f32[32,8,128]{2,1,0:T(8,128)S(1)}, f32[8,1,128]{2,1,0:T(1,128)S(1)}) custom-call(f32[309,8,128]{2,1,0:T(8,128)S(1)} %get-tuple-element.48.refs_0_.co, f32[32,8,128]{2,1,0:T(8,128)S(1)} %get-tuple-element.67.refs_1_, f32[32,8,128]{2,1,0:T(8,128)S(1)} %get-tuple-element.68.refs_2_, ...), custom_call_target="tpu_custom_call" | custom-call | tf_op jit(solution)/shard_map/pallas_call | solution.py:535
  80.9 10.7 %all_to_all.10 = f32[8,1,128]{2,1,0:T(1,128)S(1)} all-to-all(f32[8,1,128]{2,1,0:T(1,128)S(1)} %get-tuple-element.78), channel_id=1, replica_groups=mesh['rows'=8,'cols'=32] {'rows'}, dimensions={0} | all-to-all | bytes 8192 | tf_op jit(solution)/shard_map/all_to_all | solution.py:592
  92.2 4.0 %all-to-all-start.1 = ((f32[32,1,128]{2,1,0:T(1,128)}), f32[32,1,128]{2,1,0:T(1,128)S(1)}, u32[]{:S(2)}, u32[]{:S(2)}) async-start(f32[32,1,128]{2,1,0:T(1,128)} %broadcast_in_dim.2), calls=%async_computation.1 | async-start | bytes 32768 | tf_op jit(solution)/shard_map/all_to_all | solution.py:594
  96.3 1.1 %shard_map.82 = (f32[2,16,1024]{2,1,0:T(8,128)}, f32[2,16,1024]{2,1,0:T(8,128)}) custom-call(f32[309,8,128]{2,1,0:T(8,128)S(1)} %get-tuple-element.48.refs_0_.co, f32[32,8,128]{2,1,0:T(8,128)S(1)} %get-tuple-element.74.sums, f32[32,8,128]{2,1,0:T(8,128)S(1)} %get-tuple-element.75.final), custom_call_target="tpu_custom_call" | custom-call | tf_op jit(solution)/shard_map/pallas_call | solution.py:622
  97.4 7.5 %all-to-all-done.1 = f32[32,1,128]{2,1,0:T(1,128)S(1)} async-done(((f32[32,1,128]{2,1,0:T(1,128)}), f32[32,1,128]{2,1,0:T(1,128)S(1)}, u32[]{:S(2)}, u32[]{:S(2)}) %all-to-all-start.1) | async-done | bytes 16416 | tf_op jit(solution)/shard_map/all_to_all | solution.py:594
  (29 shorter events, 3.4 us)
Async XLA Ops:
  1.3 0.9 copy-start
  3.3 13.9 %collective-permute-start = (f32[2,8,128]{2,1,0:T(8,128)S(1)}, f32[2,8,128]{2,1,0:T(8,128)S(1)}, u32[]{:S(2)}, u32[]{:S(2)}) collective-permute-start(f32[2,8,128]{2,1,0:T(8,128)S(1)} %get-tuple-element.44), channel_id=1, source_target_pairs={{0,1},{1,2},{2,3},{3,4},{4,5},{5,6},{6,7},{7,8},{8,9},{9,10},{10,1... | collective-permute-start | bytes 24584 | tf_op jit(solution)/shard_map/ppermute | solution.py:549
  5.8 11.4 %collective-permute-start.1 = (f32[2,8,128]{2,1,0:T(8,128)S(1)}, f32[2,8,128]{2,1,0:T(8,128)S(1)}, u32[]{:S(2)}, u32[]{:S(2)}) collective-permute-start(f32[2,8,128]{2,1,0:T(8,128)S(1)} %get-tuple-element.45), channel_id=1, source_target_pairs={{1,0},{2,1},{3,2},{4,3},{5,4},{6,5},{7,6},{8,7},{9,8},{10,9},{11,1... | collective-permute-start | bytes 24584 | tf_op jit(solution)/shard_map/ppermute | solution.py:550
  12.3 4.9 %collective-permute-start.2 = (f32[4,8,128]{2,1,0:T(8,128)S(1)}, f32[4,8,128]{2,1,0:T(8,128)S(1)}, u32[]{:S(2)}, u32[]{:S(2)}) collective-permute-start(f32[4,8,128]{2,1,0:T(8,128)S(1)} %get-tuple-element.46), channel_id=1, source_target_pairs={{0,32},{32,64},{64,96},{96,128},{128,160},{160,192},{192,224},{224... | collective-permute-start | bytes 49160 | tf_op jit(solution)/shard_map/ppermute | solution.py:551
  14.3 3.2 %collective-permute-start.3 = (f32[4,8,128]{2,1,0:T(8,128)S(1)}, f32[4,8,128]{2,1,0:T(8,128)S(1)}, u32[]{:S(2)}, u32[]{:S(2)}) collective-permute-start(f32[4,8,128]{2,1,0:T(8,128)S(1)} %get-tuple-element.47), channel_id=1, source_target_pairs={{32,0},{64,32},{96,64},{128,96},{160,128},{192,160},{224,192},{0,2... | collective-permute-start | bytes 49160 | tf_op jit(solution)/shard_map/ppermute | solution.py:552
  33.4 8.8 %collective-permute-start.6 = (f32[64,8,128]{2,1,0:T(8,128)S(1)}, f32[64,8,128]{2,1,0:T(8,128)S(1)}, u32[]{:S(2)}, u32[]{:S(2)}) collective-permute-start(f32[64,8,128]{2,1,0:T(8,128)S(1)} %get-tuple-element.52), channel_id=1, source_target_pairs={{0,32},{32,0},{64,96},{96,64},{128,160},{160,128},{192,224},{224,1... | collective-permute-start | bytes 786440 | tf_op jit(solution)/shard_map/ppermute | solution.py:561
  35.1 7.2 %collective-permute-start.7 = (f32[64,8,128]{2,1,0:T(8,128)S(1)}, f32[64,8,128]{2,1,0:T(8,128)S(1)}, u32[]{:S(2)}, u32[]{:S(2)}) collective-permute-start(f32[64,8,128]{2,1,0:T(8,128)S(1)} %get-tuple-element.53), channel_id=1, source_target_pairs={{0,224},{32,64},{64,32},{96,128},{128,96},{160,192},{192,160},{224... | collective-permute-start | bytes 786440 | tf_op jit(solution)/shard_map/ppermute | solution.py:560
  35.1 4.1 %collective-permute-start.4 = (f32[16,2,8,128]{3,2,1,0:T(8,128)S(1)}, f32[16,2,8,128]{3,2,1,0:T(8,128)S(1)}, u32[]{:S(2)}, u32[]{:S(2)}) collective-permute-start(f32[16,2,8,128]{3,2,1,0:T(8,128)S(1)} %get-tuple-element.50), channel_id=1, source_target_pairs={{0,1},{1,0},{2,3},{3,2},{4,5},{5,4},{6,7},{7,6},{8,9},{9,8},{10,11... | collective-permute-start | bytes 393224 | tf_op jit(solution)/shard_map/ppermute | solution.py:561
  35.1 7.1 %collective-permute-start.5 = (f32[16,2,8,128]{3,2,1,0:T(8,128)S(1)}, f32[16,2,8,128]{3,2,1,0:T(8,128)S(1)}, u32[]{:S(2)}, u32[]{:S(2)}) collective-permute-start(f32[16,2,8,128]{3,2,1,0:T(8,128)S(1)} %get-tuple-element.51), channel_id=1, source_target_pairs={{0,31},{1,2},{2,1},{3,4},{4,3},{5,6},{6,5},{7,8},{8,7},{9,10},{10,... | collective-permute-start | bytes 393224 | tf_op jit(solution)/shard_map/ppermute | solution.py:560
  37.5 11.9 %collective-permute-start.8 = (f32[16,2,8,128]{3,2,1,0:T(8,128)S(1)}, f32[16,2,8,128]{3,2,1,0:T(8,128)S(1)}, u32[]{:S(2)}, u32[]{:S(2)}) collective-permute-start(f32[16,2,8,128]{3,2,1,0:T(8,128)S(1)} %get-tuple-element.57), channel_id=1, source_target_pairs={{0,1},{1,0},{2,3},{3,2},{4,5},{5,4},{6,7},{7,6},{8,9},{9,8},{10,11... | collective-permute-start | bytes 393224 | tf_op jit(solution)/shard_map/ppermute | solution.py:561
  39.2 10.2 %collective-permute-start.9 = (f32[16,2,8,128]{3,2,1,0:T(8,128)S(1)}, f32[16,2,8,128]{3,2,1,0:T(8,128)S(1)}, u32[]{:S(2)}, u32[]{:S(2)}) collective-permute-start(f32[16,2,8,128]{3,2,1,0:T(8,128)S(1)} %get-tuple-element.58), channel_id=1, source_target_pairs={{0,31},{1,2},{2,1},{3,4},{4,3},{5,6},{6,5},{7,8},{8,7},{9,10},{10,... | collective-permute-start | bytes 393224 | tf_op jit(solution)/shard_map/ppermute | solution.py:560
  56.5 10.5 %collective-permute-start.12 = (f32[64,8,128]{2,1,0:T(8,128)S(1)}, f32[64,8,128]{2,1,0:T(8,128)S(1)}, u32[]{:S(2)}, u32[]{:S(2)}) collective-permute-start(f32[64,8,128]{2,1,0:T(8,128)S(1)} %get-tuple-element.65), channel_id=1, source_target_pairs={{0,32},{32,0},{64,96},{96,64},{128,160},{160,128},{192,224},{224,1... | collective-permute-start | bytes 786440 | tf_op jit(solution)/shard_map/ppermute | solution.py:561
  59.3 7.6 %collective-permute-start.13 = (f32[64,8,128]{2,1,0:T(8,128)S(1)}, f32[64,8,128]{2,1,0:T(8,128)S(1)}, u32[]{:S(2)}, u32[]{:S(2)}) collective-permute-start(f32[64,8,128]{2,1,0:T(8,128)S(1)} %get-tuple-element.66), channel_id=1, source_target_pairs={{0,224},{32,64},{64,32},{96,128},{128,96},{160,192},{192,160},{224... | collective-permute-start | bytes 786440 | tf_op jit(solution)/shard_map/ppermute | solution.py:560
  59.8 4.1 %collective-permute-start.10 = (f32[16,2,8,128]{3,2,1,0:T(8,128)S(1)}, f32[16,2,8,128]{3,2,1,0:T(8,128)S(1)}, u32[]{:S(2)}, u32[]{:S(2)}) collective-permute-start(f32[16,2,8,128]{3,2,1,0:T(8,128)S(1)} %get-tuple-element.63), channel_id=1, source_target_pairs={{0,1},{1,0},{2,3},{3,2},{4,5},{5,4},{6,7},{7,6},{8,9},{9,8},{10,11... | collective-permute-start | bytes 393224 | tf_op jit(solution)/shard_map/ppermute | solution.py:561
  59.8 7.1 %collective-permute-start.11 = (f32[16,2,8,128]{3,2,1,0:T(8,128)S(1)}, f32[16,2,8,128]{3,2,1,0:T(8,128)S(1)}, u32[]{:S(2)}, u32[]{:S(2)}) collective-permute-start(f32[16,2,8,128]{3,2,1,0:T(8,128)S(1)} %get-tuple-element.64), channel_id=1, source_target_pairs={{0,31},{1,2},{2,1},{3,4},{4,3},{5,6},{6,5},{7,8},{8,7},{9,10},{10,... | collective-permute-start | bytes 393224 | tf_op jit(solution)/shard_map/ppermute | solution.py:560
  62.2 11.7 %collective-permute-start.14 = (f32[16,2,8,128]{3,2,1,0:T(8,128)S(1)}, f32[16,2,8,128]{3,2,1,0:T(8,128)S(1)}, u32[]{:S(2)}, u32[]{:S(2)}) collective-permute-start(f32[16,2,8,128]{3,2,1,0:T(8,128)S(1)} %get-tuple-element.70), channel_id=1, source_target_pairs={{0,1},{1,0},{2,3},{3,2},{4,5},{5,4},{6,7},{7,6},{8,9},{9,8},{10,11... | collective-permute-start | bytes 393224 | tf_op jit(solution)/shard_map/ppermute | solution.py:561
  63.9 10.0 %collective-permute-start.15 = (f32[16,2,8,128]{3,2,1,0:T(8,128)S(1)}, f32[16,2,8,128]{3,2,1,0:T(8,128)S(1)}, u32[]{:S(2)}, u32[]{:S(2)}) collective-permute-start(f32[16,2,8,128]{3,2,1,0:T(8,128)S(1)} %get-tuple-element.71), channel_id=1, source_target_pairs={{0,31},{1,2},{2,1},{3,4},{4,3},{5,6},{6,5},{7,8},{8,7},{9,10},{10,... | collective-permute-start | bytes 393224 | tf_op jit(solution)/shard_map/ppermute | solution.py:560
  92.2 12.7 %all-to-all-start.1 = ((f32[32,1,128]{2,1,0:T(1,128)}), f32[32,1,128]{2,1,0:T(1,128)S(1)}, u32[]{:S(2)}, u32[]{:S(2)}) async-start(f32[32,1,128]{2,1,0:T(1,128)} %broadcast_in_dim.2), calls=%async_computation.1 | async-start | bytes 32768 | tf_op jit(solution)/shard_map/all_to_all | solution.py:594
